TPU v7x, 512 devices: a whole 4x8x8 slice. The times are simulated.
512 devices in a mesh: sample: 16 (over x, y_lo, core), sy: 4 (over y_hi), sz: 8 (over z).
Axes of the slice: x: 4, y: 8 (y_hi: 4, y_lo: 2; y = y_hi * 2 + y_lo), z: 8, core: 2. Of those that a mesh axis runs over, the one named last changes fastest.
Arguments:
- activations: bfloat16 [16, 32, 8, 128, 128], P('sample', None, 'sy', 'sz'), may hold values from -6 to 6
- weight: bfloat16 [64, 32, 3, 3, 3], replicated, may hold values from -0.21875 to 0.21875
- pooled_grad: bfloat16 [16, 64, 4, 4096], P('sample', ('sy', 'sz')), may hold values from -6 to 6
- window_argmax: int32 [16, 64, 4, 4096], P('sample', None, 'sy', 'sz'), may hold values from 0 to 7
Outputs:
- input_grad: bfloat16 [16, 32, 8, 128, 128], P('sample', None, 'sy', 'sz')
- weight_grad: float32 [64, 32, 3, 3, 3], replicated
All inputs are finite; a program needn't handle non-finite values.
Results may differ from a plain program's by a relative error of at most 0.007.
Values may be sent and summed in bfloat16 or wider, within the bound.
No kernel may reach another device: no remote copies, remote signals or barrier semaphores. Data moves between devices by JAX's collectives and lax.ppermute only.
A program may use at most 64 MiB of HBM per device.

v0:
```python
import jax
import jax.numpy as jnp
from jax import lax
from jax.sharding import PartitionSpec as P


def padded(value, sides, width):
    for axis, dim in sides:
        size, length = (lax.axis_size(axis), value.shape[dim])
        up = [(i, (i + 1) % size) for i in range(size - 1)]
        down = [(j, i) for i, j in up]
        last = lax.slice_in_dim(value, length - width, length, axis=dim)
        leading = lax.slice_in_dim(value, 0, width, axis=dim)
        before = lax.ppermute(last, axis, up)
        after = lax.ppermute(leading, axis, down)
        value = jnp.concatenate([before, value, after], axis=dim)
    return value


def unpool(grad_vals, window_idx, rows, depth, width):
    chans = grad_vals.shape[0]
    grid = grad_vals.reshape(chans, rows, 1, depth, 1, width, 1)
    index = window_idx.reshape(chans, rows, 1, depth, 1, width, 1)
    first = lax.broadcasted_iota(jnp.int32, (1, 1, 2, 1, 1, 1, 1), 2)
    second = lax.broadcasted_iota(jnp.int32, (1, 1, 1, 1, 2, 1, 1), 4)
    third = lax.broadcasted_iota(jnp.int32, (1, 1, 1, 1, 1, 1, 2), 6)
    window_code = 4 * first + 2 * second + third
    spread = jnp.where(index == window_code, grid, jnp.zeros((), grid.dtype))
    return spread.reshape(chans, 2 * rows, 2 * depth, 2 * width)


def convolve(inputs, kernel, padding):
    return lax.conv_general_dilated(
        inputs,
        kernel,
        (1, 1, 1),
        padding,
        dimension_numbers=("NCDHW", "OIDHW", "NCDHW"),
        preferred_element_type=jnp.float32,
    )


def swap_lead(volume):
    return jnp.transpose(volume, (1, 0, 2, 3, 4))


def body(activations, weight, pooled_grad, window_argmax):
    sectioned = pooled_grad.reshape((1,) + pooled_grad.shape)
    moved = lax.all_to_all(
        lax.all_to_all(sectioned, "sy", split_axis=3, concat_axis=0, tiled=True),
        "sz",
        split_axis=4,
        concat_axis=1,
        tiled=True,
    )
    block_idx = window_argmax[0]
    rows_pooled = block_idx.shape[1]
    width = activations.shape[4] // 2
    depth = block_idx.shape[2] // width
    pooled_block = moved.reshape(block_idx.shape)
    flipped = jnp.flip(jnp.transpose(weight, (1, 0, 2, 3, 4)), (2, 3, 4))
    grad_out = unpool(pooled_block, block_idx, rows_pooled, depth, width)[None]
    grad_pad = padded(grad_out, (("sy", 2), ("sz", 3)), 1)
    input_pad = padded(activations, (("sy", 2), ("sz", 3)), 1)
    input_grad = convolve(grad_pad, flipped, ((0, 0), (0, 0), (1, 1)))
    local_dw = swap_lead(
        convolve(swap_lead(input_pad), swap_lead(grad_out), ((0, 0), (0, 0), (1, 1)))
    )
    total = lax.psum(local_dw, ("sample", "sy", "sz"))
    pooled_count = (
        lax.axis_size("sample")
        * lax.axis_size("sy")
        * lax.axis_size("sz")
        * rows_pooled
        * depth
        * width
    )
    return (input_grad.astype(jnp.bfloat16), total / jnp.sqrt(jnp.float32(pooled_count)))


def solution(mesh):
    return jax.shard_map(
        body,
        mesh=mesh,
        in_specs=(
            P("sample", None, "sy", "sz", None),
            P(),
            P("sample", ("sy", "sz"), None, None),
            P("sample", None, "sy", "sz"),
        ),
        out_specs=(P("sample", None, "sy", "sz", None), P()),
        check_vma=False,
    )
```

profile of v0, /device:TPU:1, one launch (start us, length us, event | category | flops | bytes accessed | tf_op | source)
XLA Modules:
  0.0 417.1 jit_solution(9830293381362007876)
XLA Ops:
  7.2 1.6 copy.60
  8.8 7.6 %all-to-all-start = ((bf16[1,1,2,4,4096]{4,2,1,0,3:T(2,128)(2,1)}), bf16[1,1,2,4,4096]{4,2,1,0,3:T(2,128)(2,1)S(1)}, u32[]{:S(2)}, u32[]{:S(2)}) async-start(bf16[1,1,2,4,4096]{4,2,1,0,3:T(2,128)(2,1)} %bitcast.33), calls=%async_computation | async-start | bytes 131072 | tf_op jit(solution)/shard_map/all_to_all | solution.py:50
  16.4 1.0 fusion.22
  17.5 4.3 %collective-permute-start.4 = (bf16[1,32,1,16,128]{4,1,3,2,0:T(8,128)(2,1)S(1)}, bf16[1,32,1,16,128]{4,1,3,2,0:T(8,128)(2,1)S(1)}, u32[]{:S(2)}, u32[]{:S(2)}) collective-permute-start(bf16[1,32,1,16,128]{4,1,3,2,0:T(8,128)(2,1)S(1)} %copy.58), channel_id=1, source_target_pairs={{0,8},{8,16},{16,24},{1,9},{9,17},{17,25},{2,10},{10,18},{18,26},{... | collective-permute-start | bytes 393224 | tf_op jit(solution)/shard_map/ppermute | solution.py:14
  21.8 1.3 collective-permute-start.5
  23.2 0.5 collective-permute-done.4
  23.7 1.1 constant_dynamic-update-slice_fusion.1
  24.8 8.6 %collective-permute-done.5 = bf16[1,32,1,16,128]{4,1,3,2,0:T(8,128)(2,1)S(1)} collective-permute-done((bf16[1,32,1,16,128]{4,1,3,2,0:T(8,128)(2,1)S(1)}, bf16[1,32,1,16,128]{4,1,3,2,0:T(8,128)(2,1)S(1)}, u32[]{:S(2)}, u32[]{:S(2)}) %collective-permute-start.5) | collective-permute-done | bytes 131104 | tf_op jit(solution)/shard_map/ppermute | solution.py:15
  33.4 0.7 fusion.20
  34.1 4.2 %collective-permute-start.6 = (bf16[1,32,4,1,128]{4,1,3,2,0:T(8,128)(2,1)}, bf16[1,32,4,1,128]{4,1,3,2,0:T(8,128)(2,1)S(1)}, u32[]{:S(2)}, u32[]{:S(2)}) collective-permute-start(bf16[1,32,4,1,128]{4,1,3,2,0:T(8,128)(2,1)} %get-tuple-element.10), channel_id=1, source_target_pairs={{0,1},{1,2},{2,3},{3,4},{4,5},{5,6},{6,7},{8,9},{9,10},{10,11},{11... | collective-permute-start | bytes 98312 | tf_op jit(solution)/shard_map/ppermute | solution.py:14
  38.2 1.3 collective-permute-start.7
  39.6 0.1 eq.53
  39.7 0.5 eq.54
  40.2 0.1 copy.54
  40.4 0.4 eq.50
  40.8 1.1 copy.39
  41.9 2.8 copy.41
  44.7 4.8 %reshape.101 = bf16[8,2,2048]{2,1,0:T(2,128)(2,1)} reshape(bf16[4096,1,1,2,4]{4,3,2,1,0:T(2,128)(2,1)S(1)} %bitcast.35) | data formatting | bytes 131072
  49.5 11.2 %all-to-all-start.1 = ((bf16[8,2,2048]{2,1,0:T(2,128)(2,1)}), bf16[8,2,2048]{2,1,0:T(2,128)(2,1)S(1)}, u32[]{:S(2)}, u32[]{:S(2)}) async-start(bf16[8,2,2048]{2,1,0:T(2,128)(2,1)} %reshape.101), calls=%async_computation.1 | async-start | bytes 131072 | tf_op jit(solution)/shard_map/all_to_all | solution.py:49
  60.7 1.1 maximum_bitcast_fusion.1
  61.9 8.0 %copy.52 = bf16[32,1,4,18,128]{0,1,4,3,2:T(2,128)(2,1)} copy(bf16[32,1,4,18,128]{4,0,3,2,1:T(8,128)(2,1)S(1)} %maximum_bitcast_fusion.1) | data formatting | bytes 1179648 | tf_op jit(solution)/shard_map/transpose | solution.py:44
  69.8 4.5 %reshape.102 = bf16[4096,1,1,2,4]{4,3,2,1,0:T(2,128)(2,1)S(1)} reshape(bf16[8,2,2048]{2,1,0:T(2,128)(2,1)S(1)} %all-to-all-done.1) | data formatting | bytes 131072
  74.3 1.5 copy.42
  75.8 0.1 broadcast_in_dim.22
  76.0 0.2 copy.43
  76.1 0.4 broadcast_in_dim.23
  76.5 0.3 copy.44
  76.8 1.2 compare_select_fusion.2
  78.0 0.8 copy-done.1
  78.8 0.8 fusion.21
  79.6 4.7 %collective-permute-start = (bf16[1,64,1,16,128]{4,3,2,1,0:T(8,128)(2,1)}, bf16[1,64,1,16,128]{4,3,2,1,0:T(8,128)(2,1)}, u32[]{:S(2)}, u32[]{:S(2)}) collective-permute-start(bf16[1,64,1,16,128]{4,3,2,1,0:T(8,128)(2,1)} %get-tuple-element.12), channel_id=1, source_target_pairs={{0,8},{8,16},{16,24},{1,9},{9,17},{17,25},{2,10},{10,18},{18,26},{... | collective-permute-start | bytes 786440 | tf_op jit(solution)/shard_map/ppermute | solution.py:14
  84.3 1.3 collective-permute-start.1
  85.6 32.4 %fusion.8 = f32[64,32,3,3,3]{0,1,4,3,2:T(8,128)} fusion(bf16[32,1,4,18,128]{0,1,4,3,2:T(2,128)(2,1)} %copy.52, bf16[64,16,128]{0,2,1:T(8,128)(2,1)S(1)} %bitcast.41, s32[2,16,128]{2,1,0:T(8,128)S(1)} %eq.54, s32[64,16,128]{0,2,1:T(8,128)S(1)} %bitcast.39), kind=kOutput, calls=%fused_computation.10 | convolution fusion | flops 451149824 | bytes 1613824 | tf_op jit(solution)/shard_map/transpose | solution.py:44
  118.0 1.3 pad_maximum_fusion.2
  119.4 3.4 collective-permute-start.2
  122.7 1.3 collective-permute-start.3
  124.0 264.5 %all-reduce.2.cloned.1.call-done = f32[64,32,3,3,3]{0,1,4,3,2:T(8,128)} async-done(((f32[64,32,3,3,3]{0,1,4,3,2:T(8,128)}), f32[64,32,3,3,3]{0,1,4,3,2:T(8,128)}) %all-reduce.2.cloned.1.call-update) | async-done | bytes 221200 | tf_op jit(solution)/shard_map/psum | solution.py:69
  388.5 1.8 broadcast_multiply_fusion
  390.4 3.2 maximum_bitcast_fusion
  393.6 4.7 %copy.55 = bf16[64,4,18,1,128]{0,1,4,2,3:T(4,128)(2,1)S(1)} copy(bf16[64,4,18,1,128]{4,2,1,0,3:T(8,128)(2,1)} %maximum_bitcast_fusion) | data formatting | bytes 2359296
  398.2 1.2 pad.clone
  399.5 0.3 copy.47
  399.8 0.1 slice.36
  399.9 0.2 copy-done.5
  400.2 7.9 %select_convert_fusion = bf16[2,16,8,17,32]{4,2,3,1,0:T(8,128)(2,1)S(1)} fusion(bf16[64,32,3,3,3]{0,1,4,3,2:T(8,128)(2,1)S(1)} %copy-done, bf16[64,4,18,1,7,2]{0,4,5,2,1,3:T(8,128)(2,1)S(1)} %slice.36, bf16[64,4,18,1,8,17]{0,4,5,2,1,3:T(8,128)(2,1)S(1)} %copy.47, pred[8,17]{0,1:T(8,128)(4,1)S(1)} %copy-done.5), kind=kOutput, calls=%fused_computation.9 | convolution fusion | flops 485777408 | bytes 1771656 | tf_op jit(solution)/shard_map/conv_general_dilated | solution.py:33
  408.1 0.1 copy.48
  408.3 0.2 slice_bitcast_fusion
  408.5 1.8 copy.53
  (27 shorter events, 0.3 us)
Async XLA Ops:
  7.2 392.8 %copy-start = (bf16[64,32,3,3,3]{0,1,4,3,2:T(8,128)(2,1)S(1)}, bf16[64,32,3,3,3]{0,1,4,3,2:T(8,128)(2,1)}, u32[]{:S(2)}) copy-start(bf16[64,32,3,3,3]{0,1,4,3,2:T(8,128)(2,1)} %param.5) | copy-start | bytes 331780
  7.2 33.0 %copy-start.4 = (s32[1,64,1,512]{3,2,1,0:T(1,128)S(1)}, s32[1,64,1,512]{3,2,1,0:T(1,128)}, u32[]{:S(2)}) copy-start(s32[1,64,1,512]{3,2,1,0:T(1,128)} %param.7) | copy-start | bytes 393220
  8.8 33.1 %all-to-all-start = ((bf16[1,1,2,4,4096]{4,2,1,0,3:T(2,128)(2,1)}), bf16[1,1,2,4,4096]{4,2,1,0,3:T(2,128)(2,1)S(1)}, u32[]{:S(2)}, u32[]{:S(2)}) async-start(bf16[1,1,2,4,4096]{4,2,1,0,3:T(2,128)(2,1)} %bitcast.33), calls=%async_computation | async-start | bytes 131072 | tf_op jit(solution)/shard_map/all_to_all | solution.py:50
  17.5 6.2 %collective-permute-start.4 = (bf16[1,32,1,16,128]{4,1,3,2,0:T(8,128)(2,1)S(1)}, bf16[1,32,1,16,128]{4,1,3,2,0:T(8,128)(2,1)S(1)}, u32[]{:S(2)}, u32[]{:S(2)}) collective-permute-start(bf16[1,32,1,16,128]{4,1,3,2,0:T(8,128)(2,1)S(1)} %copy.58), channel_id=1, source_target_pairs={{0,8},{8,16},{16,24},{1,9},{9,17},{17,25},{2,10},{10,18},{18,26},{... | collective-permute-start | bytes 393224 | tf_op jit(solution)/shard_map/ppermute | solution.py:14
  21.8 11.6 %collective-permute-start.5 = (bf16[1,32,1,16,128]{4,1,3,2,0:T(8,128)(2,1)S(1)}, bf16[1,32,1,16,128]{4,1,3,2,0:T(8,128)(2,1)S(1)}, u32[]{:S(2)}, u32[]{:S(2)}) collective-permute-start(bf16[1,32,1,16,128]{4,1,3,2,0:T(8,128)(2,1)S(1)} %copy.59), channel_id=1, source_target_pairs={{8,0},{16,8},{24,16},{9,1},{17,9},{25,17},{10,2},{18,10},{26,18},{... | collective-permute-start | bytes 393224 | tf_op jit(solution)/shard_map/ppermute | solution.py:15
  33.4 6.2 %copy-start.3 = (bf16[1,32,4,16,128]{4,1,3,2,0:T(8,128)(2,1)}, bf16[1,32,4,16,128]{4,1,3,2,0:T(8,128)(2,1)S(1)}, u32[]{:S(2)}) copy-start(bf16[1,32,4,16,128]{4,1,3,2,0:T(8,128)(2,1)S(1)} %constant_dynamic-update-slice_fusion) | copy-start | bytes 1572868
  34.1 26.6 %collective-permute-start.6 = (bf16[1,32,4,1,128]{4,1,3,2,0:T(8,128)(2,1)}, bf16[1,32,4,1,128]{4,1,3,2,0:T(8,128)(2,1)S(1)}, u32[]{:S(2)}, u32[]{:S(2)}) collective-permute-start(bf16[1,32,4,1,128]{4,1,3,2,0:T(8,128)(2,1)} %get-tuple-element.10), channel_id=1, source_target_pairs={{0,1},{1,2},{2,3},{3,4},{4,5},{5,6},{6,7},{8,9},{9,10},{10,11},{11... | collective-permute-start | bytes 98312 | tf_op jit(solution)/shard_map/ppermute | solution.py:14
  38.2 22.5 %collective-permute-start.7 = (bf16[1,32,4,1,128]{4,1,3,2,0:T(8,128)(2,1)S(1)}, bf16[1,32,4,1,128]{4,1,3,2,0:T(8,128)(2,1)S(1)}, u32[]{:S(2)}, u32[]{:S(2)}) collective-permute-start(bf16[1,32,4,1,128]{4,1,3,2,0:T(8,128)(2,1)S(1)} %get-tuple-element.11), channel_id=1, source_target_pairs={{1,0},{2,1},{3,2},{4,3},{5,4},{6,5},{7,6},{9,8},{10,9},{11,10},{12... | collective-permute-start | bytes 98312 | tf_op jit(solution)/shard_map/ppermute | solution.py:15
  49.5 20.4 %all-to-all-start.1 = ((bf16[8,2,2048]{2,1,0:T(2,128)(2,1)}), bf16[8,2,2048]{2,1,0:T(2,128)(2,1)S(1)}, u32[]{:S(2)}, u32[]{:S(2)}) async-start(bf16[8,2,2048]{2,1,0:T(2,128)(2,1)} %reshape.101), calls=%async_computation.1 | async-start | bytes 131072 | tf_op jit(solution)/shard_map/all_to_all | solution.py:49
  60.7 327.9 %all-reduce.2.cloned.1.call-start = ((), (), s32[]{:S(2)}) async-start(), calls=%async_computation.2 | async-start | bytes 884736 | tf_op jit(solution)/shard_map/psum | solution.py:69
  78.0 0.8 copy-start.1
  79.6 38.4 %collective-permute-start = (bf16[1,64,1,16,128]{4,3,2,1,0:T(8,128)(2,1)}, bf16[1,64,1,16,128]{4,3,2,1,0:T(8,128)(2,1)}, u32[]{:S(2)}, u32[]{:S(2)}) collective-permute-start(bf16[1,64,1,16,128]{4,3,2,1,0:T(8,128)(2,1)} %get-tuple-element.12), channel_id=1, source_target_pairs={{0,8},{8,16},{16,24},{1,9},{9,17},{17,25},{2,10},{10,18},{18,26},{... | collective-permute-start | bytes 786440 | tf_op jit(solution)/shard_map/ppermute | solution.py:14
  84.3 33.7 %collective-permute-start.1 = (bf16[1,64,1,16,128]{4,3,2,1,0:T(8,128)(2,1)}, bf16[1,64,1,16,128]{4,3,2,1,0:T(8,128)(2,1)}, u32[]{:S(2)}, u32[]{:S(2)}) collective-permute-start(bf16[1,64,1,16,128]{4,3,2,1,0:T(8,128)(2,1)} %get-tuple-element.13), channel_id=1, source_target_pairs={{8,0},{16,8},{24,16},{9,1},{17,9},{25,17},{10,2},{18,10},{26,18},{... | collective-permute-start | bytes 786440 | tf_op jit(solution)/shard_map/ppermute | solution.py:15
  85.6 32.5 %copy-start.2 = (bf16[1,64,2,16,128]{4,3,2,1,0:T(8,128)(2,1)S(1)}, bf16[1,64,2,16,128]{4,3,2,1,0:T(8,128)(2,1)}, u32[]{:S(2)}) copy-start(bf16[1,64,2,16,128]{4,3,2,1,0:T(8,128)(2,1)} %copy-done.1) | copy-start | bytes 1572868
  119.4 271.0 %collective-permute-start.2 = (bf16[1,64,4,1,128]{4,3,2,1,0:T(2,128)(2,1)S(1)}, bf16[1,64,4,1,128]{4,3,2,1,0:T(2,128)(2,1)S(1)}, u32[]{:S(2)}, u32[]{:S(2)}) collective-permute-start(bf16[1,64,4,1,128]{4,3,2,1,0:T(2,128)(2,1)S(1)} %get-tuple-element.8), channel_id=1, source_target_pairs={{0,1},{1,2},{2,3},{3,4},{4,5},{5,6},{6,7},{8,9},{9,10},{10,11},{11... | collective-permute-start | bytes 196616 | tf_op jit(solution)/shard_map/ppermute | solution.py:14
  122.7 267.6 %collective-permute-start.3 = (bf16[1,64,4,1,128]{4,3,2,1,0:T(2,128)(2,1)S(1)}, bf16[1,64,4,1,128]{4,3,2,1,0:T(2,128)(2,1)S(1)}, u32[]{:S(2)}, u32[]{:S(2)}) collective-permute-start(bf16[1,64,4,1,128]{4,3,2,1,0:T(2,128)(2,1)S(1)} %get-tuple-element.9), channel_id=1, source_target_pairs={{1,0},{2,1},{3,2},{4,3},{5,4},{6,5},{7,6},{9,8},{10,9},{11,10},{12... | collective-permute-start | bytes 196616 | tf_op jit(solution)/shard_map/ppermute | solution.py:15
  399.5 0.7 copy-start.5
Sparse Core Ops, SparseCore 0:
  118.1 270.3 all-reduce.1
where the time goes:
time: 418 us; the launch traced here: 417 us
  waiting for transfers between devices  274 us (66%)
  starting transfers between devices  40.5 us (10%)
  matrix products  40.3 us (10%)
  local copies, waits for them, and re-layouts  39.4 us (9%)
  between operations  14.4 us (3%)
  other arithmetic  8.77 us (2%)
    psum x1, waiting for transfers between devices, body(): total = lax.psum(local_dw, ('sample', 'sy', 'sz'))  265 us
    transpose x1, matrix products, swap_lead(): return jnp.transpose(volume, (1, 0, 2, 3, 4))  32.4 us
    unnamed x21, local copies, waits for them, and re-layouts  19.5 us
    ppermute x4, starting transfers between devices, padded(): before = lax.ppermute(last, axis, up)  16.5 us
    all_to_all x1, starting transfers between devices, body(): lax.all_to_all(lax.all_to_all(sectioned, 'sy', split_axis=3, concat_axis=...  11.2 us
    ppermute x4, waiting for transfers between devices, padded(): after = lax.ppermute(leading, axis, down)  8.59 us
  transfers between devices with their start and end apart: 11, of which 3 were waited for; matrix products, arithmetic and copies ran while one was open for 14% of the time, Pallas kernels for 0%

commit v1 on v0

v1 whole, which is shorter than its diff:
```python
import functools

import jax
import jax.numpy as jnp
import numpy as np
from jax import lax
from jax.experimental import pallas as pl
from jax.experimental.pallas import tpu as pltpu
from jax.sharding import PartitionSpec as P

SY, SZ, SAMPLE = 4, 8, 16
CIN, COUT = 32, 64
ROWS = 16
F32, BF16 = jnp.float32, jnp.bfloat16
LIMIT = 24 * 1024 * 1024


def selection():
    sel = np.zeros((SY * SZ * 2 * ROWS, 272), np.float32)
    for sy in range(SY):
        for sz in range(SZ):
            for ch in range(2):
                for dy in range(3):
                    py = sy + dy - 1
                    if 0 <= py < SY:
                        for j in range(5):
                            row = ((sy * SZ + sz) * 2 + ch) * ROWS + dy * 5 + j
                            sel[row, (ch * 4 + py) * 33 + 4 * sz + j] = 1
    return sel


def halves(shape):
    return lax.broadcasted_iota(jnp.int32, shape, len(shape) - 1) < 64


def roll64(value):
    return pltpu.roll(value, 64, 1)


def pack_kernel(sz_ref, pg_ref, am_ref, sel_ref, out_ref, tiles):
    low = halves((8, 128))
    pooled = jnp.concatenate([pg_ref[0, 0].astype(F32), pg_ref[0, 1].astype(F32)], axis=0)
    tiles[...] = jnp.zeros_like(tiles)
    before = jnp.zeros((8, 128), F32)
    for k in range(33):
        tile = pooled[:, k * 128:(k + 1) * 128] if k < 32 else jnp.zeros((8, 128), F32)
        tiles[pl.ds(k, 8, stride=33), :] = roll64(jnp.where(low, tile, before))
        before = tile
    sent = jnp.dot(sel_ref[...], tiles[...].astype(BF16), preferred_element_type=F32).astype(BF16)
    low = halves((32, 128))
    first = am_ref[pl.ds(0, 64, stride=4), :].astype(F32)
    last = am_ref[pl.ds(3, 64, stride=4), :].astype(F32)
    leading = jnp.where(low, first[:32], roll64(first[32:]))
    ending = jnp.where(low, roll64(last[:32]), last[32:])
    me = sz_ref[1]
    for sz in range(SZ):
        codes = jnp.where(sz < me, leading, ending).astype(BF16)
        for sy in range(SY):
            for ch in range(2):
                block = (sy * SZ + sz) * 2 + ch
                out_ref[pl.ds(block * 32, 16), :] = sent[block * 16:(block + 1) * 16]
                out_ref[pl.ds(block * 32 + 16, 16), :] = codes[ch * 16:(ch + 1) * 16]


def taps_kernel(act_ref, out_ref, wide):
    src = lax.broadcasted_iota(jnp.int32, (128, 128), 0)
    lane = lax.broadcasted_iota(jnp.int32, (128, 128), 1)
    place = 2 * (lane % 64) + lane // 64
    act = act_ref[...]
    for c in range(3):
        pick = (src == place + (c - 1)).astype(F32).astype(BF16)
        wide[...] = jnp.dot(act, pick, preferred_element_type=F32)
        for yz in range(32):
            rows = wide[pl.ds(yz, 32, stride=32), :]
            out_ref[c * 32:(c + 1) * 32, yz * 128:(yz + 1) * 128] = rows.astype(BF16)


def main_kernel(at_ref, recv_ref, own_ref, up_ref, down_ref, act_ref, dw_ref, g_ref, rows):
    my_sy, my_sz = at_ref[0], at_ref[1]
    rows[...] = recv_ref[...].astype(F32)
    low = halves((64, 128))
    low32 = halves((32, 128))
    parity = jnp.where(low, 0, 1)

    def spread(value, first):
        other = roll64(value)
        return jnp.where(low, value, other) if first else jnp.where(low, other, value)

    def halo(sy, sz):
        base = (jnp.clip(sy, 0, SY - 1) * SZ + jnp.clip(sz, 0, SZ - 1)) * 64
        packed = jnp.concatenate(
            [rows[pl.ds(pl.multiple_of(base + 16, 16), 16), :], rows[pl.ds(pl.multiple_of(base + 48, 16), 16), :]], axis=0
        )
        other = roll64(packed)
        return jnp.concatenate(
            [jnp.where(low32, packed, other), jnp.where(low32, other, packed)], axis=0
        ).astype(jnp.int32)

    for dy, (source, levels) in enumerate(((up_ref, (1,)), (own_ref, (0, 1)), (down_ref, (0,)))):
        before = halo(my_sy + dy - 1, my_sz - 1)
        after = halo(my_sy + dy - 1, my_sz + 1)
        codes = None
        values = None
        for pz in range(10):
            if pz % 2 == 0:
                values = rows[pl.ds(dy * 5 + pz // 2, 64, stride=32), :]
            value = spread(values, pz % 2 == 0)
            if pz == 0:
                code = before
            elif pz == 9:
                code = after
            else:
                if pz % 2 == 1:
                    codes = source[pl.ds((pz - 1) // 2, 64, stride=4), :]
                code = spread(codes, pz % 2 == 1)
            code = code - parity
            for a in levels:
                y = {(0, 1): 0, (1, 0): 1, (1, 1): 2, (2, 0): 3}[(dy, a)]
                for b in ((1,) if pz == 0 else (0,) if pz == 9 else (0, 1)):
                    z = 2 * pz - 1 + b
                    cell = (y * 18 + z) * 128
                    g_ref[:, cell:cell + 128] = jnp.where(code == 4 * a + 2 * b, value, 0.0).astype(BF16)

    total = jnp.zeros((96, 576), F32)
    depth = 4
    for y in range(2):
        for z in range(0, 16, depth):
            parts = []
            for a in range(3):
                for b in range(3):
                    cell = ((y + 2 - a) * 18 + z + 2 - b) * 128
                    parts.append(g_ref[:, cell:cell + 128 * depth])
            cell = (y * 16 + z) * 128
            total += lax.dot_general(
                act_ref[:, cell:cell + 128 * depth],
                jnp.concatenate(parts, axis=0),
                (((1,), (1,)), ((), ())),
                preferred_element_type=F32,
            )
    for j in range(4):
        dw_ref[j * 96:(j + 1) * 96, :] = total[:, j * 128:(j + 1) * 128]
    dw_ref[384:480, :] = jnp.concatenate([total[:, 512:], jnp.zeros((96, 64), F32)], axis=1)
    dw_ref[480:, :] = jnp.zeros((32, 128), F32)


def input_kernel(g_ref, w_ref, out_ref, cells):
    lane = lax.broadcasted_iota(jnp.int32, (32, 128), 1)
    low = lane < 64
    kernel = jnp.concatenate([w_ref[3 * ab:3 * ab + 3].reshape(96, COUT) for ab in range(9)], axis=1)
    for y in range(2):
        for z in range(0, 16, 2):
            parts = []
            for a in range(3):
                for b in range(3):
                    cell = ((y + 2 - a) * 18 + z + 2 - b) * 128
                    parts.append(g_ref[:, cell:cell + 256])
            sums = jnp.dot(kernel, jnp.concatenate(parts, axis=0), preferred_element_type=F32)
            for k in range(2):
                part = sums[:, k * 128:(k + 1) * 128]
                c0, c1, c2 = part[:32], part[32:64], part[64:]
                ahead = jnp.where(low, roll64(c0), jnp.where(lane == 127, 0.0, pltpu.roll(c0, 63, 1)))
                behind = jnp.where(low, jnp.where(lane == 0, 0.0, pltpu.roll(c2, 65, 1)), roll64(c2))
                cells[pl.ds(y * 16 + z + k, 32, stride=32), :] = c1 + ahead + behind
    src = lax.broadcasted_iota(jnp.int32, (128, 128), 0)
    dst = lax.broadcasted_iota(jnp.int32, (128, 128), 1)
    order = (dst == 2 * (src % 64) + src // 64).astype(F32).astype(BF16)
    out_ref[...] = jnp.dot(cells[...].astype(BF16), order, preferred_element_type=F32).astype(BF16)


def final_kernel(scale, in_ref, out_ref):
    for ab in range(9):
        j, half = divmod(ab, 2)
        part = in_ref[j * 96:(j + 1) * 96, half * 64:half * 64 + 64] * scale
        for c in range(3):
            out_ref[3 * ab + c] = part[c * 32:(c + 1) * 32]


def call(kernel, outs, scratch, args, smem=False, flops=0):
    vmem = pl.BlockSpec(memory_space=pltpu.VMEM)
    specs = [vmem] * len(args)
    if smem:
        specs[0] = pl.BlockSpec(memory_space=pltpu.SMEM)
    nbytes = sum(int(np.prod(v.shape)) * v.dtype.itemsize for v in list(args) + list(outs))
    return pl.pallas_call(
        kernel,
        out_shape=tuple(outs) if len(outs) > 1 else outs[0],
        in_specs=specs,
        out_specs=tuple([vmem] * len(outs)) if len(outs) > 1 else vmem,
        scratch_shapes=scratch,
        compiler_params=pltpu.CompilerParams(vmem_limit_bytes=LIMIT),
        cost_estimate=pl.CostEstimate(flops=flops, bytes_accessed=nbytes, transcendentals=0),
    )(*args)


def body(activations, weight, pooled_grad, window_argmax):
    shape = jax.ShapeDtypeStruct
    at = jnp.stack([lax.axis_index("sy"), lax.axis_index("sz")]).astype(jnp.int32)
    codes = window_argmax.reshape(256, 128)
    rise = [(i, (i + 1) % SY) for i in range(SY)]
    fall = [(j, i) for i, j in rise]
    below = lax.ppermute(codes, "sy", rise)
    above = lax.ppermute(codes, "sy", fall)
    sel = jnp.asarray(selection(), BF16)
    sent = call(
        pack_kernel, [shape((2048, 128), BF16)], [pltpu.VMEM((272, 128), F32)],
        (at, pooled_grad, codes, sel), smem=True, flops=2 * 1024 * 272 * 128,
    )
    recv = lax.all_to_all(sent.reshape(32, 64, 128), ("sy", "sz"), 0, 0).reshape(2048, 128)
    taps = call(
        taps_kernel, [shape((96, 4096), BF16)], [pltpu.VMEM((1024, 128), F32)],
        (activations.reshape(1024, 128),), flops=2 * 1024 * 128 * 384,
    )
    local, grad_out = call(
        main_kernel, [shape((512, 128), F32), shape((COUT, 72 * 128), BF16)], [pltpu.VMEM((2048, 128), F32)],
        (at, recv, codes, below, above, taps), smem=True, flops=2 * 96 * 576 * 4096,
    )
    input_grad = call(
        input_kernel, [shape((1024, 128), BF16)], [pltpu.VMEM((1024, 128), F32)],
        (grad_out, jnp.transpose(weight, (2, 3, 4, 1, 0)).reshape(27, CIN, COUT)), flops=2 * 96 * 576 * 4096,
    )
    part = jnp.sum(lax.all_to_all(local.reshape(SAMPLE, 32, 128), "sample", 0, 0), 0)
    for axis, size in (("sz", SZ), ("sy", SY)):
        part = jnp.sum(lax.all_to_all(jnp.broadcast_to(part[None], (size, 32, 128)), axis, 0, 0), 0)
    whole = lax.all_to_all(jnp.broadcast_to(part[None], (SAMPLE, 32, 128)), "sample", 0, 0).reshape(512, 128)
    pooled = SAMPLE * SY * SZ * 8 * 64
    dw = call(
        functools.partial(final_kernel, float(1.0 / np.sqrt(np.float32(pooled)))),
        [shape((27, CIN, COUT), F32)], [], (whole,),
    )
    dw = jnp.transpose(dw.reshape(3, 3, 3, CIN, COUT), (4, 3, 0, 1, 2))
    return input_grad.reshape(1, CIN, 2, 16, 128), dw


def solution(mesh):
    return jax.shard_map(
        body,
        mesh=mesh,
        in_specs=(
            P("sample", None, "sy", "sz", None),
            P(),
            P("sample", ("sy", "sz"), None, None),
            P("sample", None, "sy", "sz"),
        ),
        out_specs=(P("sample", None, "sy", "sz", None), P()),
        check_vma=False,
    )
```

time: 418 us -> 98.8 us (0.24)
  waiting for transfers between devices: 274 us -> 17 us
  matrix products: 40.3 us -> 0 us
  blocking collectives: 0 us -> 37 us
  local copies, waits for them, and re-layouts: 39.4 us -> 3.64 us
  between operations: 14.4 us -> 0.73 us
  starting transfers between devices: 40.5 us -> 30.8 us
  Pallas kernels: 0 us -> 9.08 us
  other arithmetic: 8.77 us -> 0.12 us
    psum x1 -> x0, waiting for transfers between devices: 265 us -> none  [body(): total = lax.psum(local_dw, ('sample', 'sy', 'sz'))]
    all_to_all x0 -> x3, blocking collectives: none -> 37 us  [the longest x2 24.1 us: body(): lax.all_to_all(jnp.broadcast_to(part[None], (size, 32, 128)), axis, 0, 0)]
    transpose x1 -> x0, matrix products: 32.4 us -> none  [swap_lead(): return jnp.transpose(volume, (1, 0, 2, 3, 4))]
    unnamed x21 -> x12, local copies, waits for them, and re-layouts: 19.5 us -> 2.89 us
    ppermute x8 -> x2, starting transfers between devices: 21.7 us -> 7.21 us  [the longest x1 5.29 us: body(): above = lax.ppermute(codes, 'sy', fall)]
    pallas_call x0 -> x5, Pallas kernels: none -> 9.08 us  [call(): pl.pallas_call(kernel, out_shape=tuple(outs) if len(outs) > 1 else outs[0...]
    transpose x1 -> x0, local copies, waits for them, and re-layouts: 7.96 us -> none  [swap_lead(): return jnp.transpose(volume, (1, 0, 2, 3, 4))]
    conv_general_dilated x1 -> x0, matrix products: 7.92 us -> none  [convolve(): lax.conv_general_dilated(inputs, kernel, (1, 1, 1), padding, dimension_nu...]
  transfers between devices with their start and end apart: 11 -> 4, of which waited for: 3 -> 3; matrix products, arithmetic and copies ran while one was open for 14% -> 0% of each run, Pallas kernels for 0% -> 4%
where the time goes in v1:
time: 98.8 us; the launch traced here: 98.3 us
  blocking collectives  37 us (37%)
  starting transfers between devices  30.8 us (31%)
  waiting for transfers between devices  17 us (17%)
  Pallas kernels  9.08 us (9%)
  local copies, waits for them, and re-layouts  3.64 us (4%)
    all_to_all x2, blocking collectives, body(): lax.all_to_all(jnp.broadcast_to(part[None], (size, 32, 128)), axis, 0, 0)  24.1 us
    all_to_all x1, starting transfers between devices, body(): lax.all_to_all(sent.reshape(32, 64, 128), ('sy', 'sz'), 0, 0)  16.5 us
    all_to_all x1, blocking collectives, body(): lax.all_to_all(local.reshape(SAMPLE, 32, 128), 'sample', 0, 0)  12.9 us
    ppermute x1, waiting for transfers between devices, body(): above = lax.ppermute(codes, 'sy', fall)  11.3 us
    pallas_call x5, Pallas kernels, call(): pl.pallas_call(kernel, out_shape=tuple(outs) if len(outs) > 1 else outs[0...  9.08 us
    all_to_all x1, starting transfers between devices, body(): lax.all_to_all(jnp.broadcast_to(part[None], (SAMPLE, 32, 128)), 'sample',...  7.06 us
    ppermute x1, starting transfers between devices, body(): above = lax.ppermute(codes, 'sy', fall)  5.29 us
    all_to_all x1, waiting for transfers between devices, body(): lax.all_to_all(jnp.broadcast_to(part[None], (SAMPLE, 32, 128)), 'sample',...  4.89 us
  transfers between devices with their start and end apart: 4, of which 3 were waited for; matrix products, arithmetic and copies ran while one was open for 0% of the time, Pallas kernels for 4%

profile of v1, /device:TPU:1, one launch (start us, length us, event | category | flops | bytes accessed | tf_op | source)
XLA Modules:
  0.0 98.3 jit_solution(1474455858709172166)
XLA Ops:
  0.6 0.1 pad_add_fusion.sz_ref.at_ref
  0.7 0.0 copy-start
  0.7 1.1 %copy-done = bf16[1024,272]{1,0:T(8,128)(2,1)S(1)} copy-done((bf16[1024,272]{1,0:T(8,128)(2,1)S(1)}, bf16[1024,272]{1,0:T(8,128)(2,1)}, u32[]{:S(2)}) %copy-start) | copy-done | bytes 557080
  1.8 0.0 copy-start.1
  1.8 0.9 copy-done.1
  2.7 0.0 copy-start.4
  2.8 0.8 copy-done.4
  3.6 0.0 copy-start.2
  3.6 0.0 copy-start.3
  3.6 1.8 %shard_map.68 = bf16[2048,128]{1,0:T(8,128)(2,1)} custom-call(s32[2]{0:T(128)S(1)} %pad_add_fusion.sz_ref.at_ref, bf16[1,2,4,4096]{3,2,1,0:T(4,128)(2,1)S(1)} %copy-done.4, s32[256,128]{1,0:T(8,128)S(1)} %bitcast.17, bf16[1024,272]{1,0:T(8,128)(2,1)S(1)} %copy-done), custom_call_target="tpu_custom_call" | custom-call | flops 71303168 | bytes 1277960 | tf_op jit(solution)/shard_map/pallas_call | solution.py:184
  5.4 16.5 %all-to-all-start = ((bf16[32,64,128]{2,1,0:T(8,128)(2,1)}), bf16[32,64,128]{2,1,0:T(8,128)(2,1)S(1)}, u32[]{:S(2)}, u32[]{:S(2)}) async-start(bf16[32,64,128]{2,1,0:T(8,128)(2,1)} %bitcast.3), calls=%async_computation | async-start | bytes 1048576 | tf_op jit(solution)/shard_map/all_to_all | solution.py:208
  21.9 0.0 copy-done.2
  21.9 5.3 %collective-permute-start.1 = (s32[256,128]{1,0:T(8,128)S(1)}, s32[256,128]{1,0:T(8,128)S(1)}, u32[]{:S(2)}, u32[]{:S(2)}) collective-permute-start(s32[256,128]{1,0:T(8,128)S(1)} %bitcast.18), channel_id=1, source_target_pairs={{8,0},{16,8},{24,16},{0,24},{9,1},{17,9},{25,17},{1,25},{10,2},{18... | collective-permute-start | bytes 393224 | tf_op jit(solution)/shard_map/ppermute | solution.py:202
  27.2 1.9 %collective-permute-start = (s32[256,128]{1,0:T(8,128)S(1)}, s32[256,128]{1,0:T(8,128)S(1)}, u32[]{:S(2)}, u32[]{:S(2)}) collective-permute-start(s32[256,128]{1,0:T(8,128)S(1)} %bitcast.19), channel_id=1, source_target_pairs={{0,8},{8,16},{16,24},{24,0},{1,9},{9,17},{17,25},{25,1},{2,10},{10... | collective-permute-start | bytes 393224 | tf_op jit(solution)/shard_map/ppermute | solution.py:201
  29.2 0.0 copy-done.3
  29.2 1.5 %shard_map.69.act_ref = bf16[96,4096]{1,0:T(8,128)(2,1)S(1)} custom-call(bf16[1024,128]{1,0:T(8,128)(2,1)S(1)} %bitcast.22), custom_call_target="tpu_custom_call" | custom-call | flops 100663296 | bytes 1048576 | tf_op jit(solution)/shard_map/pallas_call | solution.py:184
  30.7 11.3 %collective-permute-done.1.down_ref = s32[256,128]{1,0:T(8,128)S(1)} collective-permute-done((s32[256,128]{1,0:T(8,128)S(1)}, s32[256,128]{1,0:T(8,128)S(1)}, u32[]{:S(2)}, u32[]{:S(2)}) %collective-permute-start.1) | collective-permute-done | bytes 131104 | tf_op jit(solution)/shard_map/ppermute | solution.py:202
  42.0 0.0 collective-permute-done.up_ref
  42.0 0.8 all-to-all-done
  42.8 2.5 %shard_map.70 = (f32[512,128]{1,0:T(8,128)S(1)}, bf16[64,9216]{1,0:T(8,128)(2,1)S(1)}) custom-call(s32[2]{0:T(128)S(1)} %pad_add_fusion.sz_ref.at_ref, bf16[2048,128]{1,0:T(8,128)(2,1)S(1)} %bitcast.15, s32[256,128]{1,0:T(8,128)S(1)} %bitcast.20, s32[256,128]{1,0:T(8,128)S(1)} %collective-permute-done.up_ref, ...), custom_call_target="tpu_custom_call" | custom-call | flops 452984832 | bytes 3145736 | tf_op jit(solution)/shard_map/pallas_call | solution.py:184
  45.3 0.0 copy-start.5
  45.3 12.9 %all_to_all.25 = f32[16,32,128]{2,1,0:T(8,128)S(1)} all-to-all(f32[16,32,128]{2,1,0:T(8,128)S(1)} %bitcast.21), channel_id=1, replica_groups=mesh['sample'=16,'sy'=4,'sz'=8] {'sample'}, dimensions={0} | all-to-all | bytes 524288 | tf_op jit(solution)/shard_map/all_to_all | solution.py:221
  58.3 13.8 %all_to_all.26 = f32[8,32,128]{2,1,0:T(8,128)S(1)} all-to-all(f32[8,32,128]{2,1,0:T(8,128)S(1)} %broadcast_in_dim.6), channel_id=1, replica_groups=mesh['sample'=16,'sy'=4,'sz'=8] {'sz'}, dimensions={0} | all-to-all | bytes 262144 | tf_op jit(solution)/shard_map/all_to_all | solution.py:223
  72.1 10.2 %all_to_all.27 = f32[4,32,128]{2,1,0:T(8,128)S(1)} all-to-all(f32[4,32,128]{2,1,0:T(8,128)S(1)} %broadcast_in_dim.7), channel_id=1, replica_groups=mesh['sample'=16,'sy'=4,'sz'=8] {'sy'}, dimensions={0} | all-to-all | bytes 131072 | tf_op jit(solution)/shard_map/all_to_all | solution.py:223
  82.4 0.7 broadcast_in_dim.8
  83.1 7.1 %all-to-all-start.4 = ((f32[16,32,128]{2,1,0:T(8,128)}), f32[16,32,128]{2,1,0:T(8,128)S(1)}, u32[]{:S(2)}, u32[]{:S(2)}) async-start(f32[16,32,128]{2,1,0:T(8,128)} %broadcast_in_dim.8), calls=%async_computation.4 | async-start | bytes 524288 | tf_op jit(solution)/shard_map/all_to_all | solution.py:224
  90.2 0.0 copy-done.5
  90.2 2.3 %shard_map.71 = bf16[1024,128]{1,0:T(8,128)(2,1)} custom-call(bf16[64,9216]{1,0:T(8,128)(2,1)S(1)} %get-tuple-element.4.g_ref, bf16[27,32,64]{2,1,0:T(8,128)(2,1)S(1)} %bitcast.23), custom_call_target="tpu_custom_call" | custom-call | flops 452984832 | bytes 1552384 | tf_op jit(solution)/shard_map/pallas_call | solution.py:184
  92.5 4.9 %all-to-all-done.4 = f32[16,32,128]{2,1,0:T(8,128)S(1)} async-done(((f32[16,32,128]{2,1,0:T(8,128)}), f32[16,32,128]{2,1,0:T(8,128)S(1)}, u32[]{:S(2)}, u32[]{:S(2)}) %all-to-all-start.4) | async-done | bytes 262176 | tf_op jit(solution)/shard_map/all_to_all | solution.py:224
  97.4 0.9 shard_map.72
  (5 shorter events, 0.1 us)
Async XLA Ops:
  0.7 1.1 %copy-start = (bf16[1024,272]{1,0:T(8,128)(2,1)S(1)}, bf16[1024,272]{1,0:T(8,128)(2,1)}, u32[]{:S(2)}) copy-start(bf16[1024,272]{1,0:T(8,128)(2,1)} %constant.12.clone.sel_ref) | copy-start | bytes 1671172
  1.8 0.9 copy-start.1
  2.7 0.8 copy-start.4
  3.6 18.3 %copy-start.2 = (s32[1,64,1,512]{3,2,1,0:T(1,128)S(1)}, s32[1,64,1,512]{3,2,1,0:T(1,128)}, u32[]{:S(2)}) copy-start(s32[1,64,1,512]{3,2,1,0:T(1,128)} %param.8) | copy-start | bytes 393220
  3.6 25.6 %copy-start.3 = (bf16[1,32,2,16,128]{4,3,2,1,0:T(8,128)(2,1)S(1)}, bf16[1,32,2,16,128]{4,3,2,1,0:T(8,128)(2,1)}, u32[]{:S(2)}) copy-start(bf16[1,32,2,16,128]{4,3,2,1,0:T(8,128)(2,1)} %param.5) | copy-start | bytes 786436
  5.4 37.4 %all-to-all-start = ((bf16[32,64,128]{2,1,0:T(8,128)(2,1)}), bf16[32,64,128]{2,1,0:T(8,128)(2,1)S(1)}, u32[]{:S(2)}, u32[]{:S(2)}) async-start(bf16[32,64,128]{2,1,0:T(8,128)(2,1)} %bitcast.3), calls=%async_computation | async-start | bytes 1048576 | tf_op jit(solution)/shard_map/all_to_all | solution.py:208
  21.9 20.1 %collective-permute-start.1 = (s32[256,128]{1,0:T(8,128)S(1)}, s32[256,128]{1,0:T(8,128)S(1)}, u32[]{:S(2)}, u32[]{:S(2)}) collective-permute-start(s32[256,128]{1,0:T(8,128)S(1)} %bitcast.18), channel_id=1, source_target_pairs={{8,0},{16,8},{24,16},{0,24},{9,1},{17,9},{25,17},{1,25},{10,2},{18... | collective-permute-start | bytes 393224 | tf_op jit(solution)/shard_map/ppermute | solution.py:202
  27.2 14.8 %collective-permute-start = (s32[256,128]{1,0:T(8,128)S(1)}, s32[256,128]{1,0:T(8,128)S(1)}, u32[]{:S(2)}, u32[]{:S(2)}) collective-permute-start(s32[256,128]{1,0:T(8,128)S(1)} %bitcast.19), channel_id=1, source_target_pairs={{0,8},{8,16},{16,24},{24,0},{1,9},{9,17},{17,25},{25,1},{2,10},{10... | collective-permute-start | bytes 393224 | tf_op jit(solution)/shard_map/ppermute | solution.py:201
  45.3 44.8 %copy-start.5 = (bf16[64,32,3,3,3]{0,1,4,3,2:T(8,128)(2,1)S(1)}, bf16[64,32,3,3,3]{0,1,4,3,2:T(8,128)(2,1)}, u32[]{:S(2)}) copy-start(bf16[64,32,3,3,3]{0,1,4,3,2:T(8,128)(2,1)} %param.6) | copy-start | bytes 331780
  83.1 14.3 %all-to-all-start.4 = ((f32[16,32,128]{2,1,0:T(8,128)}), f32[16,32,128]{2,1,0:T(8,128)S(1)}, u32[]{:S(2)}, u32[]{:S(2)}) async-start(f32[16,32,128]{2,1,0:T(8,128)} %broadcast_in_dim.8), calls=%async_computation.4 | async-start | bytes 524288 | tf_op jit(solution)/shard_map/all_to_all | solution.py:224

commit v2 on v1

--- a/solution.py
+++ b/solution.py
@@ -12,6 +12,7 @@
 CIN, COUT = 32, 64
 ROWS = 16
 F32, BF16 = jnp.float32, jnp.bfloat16
+PACK, TAPS = int(2e10), int(1e10)
 LIMIT = 24 * 1024 * 1024
 
 
@@ -37,7 +38,14 @@
     return pltpu.roll(value, 64, 1)
 
 
-def pack_kernel(sz_ref, pg_ref, am_ref, sel_ref, out_ref, tiles):
+def pack_kernel(sz_ref, pg_any, am_any, sel_any, out_ref, tiles, pg_ref, am_ref, sel_ref, sems):
+    copies = [
+        pltpu.make_async_copy(src, dst, sems.at[k])
+        for k, (src, dst) in enumerate(((pg_any, pg_ref), (am_any, am_ref), (sel_any, sel_ref)))
+    ]
+    for copy in copies:
+        copy.start()
+    copies[0].wait()
     low = halves((8, 128))
     pooled = jnp.concatenate([pg_ref[0, 0].astype(F32), pg_ref[0, 1].astype(F32)], axis=0)
     tiles[...] = jnp.zeros_like(tiles)
@@ -46,7 +54,9 @@
         tile = pooled[:, k * 128:(k + 1) * 128] if k < 32 else jnp.zeros((8, 128), F32)
         tiles[pl.ds(k, 8, stride=33), :] = roll64(jnp.where(low, tile, before))
         before = tile
+    copies[2].wait()
     sent = jnp.dot(sel_ref[...], tiles[...].astype(BF16), preferred_element_type=F32).astype(BF16)
+    copies[1].wait()
     low = halves((32, 128))
     first = am_ref[pl.ds(0, 64, stride=4), :].astype(F32)
     last = am_ref[pl.ds(3, 64, stride=4), :].astype(F32)
@@ -62,11 +72,14 @@
                 out_ref[pl.ds(block * 32 + 16, 16), :] = codes[ch * 16:(ch + 1) * 16]
 
 
-def taps_kernel(act_ref, out_ref, wide):
+def taps_kernel(act_ref, below_ref, above_ref, out_ref, codes_ref, wide):
     src = lax.broadcasted_iota(jnp.int32, (128, 128), 0)
     lane = lax.broadcasted_iota(jnp.int32, (128, 128), 1)
     place = 2 * (lane % 64) + lane // 64
     act = act_ref[...]
+    for t in range(4):
+        codes_ref[t] = below_ref[pl.ds(t, 64, stride=4), :]
+        codes_ref[4 + t] = above_ref[pl.ds(t, 64, stride=4), :]
     for c in range(3):
         pick = (src == place + (c - 1)).astype(F32).astype(BF16)
         wide[...] = jnp.dot(act, pick, preferred_element_type=F32)
@@ -75,7 +88,7 @@
             out_ref[c * 32:(c + 1) * 32, yz * 128:(yz + 1) * 128] = rows.astype(BF16)
 
 
-def main_kernel(at_ref, recv_ref, own_ref, up_ref, down_ref, act_ref, dw_ref, g_ref, rows):
+def main_kernel(at_ref, recv_ref, own_ref, near_ref, act_ref, dw_ref, g_ref, rows):
     my_sy, my_sz = at_ref[0], at_ref[1]
     rows[...] = recv_ref[...].astype(F32)
     low = halves((64, 128))
@@ -96,7 +109,7 @@
             [jnp.where(low32, packed, other), jnp.where(low32, other, packed)], axis=0
         ).astype(jnp.int32)
 
-    for dy, (source, levels) in enumerate(((up_ref, (1,)), (own_ref, (0, 1)), (down_ref, (0,)))):
+    for dy, levels in enumerate(((1,), (0, 1), (0,))):
         before = halo(my_sy + dy - 1, my_sz - 1)
         after = halo(my_sy + dy - 1, my_sz + 1)
         codes = None
@@ -111,7 +124,8 @@
                 code = after
             else:
                 if pz % 2 == 1:
-                    codes = source[pl.ds((pz - 1) // 2, 64, stride=4), :]
+                    t = (pz - 1) // 2
+                    codes = own_ref[pl.ds(t, 64, stride=4), :] if dy == 1 else near_ref[2 * dy + t]
                 code = spread(codes, pz % 2 == 1)
             code = code - parity
             for a in levels:
@@ -175,9 +189,9 @@
             out_ref[3 * ab + c] = part[c * 32:(c + 1) * 32]
 
 
-def call(kernel, outs, scratch, args, smem=False, flops=0):
+def call(kernel, outs, scratch, args, smem=False, flops=0, hbm=False):
     vmem = pl.BlockSpec(memory_space=pltpu.VMEM)
-    specs = [vmem] * len(args)
+    specs = [pl.BlockSpec(memory_space=pltpu.HBM) if hbm else vmem] * len(args)
     if smem:
         specs[0] = pl.BlockSpec(memory_space=pltpu.SMEM)
     nbytes = sum(int(np.prod(v.shape)) * v.dtype.itemsize for v in list(args) + list(outs))
@@ -187,7 +201,7 @@
         in_specs=specs,
         out_specs=tuple([vmem] * len(outs)) if len(outs) > 1 else vmem,
         scratch_shapes=scratch,
-        compiler_params=pltpu.CompilerParams(vmem_limit_bytes=LIMIT),
+        compiler_params=pltpu.CompilerParams(vmem_limit_bytes=60 * 1024 * 1024 if hbm else LIMIT),
         cost_estimate=pl.CostEstimate(flops=flops, bytes_accessed=nbytes, transcendentals=0),
     )(*args)
 
@@ -202,17 +216,20 @@
     above = lax.ppermute(codes, "sy", fall)
     sel = jnp.asarray(selection(), BF16)
     sent = call(
-        pack_kernel, [shape((2048, 128), BF16)], [pltpu.VMEM((272, 128), F32)],
-        (at, pooled_grad, codes, sel), smem=True, flops=2 * 1024 * 272 * 128,
+        pack_kernel, [shape((2048, 128), BF16)], [
+            pltpu.VMEM((272, 128), F32), pltpu.VMEM((1, 2, SY, 4096), BF16), pltpu.VMEM((256, 128), jnp.int32),
+            pltpu.VMEM((1024, 272), BF16), pltpu.SemaphoreType.DMA((3,)),
+        ],
+        (at, pooled_grad, codes, sel), smem=True, flops=PACK, hbm=True,
     )
     recv = lax.all_to_all(sent.reshape(32, 64, 128), ("sy", "sz"), 0, 0).reshape(2048, 128)
-    taps = call(
-        taps_kernel, [shape((96, 4096), BF16)], [pltpu.VMEM((1024, 128), F32)],
-        (activations.reshape(1024, 128),), flops=2 * 1024 * 128 * 384,
+    taps, near = call(
+        taps_kernel, [shape((96, 4096), BF16), shape((8, 64, 128), jnp.int32)], [pltpu.VMEM((1024, 128), F32)],
+        (activations.reshape(1024, 128), below, above), flops=TAPS,
     )
     local, grad_out = call(
         main_kernel, [shape((512, 128), F32), shape((COUT, 72 * 128), BF16)], [pltpu.VMEM((2048, 128), F32)],
-        (at, recv, codes, below, above, taps), smem=True, flops=2 * 96 * 576 * 4096,
+        (at, recv, codes, near, taps), smem=True, flops=2 * 96 * 576 * 4096,
     )
     input_grad = call(
         input_kernel, [shape((1024, 128), BF16)], [pltpu.VMEM((1024, 128), F32)],

time: 98.8 us -> 99.9 us (1.011)
  waiting for transfers between devices: 17 us -> 21 us
  local copies, waits for them, and re-layouts: 3.64 us -> 0.77 us
  Pallas kernels: 9.08 us -> 10.5 us
  blocking collectives: 37 us -> 35.9 us
  starting transfers between devices: 30.8 us -> 29.8 us
    all_to_all x1, waiting for transfers between devices: 0.77 us -> 16.1 us  [body(): lax.all_to_all(sent.reshape(32, 64, 128), ('sy', 'sz'), 0, 0)]
    ppermute x1, waiting for transfers between devices: 11.3 us -> 0.01 us  [body(): above = lax.ppermute(codes, 'sy', fall)]
    unnamed x12 -> x8, local copies, waits for them, and re-layouts: 2.89 us -> 0.02 us
    all_to_all x1, starting transfers between devices: 16.5 us -> 14.1 us  [body(): lax.all_to_all(sent.reshape(32, 64, 128), ('sy', 'sz'), 0, 0)]
    all_to_all x2, blocking collectives: 24.1 us -> 21.8 us  [body(): lax.all_to_all(jnp.broadcast_to(part[None], (size, 32, 128)), axis, 0, 0)]
    pallas_call x5, Pallas kernels: 9.08 us -> 10.5 us  [call(): pl.pallas_call(kernel, out_shape=tuple(outs) if len(outs) > 1 else outs[0...]
    ppermute x1, starting transfers between devices: 5.29 us -> 6.71 us  [body(): above = lax.ppermute(codes, 'sy', fall)]
    all_to_all x1, blocking collectives: 12.9 us -> 14 us  [body(): lax.all_to_all(local.reshape(SAMPLE, 32, 128), 'sample', 0, 0)]
  transfers between devices with their start and end apart: 4 -> 4, of which waited for: 3 -> 2; matrix products, arithmetic and copies ran while one was open for 0% -> 1% of each run, Pallas kernels for 4% -> 7%
where the time goes in v2:
time: 99.9 us; the launch traced here: 99.3 us
  blocking collectives  35.9 us (36%)
  starting transfers between devices  29.8 us (30%)
  waiting for transfers between devices  21 us (21%)
  Pallas kernels  10.5 us (11%)
    all_to_all x2, blocking collectives, body(): lax.all_to_all(jnp.broadcast_to(part[None], (size, 32, 128)), axis, 0, 0)  21.8 us
    all_to_all x1, waiting for transfers between devices, body(): lax.all_to_all(sent.reshape(32, 64, 128), ('sy', 'sz'), 0, 0)  16.1 us
    all_to_all x1, starting transfers between devices, body(): lax.all_to_all(sent.reshape(32, 64, 128), ('sy', 'sz'), 0, 0)  14.1 us
    all_to_all x1, blocking collectives, body(): lax.all_to_all(local.reshape(SAMPLE, 32, 128), 'sample', 0, 0)  14 us
    pallas_call x5, Pallas kernels, call(): pl.pallas_call(kernel, out_shape=tuple(outs) if len(outs) > 1 else outs[0...  10.5 us
    all_to_all x1, starting transfers between devices, body(): lax.all_to_all(jnp.broadcast_to(part[None], (SAMPLE, 32, 128)), 'sample',...  7.06 us
    ppermute x1, starting transfers between devices, body(): above = lax.ppermute(codes, 'sy', fall)  6.71 us
    all_to_all x1, waiting for transfers between devices, body(): lax.all_to_all(jnp.broadcast_to(part[None], (SAMPLE, 32, 128)), 'sample',...  4.95 us
  transfers between devices with their start and end apart: 4, of which 2 were waited for; matrix products, arithmetic and copies ran while one was open for 1% of the time, Pallas kernels for 7%

profile of v2, /device:TPU:1, one launch (start us, length us, event | category | flops | bytes accessed | tf_op | source)
XLA Modules:
  0.0 99.3 jit_solution(4486011389194929100)
XLA Ops:
  0.6 6.7 %collective-permute-start.1 = (s32[256,128]{1,0:T(8,128)}, s32[256,128]{1,0:T(8,128)S(1)}, u32[]{:S(2)}, u32[]{:S(2)}) collective-permute-start(s32[256,128]{1,0:T(8,128)} %bitcast.18), channel_id=1, source_target_pairs={{8,0},{16,8},{24,16},{0,24},{9,1},{17,9},{25,17},{1,25},{10,2},{18... | collective-permute-start | bytes 393224 | tf_op jit(solution)/shard_map/ppermute | solution.py:216
  7.4 1.9 %collective-permute-start = (s32[256,128]{1,0:T(8,128)}, s32[256,128]{1,0:T(8,128)S(1)}, u32[]{:S(2)}, u32[]{:S(2)}) collective-permute-start(s32[256,128]{1,0:T(8,128)} %bitcast.19), channel_id=1, source_target_pairs={{0,8},{8,16},{16,24},{24,0},{1,9},{9,17},{17,25},{25,1},{2,10},{10... | collective-permute-start | bytes 393224 | tf_op jit(solution)/shard_map/ppermute | solution.py:215
  9.3 0.6 pad_add_fusion.sz_ref.at_ref
  9.9 0.0 copy-start.2
  9.9 3.3 %shard_map.68 = bf16[2048,128]{1,0:T(8,128)(2,1)} custom-call(s32[2]{0:T(128)} %pad_add_fusion.sz_ref.at_ref, bf16[1,2,4,4096]{3,2,1,0:T(4,128)(2,1)} %pg_any.1, s32[256,128]{1,0:T(8,128)} %bitcast.20, bf16[1024,272]{1,0:T(8,128)(2,1)} %constant.12.clone.sel_any), custom_call_target="tpu_custom_call" | custom-call | flops 20000000000 | bytes 1277960 | tf_op jit(solution)/shard_map/pallas_call | solution.py:198
  13.2 14.1 %all-to-all-start = ((bf16[32,64,128]{2,1,0:T(8,128)(2,1)}), bf16[32,64,128]{2,1,0:T(8,128)(2,1)S(1)}, u32[]{:S(2)}, u32[]{:S(2)}) async-start(bf16[32,64,128]{2,1,0:T(8,128)(2,1)} %bitcast.24), calls=%async_computation | async-start | bytes 1048576 | tf_op jit(solution)/shard_map/all_to_all | solution.py:225
  27.3 0.0 collective-permute-done.1.above_ref
  27.3 0.0 collective-permute-done.below_ref
  27.3 0.0 copy-done.2
  27.3 0.0 copy-start
  27.3 0.0 copy-start.1
  27.3 1.6 %shard_map.69 = (bf16[96,4096]{1,0:T(8,128)(2,1)S(1)}, s32[8,64,128]{2,1,0:T(8,128)S(1)}) custom-call(bf16[1024,128]{1,0:T(8,128)(2,1)S(1)} %bitcast.22, s32[256,128]{1,0:T(8,128)S(1)} %collective-permute-done.below_ref, s32[256,128]{1,0:T(8,128)S(1)} %collective-permute-done.1.above_ref), custom_call_target="tpu_custom_call" | custom-call | flops 10000000000 | bytes 1572864 | tf_op jit(solution)/shard_map/pallas_call | solution.py:198
  28.9 16.1 %all-to-all-done = bf16[32,64,128]{2,1,0:T(8,128)(2,1)S(1)} async-done(((bf16[32,64,128]{2,1,0:T(8,128)(2,1)}), bf16[32,64,128]{2,1,0:T(8,128)(2,1)S(1)}, u32[]{:S(2)}, u32[]{:S(2)}) %all-to-all-start) | async-done | bytes 524320 | tf_op jit(solution)/shard_map/all_to_all | solution.py:225
  45.0 0.0 copy-done
  45.0 0.0 copy-done.1
  45.0 2.5 %shard_map.70 = (f32[512,128]{1,0:T(8,128)S(1)}, bf16[64,9216]{1,0:T(8,128)(2,1)S(1)}) custom-call(s32[2]{0:T(128)S(1)} %copy-done.1, bf16[2048,128]{1,0:T(8,128)(2,1)S(1)} %bitcast.15, s32[256,128]{1,0:T(8,128)S(1)} %bitcast.21, s32[8,64,128]{2,1,0:T(8,128)S(1)} %get-tuple-element.6.near_ref, bf16[96,4096]{1,0:T(8,128)(2,1)S(1)} %get-tuple-element.7.act_ref), custom_call_target="tpu_custom_call" | custom-call | flops 452984832 | bytes 3145736 | tf_op jit(solution)/shard_map/pallas_call | solution.py:198
  47.5 0.0 copy-start.3
  47.5 14.0 %all_to_all.25 = f32[16,32,128]{2,1,0:T(8,128)S(1)} all-to-all(f32[16,32,128]{2,1,0:T(8,128)S(1)} %bitcast.17), channel_id=1, replica_groups=mesh['sample'=16,'sy'=4,'sz'=8] {'sample'}, dimensions={0} | all-to-all | bytes 524288 | tf_op jit(solution)/shard_map/all_to_all | solution.py:238
  61.6 11.2 %all_to_all.26 = f32[8,32,128]{2,1,0:T(8,128)S(1)} all-to-all(f32[8,32,128]{2,1,0:T(8,128)S(1)} %broadcast_in_dim.6), channel_id=1, replica_groups=mesh['sample'=16,'sy'=4,'sz'=8] {'sz'}, dimensions={0} | all-to-all | bytes 262144 | tf_op jit(solution)/shard_map/all_to_all | solution.py:240
  72.8 10.6 %all_to_all.27 = f32[4,32,128]{2,1,0:T(8,128)S(1)} all-to-all(f32[4,32,128]{2,1,0:T(8,128)S(1)} %broadcast_in_dim.7), channel_id=1, replica_groups=mesh['sample'=16,'sy'=4,'sz'=8] {'sy'}, dimensions={0} | all-to-all | bytes 131072 | tf_op jit(solution)/shard_map/all_to_all | solution.py:240
  83.4 0.7 broadcast_in_dim.8
  84.2 7.1 %all-to-all-start.4 = ((f32[16,32,128]{2,1,0:T(8,128)}), f32[16,32,128]{2,1,0:T(8,128)S(1)}, u32[]{:S(2)}, u32[]{:S(2)}) async-start(f32[16,32,128]{2,1,0:T(8,128)} %broadcast_in_dim.8), calls=%async_computation.4 | async-start | bytes 524288 | tf_op jit(solution)/shard_map/all_to_all | solution.py:241
  91.2 0.0 copy-done.3
  91.2 2.3 %shard_map.71 = bf16[1024,128]{1,0:T(8,128)(2,1)} custom-call(bf16[64,9216]{1,0:T(8,128)(2,1)S(1)} %get-tuple-element.8.g_ref, bf16[27,32,64]{2,1,0:T(8,128)(2,1)S(1)} %bitcast.23), custom_call_target="tpu_custom_call" | custom-call | flops 452984832 | bytes 1552384 | tf_op jit(solution)/shard_map/pallas_call | solution.py:198
  93.5 4.9 %all-to-all-done.4 = f32[16,32,128]{2,1,0:T(8,128)S(1)} async-done(((f32[16,32,128]{2,1,0:T(8,128)}), f32[16,32,128]{2,1,0:T(8,128)S(1)}, u32[]{:S(2)}, u32[]{:S(2)}) %all-to-all-start.4) | async-done | bytes 262176 | tf_op jit(solution)/shard_map/all_to_all | solution.py:241
  98.4 0.9 shard_map.72
  (5 shorter events, 0.1 us)
Async XLA Ops:
  0.6 26.7 %collective-permute-start.1 = (s32[256,128]{1,0:T(8,128)}, s32[256,128]{1,0:T(8,128)S(1)}, u32[]{:S(2)}, u32[]{:S(2)}) collective-permute-start(s32[256,128]{1,0:T(8,128)} %bitcast.18), channel_id=1, source_target_pairs={{8,0},{16,8},{24,16},{0,24},{9,1},{17,9},{25,17},{1,25},{10,2},{18... | collective-permute-start | bytes 393224 | tf_op jit(solution)/shard_map/ppermute | solution.py:216
  7.4 19.9 %collective-permute-start = (s32[256,128]{1,0:T(8,128)}, s32[256,128]{1,0:T(8,128)S(1)}, u32[]{:S(2)}, u32[]{:S(2)}) collective-permute-start(s32[256,128]{1,0:T(8,128)} %bitcast.19), channel_id=1, source_target_pairs={{0,8},{8,16},{16,24},{24,0},{1,9},{9,17},{17,25},{25,1},{2,10},{10... | collective-permute-start | bytes 393224 | tf_op jit(solution)/shard_map/ppermute | solution.py:215
  9.9 17.4 %copy-start.2 = (bf16[1,32,2,16,128]{4,3,2,1,0:T(8,128)(2,1)S(1)}, bf16[1,32,2,16,128]{4,3,2,1,0:T(8,128)(2,1)}, u32[]{:S(2)}) copy-start(bf16[1,32,2,16,128]{4,3,2,1,0:T(8,128)(2,1)} %param.5) | copy-start | bytes 786436
  13.2 31.8 %all-to-all-start = ((bf16[32,64,128]{2,1,0:T(8,128)(2,1)}), bf16[32,64,128]{2,1,0:T(8,128)(2,1)S(1)}, u32[]{:S(2)}, u32[]{:S(2)}) async-start(bf16[32,64,128]{2,1,0:T(8,128)(2,1)} %bitcast.24), calls=%async_computation | async-start | bytes 1048576 | tf_op jit(solution)/shard_map/all_to_all | solution.py:225
  27.3 17.7 %copy-start = (s32[1,64,1,512]{3,2,1,0:T(1,128)S(1)}, s32[1,64,1,512]{3,2,1,0:T(1,128)}, u32[]{:S(2)}) copy-start(s32[1,64,1,512]{3,2,1,0:T(1,128)} %param.8) | copy-start | bytes 393220
  27.3 17.7 %copy-start.1 = (s32[2]{0:T(128)S(1)}, s32[2]{0:T(128)}, u32[]{:S(2)}) copy-start(s32[2]{0:T(128)} %pad_add_fusion.sz_ref.at_ref) | copy-start | bytes 28
  47.5 43.7 %copy-start.3 = (bf16[64,32,3,3,3]{0,1,4,3,2:T(8,128)(2,1)S(1)}, bf16[64,32,3,3,3]{0,1,4,3,2:T(8,128)(2,1)}, u32[]{:S(2)}) copy-start(bf16[64,32,3,3,3]{0,1,4,3,2:T(8,128)(2,1)} %param.6) | copy-start | bytes 331780
  84.2 14.3 %all-to-all-start.4 = ((f32[16,32,128]{2,1,0:T(8,128)}), f32[16,32,128]{2,1,0:T(8,128)S(1)}, u32[]{:S(2)}, u32[]{:S(2)}) async-start(f32[16,32,128]{2,1,0:T(8,128)} %broadcast_in_dim.8), calls=%async_computation.4 | async-start | bytes 524288 | tf_op jit(solution)/shard_map/all_to_all | solution.py:241

commit v3 on v2

--- a/solution.py
+++ b/solution.py
@@ -12,7 +12,6 @@
 CIN, COUT = 32, 64
 ROWS = 16
 F32, BF16 = jnp.float32, jnp.bfloat16
-PACK, TAPS = int(2e10), int(1e10)
 LIMIT = 24 * 1024 * 1024
 
 
@@ -38,7 +37,7 @@
     return pltpu.roll(value, 64, 1)
 
 
-def pack_kernel(sz_ref, pg_any, am_any, sel_any, out_ref, tiles, pg_ref, am_ref, sel_ref, sems):
+def pack_kernel(pg_any, am_any, sel_any, out_ref, codes_ref, tiles, pg_ref, am_ref, sel_ref, sems):
     copies = [
         pltpu.make_async_copy(src, dst, sems.at[k])
         for k, (src, dst) in enumerate(((pg_any, pg_ref), (am_any, am_ref), (sel_any, sel_ref)))
@@ -58,28 +57,27 @@
     sent = jnp.dot(sel_ref[...], tiles[...].astype(BF16), preferred_element_type=F32).astype(BF16)
     copies[1].wait()
     low = halves((32, 128))
-    first = am_ref[pl.ds(0, 64, stride=4), :].astype(F32)
-    last = am_ref[pl.ds(3, 64, stride=4), :].astype(F32)
+    codes = [am_ref[pl.ds(t, 64, stride=4), :].astype(F32) for t in range(4)]
+    for t in range(4):
+        codes_ref[t * 64:(t + 1) * 64] = codes[t].astype(BF16)
+    first, last = codes[0], codes[3]
     leading = jnp.where(low, first[:32], roll64(first[32:]))
     ending = jnp.where(low, roll64(last[:32]), last[32:])
-    me = sz_ref[1]
+    me = lax.axis_index("sz")
     for sz in range(SZ):
-        codes = jnp.where(sz < me, leading, ending).astype(BF16)
+        edge = jnp.where(sz < me, leading, ending).astype(BF16)
         for sy in range(SY):
             for ch in range(2):
                 block = (sy * SZ + sz) * 2 + ch
                 out_ref[pl.ds(block * 32, 16), :] = sent[block * 16:(block + 1) * 16]
-                out_ref[pl.ds(block * 32 + 16, 16), :] = codes[ch * 16:(ch + 1) * 16]
-
-
-def taps_kernel(act_ref, below_ref, above_ref, out_ref, codes_ref, wide):
+                out_ref[pl.ds(block * 32 + 16, 16), :] = edge[ch * 16:(ch + 1) * 16]
+
+
+def taps_kernel(act_ref, out_ref, wide):
     src = lax.broadcasted_iota(jnp.int32, (128, 128), 0)
     lane = lax.broadcasted_iota(jnp.int32, (128, 128), 1)
     place = 2 * (lane % 64) + lane // 64
     act = act_ref[...]
-    for t in range(4):
-        codes_ref[t] = below_ref[pl.ds(t, 64, stride=4), :]
-        codes_ref[4 + t] = above_ref[pl.ds(t, 64, stride=4), :]
     for c in range(3):
         pick = (src == place + (c - 1)).astype(F32).astype(BF16)
         wide[...] = jnp.dot(act, pick, preferred_element_type=F32)
@@ -88,12 +86,12 @@
             out_ref[c * 32:(c + 1) * 32, yz * 128:(yz + 1) * 128] = rows.astype(BF16)
 
 
-def main_kernel(at_ref, recv_ref, own_ref, near_ref, act_ref, dw_ref, g_ref, rows):
-    my_sy, my_sz = at_ref[0], at_ref[1]
+def main_kernel(recv_ref, own_ref, below_ref, above_ref, act_ref, dw_ref, g_ref, rows):
+    my_sy, my_sz = lax.axis_index("sy"), lax.axis_index("sz")
     rows[...] = recv_ref[...].astype(F32)
     low = halves((64, 128))
     low32 = halves((32, 128))
-    parity = jnp.where(low, 0, 1)
+    parity = jnp.where(low, 0.0, 1.0)
 
     def spread(value, first):
         other = roll64(value)
@@ -107,9 +105,9 @@
         other = roll64(packed)
         return jnp.concatenate(
             [jnp.where(low32, packed, other), jnp.where(low32, other, packed)], axis=0
-        ).astype(jnp.int32)
-
-    for dy, levels in enumerate(((1,), (0, 1), (0,))):
+        )
+
+    for dy, (source, levels) in enumerate(((below_ref, (1,)), (own_ref, (0, 1)), (above_ref, (0,)))):
         before = halo(my_sy + dy - 1, my_sz - 1)
         after = halo(my_sy + dy - 1, my_sz + 1)
         codes = None
@@ -125,7 +123,7 @@
             else:
                 if pz % 2 == 1:
                     t = (pz - 1) // 2
-                    codes = own_ref[pl.ds(t, 64, stride=4), :] if dy == 1 else near_ref[2 * dy + t]
+                    codes = source[t * 64:(t + 1) * 64].astype(F32)
                 code = spread(codes, pz % 2 == 1)
             code = code - parity
             for a in levels:
@@ -133,7 +131,7 @@
                 for b in ((1,) if pz == 0 else (0,) if pz == 9 else (0, 1)):
                     z = 2 * pz - 1 + b
                     cell = (y * 18 + z) * 128
-                    g_ref[:, cell:cell + 128] = jnp.where(code == 4 * a + 2 * b, value, 0.0).astype(BF16)
+                    g_ref[:, cell:cell + 128] = jnp.where(code == float(4 * a + 2 * b), value, 0.0).astype(BF16)
 
     total = jnp.zeros((96, 576), F32)
     depth = 4
@@ -189,11 +187,9 @@
             out_ref[3 * ab + c] = part[c * 32:(c + 1) * 32]
 
 
-def call(kernel, outs, scratch, args, smem=False, flops=0, hbm=False):
+def call(kernel, outs, scratch, args, flops=0, hbm=False):
     vmem = pl.BlockSpec(memory_space=pltpu.VMEM)
     specs = [pl.BlockSpec(memory_space=pltpu.HBM) if hbm else vmem] * len(args)
-    if smem:
-        specs[0] = pl.BlockSpec(memory_space=pltpu.SMEM)
     nbytes = sum(int(np.prod(v.shape)) * v.dtype.itemsize for v in list(args) + list(outs))
     return pl.pallas_call(
         kernel,
@@ -208,28 +204,27 @@
 
 def body(activations, weight, pooled_grad, window_argmax):
     shape = jax.ShapeDtypeStruct
-    at = jnp.stack([lax.axis_index("sy"), lax.axis_index("sz")]).astype(jnp.int32)
-    codes = window_argmax.reshape(256, 128)
     rise = [(i, (i + 1) % SY) for i in range(SY)]
     fall = [(j, i) for i, j in rise]
-    below = lax.ppermute(codes, "sy", rise)
-    above = lax.ppermute(codes, "sy", fall)
     sel = jnp.asarray(selection(), BF16)
-    sent = call(
-        pack_kernel, [shape((2048, 128), BF16)], [
+    sent, codes = call(
+        pack_kernel, [shape((2048, 128), BF16), shape((256, 128), BF16)],
+        [
             pltpu.VMEM((272, 128), F32), pltpu.VMEM((1, 2, SY, 4096), BF16), pltpu.VMEM((256, 128), jnp.int32),
             pltpu.VMEM((1024, 272), BF16), pltpu.SemaphoreType.DMA((3,)),
         ],
-        (at, pooled_grad, codes, sel), smem=True, flops=PACK, hbm=True,
-    )
+        (pooled_grad, window_argmax.reshape(256, 128), sel), flops=2 * 1024 * 272 * 128, hbm=True,
+    )
+    below = lax.ppermute(codes, "sy", rise)
+    above = lax.ppermute(codes, "sy", fall)
     recv = lax.all_to_all(sent.reshape(32, 64, 128), ("sy", "sz"), 0, 0).reshape(2048, 128)
-    taps, near = call(
-        taps_kernel, [shape((96, 4096), BF16), shape((8, 64, 128), jnp.int32)], [pltpu.VMEM((1024, 128), F32)],
-        (activations.reshape(1024, 128), below, above), flops=TAPS,
+    taps = call(
+        taps_kernel, [shape((96, 4096), BF16)], [pltpu.VMEM((1024, 128), F32)],
+        (activations.reshape(1024, 128),), flops=2 * 1024 * 128 * 384,
     )
     local, grad_out = call(
         main_kernel, [shape((512, 128), F32), shape((COUT, 72 * 128), BF16)], [pltpu.VMEM((2048, 128), F32)],
-        (at, recv, codes, near, taps), smem=True, flops=2 * 96 * 576 * 4096,
+        (recv, codes, below, above, taps), flops=2 * 96 * 576 * 4096,
     )
     input_grad = call(
         input_kernel, [shape((1024, 128), BF16)], [pltpu.VMEM((1024, 128), F32)],

time: 99.9 us -> 93.5 us (0.936)
  waiting for transfers between devices: 21 us -> 15.3 us
  Pallas kernels: 10.5 us -> 9.24 us
  starting transfers between devices: 29.8 us -> 30.9 us
    all_to_all x1, waiting for transfers between devices: 16.1 us -> 1.81 us  [body(): lax.all_to_all(sent.reshape(32, 64, 128), ('sy', 'sz'), 0, 0)]
    ppermute x1, waiting for transfers between devices: 0.01 us -> 8.51 us  [body(): above = lax.ppermute(codes, 'sy', fall)]
    all_to_all x1, starting transfers between devices: 14.1 us -> 16.7 us  [body(): lax.all_to_all(sent.reshape(32, 64, 128), ('sy', 'sz'), 0, 0)]
    ppermute x1, starting transfers between devices: 6.71 us -> 5.29 us  [body(): above = lax.ppermute(codes, 'sy', fall)]
    pallas_call x5, Pallas kernels: 10.5 us -> 9.24 us  [call(): pl.pallas_call(kernel, out_shape=tuple(outs) if len(outs) > 1 else outs[0...]
  transfers between devices with their start and end apart: 4 -> 4, of which waited for: 2 -> 3; matrix products, arithmetic and copies ran while one was open for 1% -> 0% of each run, Pallas kernels for 7% -> 4%
where the time goes in v3:
time: 93.5 us; the launch traced here: 93 us
  blocking collectives  36 us (39%)
  starting transfers between devices  30.9 us (33%)
  waiting for transfers between devices  15.3 us (16%)
  Pallas kernels  9.24 us (10%)
    all_to_all x2, blocking collectives, body(): lax.all_to_all(jnp.broadcast_to(part[None], (size, 32, 128)), axis, 0, 0)  22.3 us
    all_to_all x1, starting transfers between devices, body(): lax.all_to_all(sent.reshape(32, 64, 128), ('sy', 'sz'), 0, 0)  16.7 us
    all_to_all x1, blocking collectives, body(): lax.all_to_all(local.reshape(SAMPLE, 32, 128), 'sample', 0, 0)  13.7 us
    pallas_call x5, Pallas kernels, call(): pl.pallas_call(kernel, out_shape=tuple(outs) if len(outs) > 1 else outs[0...  9.24 us
    ppermute x1, waiting for transfers between devices, body(): above = lax.ppermute(codes, 'sy', fall)  8.51 us
    all_to_all x1, starting transfers between devices, body(): lax.all_to_all(jnp.broadcast_to(part[None], (SAMPLE, 32, 128)), 'sample',...  7.06 us
    ppermute x1, starting transfers between devices, body(): above = lax.ppermute(codes, 'sy', fall)  5.29 us
    all_to_all x1, waiting for transfers between devices, body(): lax.all_to_all(jnp.broadcast_to(part[None], (SAMPLE, 32, 128)), 'sample',...  4.95 us
  transfers between devices with their start and end apart: 4, of which 3 were waited for; matrix products, arithmetic and copies ran while one was open for 0% of the time, Pallas kernels for 4%

profile of v3, /device:TPU:1, one launch (start us, length us, event | category | flops | bytes accessed | tf_op | source)
XLA Modules:
  0.0 93.0 jit_solution(15485767732332011682)
XLA Ops:
  0.6 0.0 copy-start
  0.6 2.6 %shard_map.68 = (bf16[2048,128]{1,0:T(8,128)(2,1)}, bf16[256,128]{1,0:T(8,128)(2,1)}) custom-call(bf16[1,2,4,4096]{3,2,1,0:T(4,128)(2,1)} %pg_any.1, s32[256,128]{1,0:T(8,128)} %bitcast.20, bf16[1024,272]{1,0:T(8,128)(2,1)} %constant.4.clone.sel_any), custom_call_target="tpu_custom_call" | custom-call | flops 71303168 | bytes 1343488 | tf_op jit(solution)/shard_map/pallas_call | solution.py:194
  3.2 0.0 copy-start.2
  3.2 16.7 %all-to-all-start = ((bf16[32,64,128]{2,1,0:T(8,128)(2,1)}), bf16[32,64,128]{2,1,0:T(8,128)(2,1)S(1)}, u32[]{:S(2)}, u32[]{:S(2)}) async-start(bf16[32,64,128]{2,1,0:T(8,128)(2,1)} %bitcast.18), calls=%async_computation | async-start | bytes 1048576 | tf_op jit(solution)/shard_map/all_to_all | solution.py:220
  19.9 5.3 %collective-permute-start.1 = (bf16[256,128]{1,0:T(8,128)(2,1)}, bf16[256,128]{1,0:T(8,128)(2,1)S(1)}, u32[]{:S(2)}, u32[]{:S(2)}) collective-permute-start(bf16[256,128]{1,0:T(8,128)(2,1)} %get-tuple-element.7.own_ref), channel_id=1, source_target_pairs={{8,0},{16,8},{24,16},{0,24},{9,1},{17,9},{25,17},{1,25},{10,2},{18... | collective-permute-start | bytes 196616 | tf_op jit(solution)/shard_map/ppermute | solution.py:219
  25.2 1.9 %collective-permute-start = (bf16[256,128]{1,0:T(8,128)(2,1)}, bf16[256,128]{1,0:T(8,128)(2,1)S(1)}, u32[]{:S(2)}, u32[]{:S(2)}) collective-permute-start(bf16[256,128]{1,0:T(8,128)(2,1)} %get-tuple-element.7.own_ref), channel_id=1, source_target_pairs={{0,8},{8,16},{16,24},{24,0},{1,9},{9,17},{17,25},{25,1},{2,10},{10... | collective-permute-start | bytes 196616 | tf_op jit(solution)/shard_map/ppermute | solution.py:218
  27.1 0.0 copy-done
  27.1 1.5 %shard_map.69.act_ref = bf16[96,4096]{1,0:T(8,128)(2,1)S(1)} custom-call(bf16[1024,128]{1,0:T(8,128)(2,1)S(1)} %bitcast.16), custom_call_target="tpu_custom_call" | custom-call | flops 100663296 | bytes 1048576 | tf_op jit(solution)/shard_map/pallas_call | solution.py:194
  28.7 8.5 %collective-permute-done.1.above_ref = bf16[256,128]{1,0:T(8,128)(2,1)S(1)} collective-permute-done((bf16[256,128]{1,0:T(8,128)(2,1)}, bf16[256,128]{1,0:T(8,128)(2,1)S(1)}, u32[]{:S(2)}, u32[]{:S(2)}) %collective-permute-start.1) | collective-permute-done | bytes 65568 | tf_op jit(solution)/shard_map/ppermute | solution.py:219
  37.2 0.0 collective-permute-done.below_ref
  37.2 1.8 %all-to-all-done = bf16[32,64,128]{2,1,0:T(8,128)(2,1)S(1)} async-done(((bf16[32,64,128]{2,1,0:T(8,128)(2,1)}), bf16[32,64,128]{2,1,0:T(8,128)(2,1)S(1)}, u32[]{:S(2)}, u32[]{:S(2)}) %all-to-all-start) | async-done | bytes 524320 | tf_op jit(solution)/shard_map/all_to_all | solution.py:220
  39.0 0.0 copy-done.2
  39.0 2.0 %shard_map.70 = (f32[512,128]{1,0:T(8,128)S(1)}, bf16[64,9216]{1,0:T(8,128)(2,1)S(1)}) custom-call(bf16[2048,128]{1,0:T(8,128)(2,1)S(1)} %bitcast.14, bf16[256,128]{1,0:T(8,128)(2,1)S(1)} %copy-done.2, bf16[256,128]{1,0:T(8,128)(2,1)S(1)} %collective-permute-done.below_ref, bf16[256,128]{1,0:T(8,128)(2,1)S(1)} %collective-permute-done.1.above_ref, ...), custom_call_target="tpu_custom_call" | custom-call | flops 452984832 | bytes 2949120 | tf_op jit(solution)/shard_map/pallas_call | solution.py:194
  41.0 0.0 copy-start.1
  41.0 13.7 %all_to_all.25 = f32[16,32,128]{2,1,0:T(8,128)S(1)} all-to-all(f32[16,32,128]{2,1,0:T(8,128)S(1)} %bitcast.15), channel_id=1, replica_groups=mesh['sample'=16,'sy'=4,'sz'=8] {'sample'}, dimensions={0} | all-to-all | bytes 524288 | tf_op jit(solution)/shard_map/all_to_all | solution.py:233
  54.7 12.4 %all_to_all.26 = f32[8,32,128]{2,1,0:T(8,128)S(1)} all-to-all(f32[8,32,128]{2,1,0:T(8,128)S(1)} %broadcast_in_dim.6), channel_id=1, replica_groups=mesh['sample'=16,'sy'=4,'sz'=8] {'sz'}, dimensions={0} | all-to-all | bytes 262144 | tf_op jit(solution)/shard_map/all_to_all | solution.py:235
  67.2 9.9 %all_to_all.27 = f32[4,32,128]{2,1,0:T(8,128)S(1)} all-to-all(f32[4,32,128]{2,1,0:T(8,128)S(1)} %broadcast_in_dim.7), channel_id=1, replica_groups=mesh['sample'=16,'sy'=4,'sz'=8] {'sy'}, dimensions={0} | all-to-all | bytes 131072 | tf_op jit(solution)/shard_map/all_to_all | solution.py:235
  77.1 0.7 broadcast_in_dim.8
  77.8 7.1 %all-to-all-start.4 = ((f32[16,32,128]{2,1,0:T(8,128)}), f32[16,32,128]{2,1,0:T(8,128)S(1)}, u32[]{:S(2)}, u32[]{:S(2)}) async-start(f32[16,32,128]{2,1,0:T(8,128)} %broadcast_in_dim.8), calls=%async_computation.4 | async-start | bytes 524288 | tf_op jit(solution)/shard_map/all_to_all | solution.py:236
  84.9 0.0 copy-done.1
  84.9 2.3 %shard_map.71 = bf16[1024,128]{1,0:T(8,128)(2,1)} custom-call(bf16[64,9216]{1,0:T(8,128)(2,1)S(1)} %get-tuple-element.8.g_ref, bf16[27,32,64]{2,1,0:T(8,128)(2,1)S(1)} %bitcast.17), custom_call_target="tpu_custom_call" | custom-call | flops 452984832 | bytes 1552384 | tf_op jit(solution)/shard_map/pallas_call | solution.py:194
  87.2 5.0 %all-to-all-done.4 = f32[16,32,128]{2,1,0:T(8,128)S(1)} async-done(((f32[16,32,128]{2,1,0:T(8,128)}), f32[16,32,128]{2,1,0:T(8,128)S(1)}, u32[]{:S(2)}, u32[]{:S(2)}) %all-to-all-start.4) | async-done | bytes 262176 | tf_op jit(solution)/shard_map/all_to_all | solution.py:236
  92.1 0.9 shard_map.72
  (5 shorter events, 0.1 us)
Async XLA Ops:
  0.6 26.5 %copy-start = (bf16[1,32,2,16,128]{4,3,2,1,0:T(8,128)(2,1)S(1)}, bf16[1,32,2,16,128]{4,3,2,1,0:T(8,128)(2,1)}, u32[]{:S(2)}) copy-start(bf16[1,32,2,16,128]{4,3,2,1,0:T(8,128)(2,1)} %param.5) | copy-start | bytes 786436
  3.2 35.8 %copy-start.2 = (bf16[256,128]{1,0:T(8,128)(2,1)S(1)}, bf16[256,128]{1,0:T(8,128)(2,1)}, u32[]{:S(2)}) copy-start(bf16[256,128]{1,0:T(8,128)(2,1)} %get-tuple-element.7.own_ref) | copy-start | bytes 196612
  3.2 35.8 %all-to-all-start = ((bf16[32,64,128]{2,1,0:T(8,128)(2,1)}), bf16[32,64,128]{2,1,0:T(8,128)(2,1)S(1)}, u32[]{:S(2)}, u32[]{:S(2)}) async-start(bf16[32,64,128]{2,1,0:T(8,128)(2,1)} %bitcast.18), calls=%async_computation | async-start | bytes 1048576 | tf_op jit(solution)/shard_map/all_to_all | solution.py:220
  19.9 17.3 %collective-permute-start.1 = (bf16[256,128]{1,0:T(8,128)(2,1)}, bf16[256,128]{1,0:T(8,128)(2,1)S(1)}, u32[]{:S(2)}, u32[]{:S(2)}) collective-permute-start(bf16[256,128]{1,0:T(8,128)(2,1)} %get-tuple-element.7.own_ref), channel_id=1, source_target_pairs={{8,0},{16,8},{24,16},{0,24},{9,1},{17,9},{25,17},{1,25},{10,2},{18... | collective-permute-start | bytes 196616 | tf_op jit(solution)/shard_map/ppermute | solution.py:219
  25.2 12.0 %collective-permute-start = (bf16[256,128]{1,0:T(8,128)(2,1)}, bf16[256,128]{1,0:T(8,128)(2,1)S(1)}, u32[]{:S(2)}, u32[]{:S(2)}) collective-permute-start(bf16[256,128]{1,0:T(8,128)(2,1)} %get-tuple-element.7.own_ref), channel_id=1, source_target_pairs={{0,8},{8,16},{16,24},{24,0},{1,9},{9,17},{17,25},{25,1},{2,10},{10... | collective-permute-start | bytes 196616 | tf_op jit(solution)/shard_map/ppermute | solution.py:218
  41.0 43.9 %copy-start.1 = (bf16[64,32,3,3,3]{0,1,4,3,2:T(8,128)(2,1)S(1)}, bf16[64,32,3,3,3]{0,1,4,3,2:T(8,128)(2,1)}, u32[]{:S(2)}) copy-start(bf16[64,32,3,3,3]{0,1,4,3,2:T(8,128)(2,1)} %param.6) | copy-start | bytes 331780
  77.8 14.3 %all-to-all-start.4 = ((f32[16,32,128]{2,1,0:T(8,128)}), f32[16,32,128]{2,1,0:T(8,128)S(1)}, u32[]{:S(2)}, u32[]{:S(2)}) async-start(f32[16,32,128]{2,1,0:T(8,128)} %broadcast_in_dim.8), calls=%async_computation.4 | async-start | bytes 524288 | tf_op jit(solution)/shard_map/all_to_all | solution.py:236

commit v4 on v3

--- a/solution.py
+++ b/solution.py
@@ -150,9 +150,9 @@
                 preferred_element_type=F32,
             )
     for j in range(4):
-        dw_ref[j * 96:(j + 1) * 96, :] = total[:, j * 128:(j + 1) * 128]
-    dw_ref[384:480, :] = jnp.concatenate([total[:, 512:], jnp.zeros((96, 64), F32)], axis=1)
-    dw_ref[480:, :] = jnp.zeros((32, 128), F32)
+        dw_ref[j * 96:(j + 1) * 96, :] = total[:, j * 128:(j + 1) * 128].astype(BF16)
+    dw_ref[384:480, :] = jnp.concatenate([total[:, 512:], jnp.zeros((96, 64), F32)], axis=1).astype(BF16)
+    dw_ref[480:, :] = jnp.zeros((32, 128), BF16)
 
 
 def input_kernel(g_ref, w_ref, out_ref, cells):
@@ -179,10 +179,19 @@
     out_ref[...] = jnp.dot(cells[...].astype(BF16), order, preferred_element_type=F32).astype(BF16)
 
 
+def sum_kernel(in_ref, out_ref):
+    total = in_ref[0].astype(F32)
+    for k in range(1, in_ref.shape[0]):
+        total += in_ref[k].astype(F32)
+    total = total.astype(BF16)
+    for k in range(out_ref.shape[0]):
+        out_ref[k] = total
+
+
 def final_kernel(scale, in_ref, out_ref):
     for ab in range(9):
         j, half = divmod(ab, 2)
-        part = in_ref[j * 96:(j + 1) * 96, half * 64:half * 64 + 64] * scale
+        part = in_ref[j * 96:(j + 1) * 96, half * 64:half * 64 + 64].astype(F32) * scale
         for c in range(3):
             out_ref[3 * ab + c] = part[c * 32:(c + 1) * 32]
 
@@ -223,17 +232,18 @@
         (activations.reshape(1024, 128),), flops=2 * 1024 * 128 * 384,
     )
     local, grad_out = call(
-        main_kernel, [shape((512, 128), F32), shape((COUT, 72 * 128), BF16)], [pltpu.VMEM((2048, 128), F32)],
+        main_kernel, [shape((512, 128), BF16), shape((COUT, 72 * 128), BF16)], [pltpu.VMEM((2048, 128), F32)],
         (recv, codes, below, above, taps), flops=2 * 96 * 576 * 4096,
     )
     input_grad = call(
         input_kernel, [shape((1024, 128), BF16)], [pltpu.VMEM((1024, 128), F32)],
         (grad_out, jnp.transpose(weight, (2, 3, 4, 1, 0)).reshape(27, CIN, COUT)), flops=2 * 96 * 576 * 4096,
     )
-    part = jnp.sum(lax.all_to_all(local.reshape(SAMPLE, 32, 128), "sample", 0, 0), 0)
-    for axis, size in (("sz", SZ), ("sy", SY)):
-        part = jnp.sum(lax.all_to_all(jnp.broadcast_to(part[None], (size, 32, 128)), axis, 0, 0), 0)
-    whole = lax.all_to_all(jnp.broadcast_to(part[None], (SAMPLE, 32, 128)), "sample", 0, 0).reshape(512, 128)
+    part = lax.all_to_all(local.reshape(SAMPLE, 32, 128), "sample", 0, 0)
+    part = call(sum_kernel, [shape((SY * SZ, 32, 128), BF16)], [], (part,))
+    part = lax.all_to_all(part, ("sy", "sz"), 0, 0)
+    part = call(sum_kernel, [shape((SAMPLE, 32, 128), BF16)], [], (part,))
+    whole = lax.all_to_all(part, "sample", 0, 0).reshape(512, 128)
     pooled = SAMPLE * SY * SZ * 8 * 64
     dw = call(
         functools.partial(final_kernel, float(1.0 / np.sqrt(np.float32(pooled)))),

time: 93.5 us -> 86.8 us (0.928)
  blocking collectives: 36 us -> 31.5 us
  starting transfers between devices: 30.9 us -> 29.8 us
  waiting for transfers between devices: 15.3 us -> 14.3 us
    all_to_all x3 -> x2, blocking collectives: 36 us -> 31.5 us  [the longest x1 18.8 us: body(): part = lax.all_to_all(part, ('sy', 'sz'), 0, 0)]
    all_to_all x1, starting transfers between devices: 7.06 us -> 5.95 us  [body(): whole = lax.all_to_all(part, 'sample', 0, 0).reshape(512, 128)]
    all_to_all x1, waiting for transfers between devices: 4.95 us -> 3.93 us  [body(): whole = lax.all_to_all(part, 'sample', 0, 0).reshape(512, 128)]
    pallas_call x5 -> x7, Pallas kernels: 9.24 us -> 10 us  [call(): pl.pallas_call(kernel, out_shape=tuple(outs) if len(outs) > 1 else outs[0...]
where the time goes in v4:
time: 86.8 us; the launch traced here: 86.3 us
  blocking collectives  31.5 us (36%)
  starting transfers between devices  29.8 us (34%)
  waiting for transfers between devices  14.3 us (16%)
  Pallas kernels  10 us (12%)
    all_to_all x1, blocking collectives, body(): part = lax.all_to_all(part, ('sy', 'sz'), 0, 0)  18.8 us
    all_to_all x1, starting transfers between devices, body(): lax.all_to_all(sent.reshape(32, 64, 128), ('sy', 'sz'), 0, 0)  16.7 us
    all_to_all x1, blocking collectives, body(): part = lax.all_to_all(local.reshape(SAMPLE, 32, 128), 'sample', 0, 0)  12.7 us
    pallas_call x7, Pallas kernels, call(): pl.pallas_call(kernel, out_shape=tuple(outs) if len(outs) > 1 else outs[0...  10 us
    ppermute x1, waiting for transfers between devices, body(): above = lax.ppermute(codes, 'sy', fall)  8.51 us
    all_to_all x1, starting transfers between devices, body(): whole = lax.all_to_all(part, 'sample', 0, 0).reshape(512, 128)  5.95 us
    ppermute x1, starting transfers between devices, body(): above = lax.ppermute(codes, 'sy', fall)  5.29 us
    all_to_all x1, waiting for transfers between devices, body(): whole = lax.all_to_all(part, 'sample', 0, 0).reshape(512, 128)  3.93 us
  transfers between devices with their start and end apart: 4, of which 3 were waited for; matrix products, arithmetic and copies ran while one was open for 0% of the time, Pallas kernels for 4%

profile of v4, /device:TPU:1, one launch (start us, length us, event | category | flops | bytes accessed | tf_op | source)
XLA Modules:
  0.0 86.3 jit_solution(14995289686377540681)
XLA Ops:
  0.6 0.0 copy-start
  0.6 2.6 %shard_map.68 = (bf16[2048,128]{1,0:T(8,128)(2,1)}, bf16[256,128]{1,0:T(8,128)(2,1)}) custom-call(bf16[1,2,4,4096]{3,2,1,0:T(4,128)(2,1)} %pg_any.1, s32[256,128]{1,0:T(8,128)} %bitcast.20, bf16[1024,272]{1,0:T(8,128)(2,1)} %constant.2.clone.sel_any), custom_call_target="tpu_custom_call" | custom-call | flops 71303168 | bytes 1343488 | tf_op jit(solution)/shard_map/pallas_call | solution.py:203
  3.2 0.0 copy-start.2
  3.2 16.7 %all-to-all-start = ((bf16[32,64,128]{2,1,0:T(8,128)(2,1)}), bf16[32,64,128]{2,1,0:T(8,128)(2,1)S(1)}, u32[]{:S(2)}, u32[]{:S(2)}) async-start(bf16[32,64,128]{2,1,0:T(8,128)(2,1)} %bitcast.18), calls=%async_computation | async-start | bytes 1048576 | tf_op jit(solution)/shard_map/all_to_all | solution.py:229
  19.9 5.3 %collective-permute-start.1 = (bf16[256,128]{1,0:T(8,128)(2,1)}, bf16[256,128]{1,0:T(8,128)(2,1)S(1)}, u32[]{:S(2)}, u32[]{:S(2)}) collective-permute-start(bf16[256,128]{1,0:T(8,128)(2,1)} %get-tuple-element.7.own_ref), channel_id=1, source_target_pairs={{8,0},{16,8},{24,16},{0,24},{9,1},{17,9},{25,17},{1,25},{10,2},{18... | collective-permute-start | bytes 196616 | tf_op jit(solution)/shard_map/ppermute | solution.py:228
  25.2 1.9 %collective-permute-start = (bf16[256,128]{1,0:T(8,128)(2,1)}, bf16[256,128]{1,0:T(8,128)(2,1)S(1)}, u32[]{:S(2)}, u32[]{:S(2)}) collective-permute-start(bf16[256,128]{1,0:T(8,128)(2,1)} %get-tuple-element.7.own_ref), channel_id=1, source_target_pairs={{0,8},{8,16},{16,24},{24,0},{1,9},{9,17},{17,25},{25,1},{2,10},{10... | collective-permute-start | bytes 196616 | tf_op jit(solution)/shard_map/ppermute | solution.py:227
  27.1 0.0 copy-done
  27.1 1.5 %shard_map.69.act_ref = bf16[96,4096]{1,0:T(8,128)(2,1)S(1)} custom-call(bf16[1024,128]{1,0:T(8,128)(2,1)S(1)} %bitcast.15), custom_call_target="tpu_custom_call" | custom-call | flops 100663296 | bytes 1048576 | tf_op jit(solution)/shard_map/pallas_call | solution.py:203
  28.7 8.5 %collective-permute-done.1.above_ref = bf16[256,128]{1,0:T(8,128)(2,1)S(1)} collective-permute-done((bf16[256,128]{1,0:T(8,128)(2,1)}, bf16[256,128]{1,0:T(8,128)(2,1)S(1)}, u32[]{:S(2)}, u32[]{:S(2)}) %collective-permute-start.1) | collective-permute-done | bytes 65568 | tf_op jit(solution)/shard_map/ppermute | solution.py:228
  37.2 0.0 collective-permute-done.below_ref
  37.2 1.8 %all-to-all-done = bf16[32,64,128]{2,1,0:T(8,128)(2,1)S(1)} async-done(((bf16[32,64,128]{2,1,0:T(8,128)(2,1)}), bf16[32,64,128]{2,1,0:T(8,128)(2,1)S(1)}, u32[]{:S(2)}, u32[]{:S(2)}) %all-to-all-start) | async-done | bytes 524320 | tf_op jit(solution)/shard_map/all_to_all | solution.py:229
  39.0 0.0 copy-done.2
  39.0 2.0 %shard_map.70 = (bf16[512,128]{1,0:T(8,128)(2,1)S(1)}, bf16[64,9216]{1,0:T(8,128)(2,1)S(1)}) custom-call(bf16[2048,128]{1,0:T(8,128)(2,1)S(1)} %bitcast.13, bf16[256,128]{1,0:T(8,128)(2,1)S(1)} %copy-done.2, bf16[256,128]{1,0:T(8,128)(2,1)S(1)} %collective-permute-done.below_ref, bf16[256,128]{1,0:T(8,128)(2,1)S(1)} %collective-permute-done.1.above_ref, ...), custom_call_target="tpu_custom_call" | custom-call | flops 452984832 | bytes 2818048 | tf_op jit(solution)/shard_map/pallas_call | solution.py:203
  41.0 0.0 copy-start.1
  41.0 12.7 %all_to_all.20.in_ref = bf16[16,32,128]{2,1,0:T(8,128)(2,1)S(1)} all-to-all(bf16[16,32,128]{2,1,0:T(8,128)(2,1)S(1)} %bitcast.16), channel_id=1, replica_groups=mesh['sample'=16,'sy'=4,'sz'=8] {'sample'}, dimensions={0} | all-to-all | bytes 262144 | tf_op jit(solution)/shard_map/all_to_all | solution.py:242
  53.7 18.8 %all_to_all.21.in_ref = bf16[32,32,128]{2,1,0:T(8,128)(2,1)S(1)} all-to-all(bf16[32,32,128]{2,1,0:T(8,128)(2,1)S(1)} %shard_map.72), channel_id=1, replica_groups=mesh['sample'=16,'sy'=4,'sz'=8] {'sy','sz'}, dimensions={0} | all-to-all | bytes 524288 | tf_op jit(solution)/shard_map/all_to_all | solution.py:244
  72.6 0.7 shard_map.73
  73.3 6.0 %all-to-all-start.3 = ((bf16[16,32,128]{2,1,0:T(8,128)(2,1)}), bf16[16,32,128]{2,1,0:T(8,128)(2,1)S(1)}, u32[]{:S(2)}, u32[]{:S(2)}) async-start(bf16[16,32,128]{2,1,0:T(8,128)(2,1)} %shard_map.73), calls=%async_computation.3 | async-start | bytes 262144 | tf_op jit(solution)/shard_map/all_to_all | solution.py:246
  79.2 0.0 copy-done.1
  79.2 2.3 %shard_map.71 = bf16[1024,128]{1,0:T(8,128)(2,1)} custom-call(bf16[64,9216]{1,0:T(8,128)(2,1)S(1)} %get-tuple-element.8.g_ref, bf16[27,32,64]{2,1,0:T(8,128)(2,1)S(1)} %bitcast.17), custom_call_target="tpu_custom_call" | custom-call | flops 452984832 | bytes 1552384 | tf_op jit(solution)/shard_map/pallas_call | solution.py:203
  81.5 3.9 %all-to-all-done.3 = bf16[16,32,128]{2,1,0:T(8,128)(2,1)S(1)} async-done(((bf16[16,32,128]{2,1,0:T(8,128)(2,1)}), bf16[16,32,128]{2,1,0:T(8,128)(2,1)S(1)}, u32[]{:S(2)}, u32[]{:S(2)}) %all-to-all-start.3) | async-done | bytes 131104 | tf_op jit(solution)/shard_map/all_to_all | solution.py:246
  85.4 0.9 %shard_map.74 = f32[27,32,64]{2,1,0:T(8,128)} custom-call(bf16[512,128]{1,0:T(8,128)(2,1)S(1)} %bitcast.14), custom_call_target="tpu_custom_call" | custom-call | bytes 352256 | tf_op jit(solution)/shard_map/pallas_call | solution.py:203
  (1 shorter events, 0.0 us)
Async XLA Ops:
  0.6 26.5 %copy-start = (bf16[1,32,2,16,128]{4,3,2,1,0:T(8,128)(2,1)S(1)}, bf16[1,32,2,16,128]{4,3,2,1,0:T(8,128)(2,1)}, u32[]{:S(2)}) copy-start(bf16[1,32,2,16,128]{4,3,2,1,0:T(8,128)(2,1)} %param.5) | copy-start | bytes 786436
  3.2 35.8 %copy-start.2 = (bf16[256,128]{1,0:T(8,128)(2,1)S(1)}, bf16[256,128]{1,0:T(8,128)(2,1)}, u32[]{:S(2)}) copy-start(bf16[256,128]{1,0:T(8,128)(2,1)} %get-tuple-element.7.own_ref) | copy-start | bytes 196612
  3.2 35.8 %all-to-all-start = ((bf16[32,64,128]{2,1,0:T(8,128)(2,1)}), bf16[32,64,128]{2,1,0:T(8,128)(2,1)S(1)}, u32[]{:S(2)}, u32[]{:S(2)}) async-start(bf16[32,64,128]{2,1,0:T(8,128)(2,1)} %bitcast.18), calls=%async_computation | async-start | bytes 1048576 | tf_op jit(solution)/shard_map/all_to_all | solution.py:229
  19.9 17.3 %collective-permute-start.1 = (bf16[256,128]{1,0:T(8,128)(2,1)}, bf16[256,128]{1,0:T(8,128)(2,1)S(1)}, u32[]{:S(2)}, u32[]{:S(2)}) collective-permute-start(bf16[256,128]{1,0:T(8,128)(2,1)} %get-tuple-element.7.own_ref), channel_id=1, source_target_pairs={{8,0},{16,8},{24,16},{0,24},{9,1},{17,9},{25,17},{1,25},{10,2},{18... | collective-permute-start | bytes 196616 | tf_op jit(solution)/shard_map/ppermute | solution.py:228
  25.2 12.0 %collective-permute-start = (bf16[256,128]{1,0:T(8,128)(2,1)}, bf16[256,128]{1,0:T(8,128)(2,1)S(1)}, u32[]{:S(2)}, u32[]{:S(2)}) collective-permute-start(bf16[256,128]{1,0:T(8,128)(2,1)} %get-tuple-element.7.own_ref), channel_id=1, source_target_pairs={{0,8},{8,16},{16,24},{24,0},{1,9},{9,17},{17,25},{25,1},{2,10},{10... | collective-permute-start | bytes 196616 | tf_op jit(solution)/shard_map/ppermute | solution.py:227
  41.0 38.2 %copy-start.1 = (bf16[64,32,3,3,3]{0,1,4,3,2:T(8,128)(2,1)S(1)}, bf16[64,32,3,3,3]{0,1,4,3,2:T(8,128)(2,1)}, u32[]{:S(2)}) copy-start(bf16[64,32,3,3,3]{0,1,4,3,2:T(8,128)(2,1)} %param.6) | copy-start | bytes 331780
  73.3 12.2 %all-to-all-start.3 = ((bf16[16,32,128]{2,1,0:T(8,128)(2,1)}), bf16[16,32,128]{2,1,0:T(8,128)(2,1)S(1)}, u32[]{:S(2)}, u32[]{:S(2)}) async-start(bf16[16,32,128]{2,1,0:T(8,128)(2,1)} %shard_map.73), calls=%async_computation.3 | async-start | bytes 262144 | tf_op jit(solution)/shard_map/all_to_all | solution.py:246

commit v5 on v4

--- a/solution.py
+++ b/solution.py
@@ -63,7 +63,7 @@
     first, last = codes[0], codes[3]
     leading = jnp.where(low, first[:32], roll64(first[32:]))
     ending = jnp.where(low, roll64(last[:32]), last[32:])
-    me = lax.axis_index("sz")
+    me = (lax.axis_index("zh") * 2 + lax.axis_index("zl"))
     for sz in range(SZ):
         edge = jnp.where(sz < me, leading, ending).astype(BF16)
         for sy in range(SY):
@@ -87,7 +87,7 @@
 
 
 def main_kernel(recv_ref, own_ref, below_ref, above_ref, act_ref, dw_ref, g_ref, rows):
-    my_sy, my_sz = lax.axis_index("sy"), lax.axis_index("sz")
+    my_sy, my_sz = lax.axis_index("sy"), (lax.axis_index("zh") * 2 + lax.axis_index("zl"))
     rows[...] = recv_ref[...].astype(F32)
     low = halves((64, 128))
     low32 = halves((32, 128))
@@ -226,7 +226,7 @@
     )
     below = lax.ppermute(codes, "sy", rise)
     above = lax.ppermute(codes, "sy", fall)
-    recv = lax.all_to_all(sent.reshape(32, 64, 128), ("sy", "sz"), 0, 0).reshape(2048, 128)
+    recv = lax.all_to_all(sent.reshape(32, 64, 128), ("sy", "zh", "zl"), 0, 0).reshape(2048, 128)
     taps = call(
         taps_kernel, [shape((96, 4096), BF16)], [pltpu.VMEM((1024, 128), F32)],
         (activations.reshape(1024, 128),), flops=2 * 1024 * 128 * 384,
@@ -239,11 +239,12 @@
         input_kernel, [shape((1024, 128), BF16)], [pltpu.VMEM((1024, 128), F32)],
         (grad_out, jnp.transpose(weight, (2, 3, 4, 1, 0)).reshape(27, CIN, COUT)), flops=2 * 96 * 576 * 4096,
     )
-    part = lax.all_to_all(local.reshape(SAMPLE, 32, 128), "sample", 0, 0)
-    part = call(sum_kernel, [shape((SY * SZ, 32, 128), BF16)], [], (part,))
-    part = lax.all_to_all(part, ("sy", "sz"), 0, 0)
-    part = call(sum_kernel, [shape((SAMPLE, 32, 128), BF16)], [], (part,))
-    whole = lax.all_to_all(part, "sample", 0, 0).reshape(512, 128)
+    near, far = ("sample", "zl"), ("sy", "zh")
+    part = lax.all_to_all(local.reshape(2 * SAMPLE, 16, 128), near, 0, 0)
+    part = call(sum_kernel, [shape((SY * SZ // 2, 16, 128), BF16)], [], (part,))
+    part = lax.all_to_all(part, far, 0, 0)
+    part = call(sum_kernel, [shape((2 * SAMPLE, 16, 128), BF16)], [], (part,))
+    whole = lax.all_to_all(part, near, 0, 0).reshape(512, 128)
     pooled = SAMPLE * SY * SZ * 8 * 64
     dw = call(
         functools.partial(final_kernel, float(1.0 / np.sqrt(np.float32(pooled)))),
@@ -254,15 +255,17 @@
 
 
 def solution(mesh):
+    mesh = jax.sharding.Mesh(mesh.devices.reshape(SAMPLE, SY, SZ // 2, 2), ("sample", "sy", "zh", "zl"))
+    volume = P("sample", None, "sy", ("zh", "zl"), None)
     return jax.shard_map(
         body,
         mesh=mesh,
         in_specs=(
-            P("sample", None, "sy", "sz", None),
+            volume,
             P(),
-            P("sample", ("sy", "sz"), None, None),
-            P("sample", None, "sy", "sz"),
+            P("sample", ("sy", "zh", "zl"), None, None),
+            P("sample", None, "sy", ("zh", "zl")),
         ),
-        out_specs=(P("sample", None, "sy", "sz", None), P()),
+        out_specs=(volume, P()),
         check_vma=False,
     )

time: 86.8 us -> 86.7 us (level)
  waiting for transfers between devices: 14.3 us -> 15.2 us
    all_to_all x2, waiting for transfers between devices: 5.74 us -> 6.71 us  [the longest x1 4.9 us: body(): whole = lax.all_to_all(part, near, 0, 0).reshape(512, 128)]
where the time goes in v5:
time: 86.7 us; the launch traced here: 86.3 us
  blocking collectives  30.9 us (36%)
  starting transfers between devices  29.4 us (34%)
  waiting for transfers between devices  15.2 us (18%)
  Pallas kernels  9.99 us (12%)
    all_to_all x1, starting transfers between devices, body(): lax.all_to_all(sent.reshape(32, 64, 128), ('sy', 'zh', 'zl'), 0, 0)  16.7 us
    all_to_all x1, blocking collectives, body(): part = lax.all_to_all(local.reshape(2 * SAMPLE, 16, 128), near, 0, 0)  15.6 us
    all_to_all x1, blocking collectives, body(): part = lax.all_to_all(part, far, 0, 0)  15.4 us
    pallas_call x7, Pallas kernels, call(): pl.pallas_call(kernel, out_shape=tuple(outs) if len(outs) > 1 else outs[0...  9.99 us
    ppermute x1, waiting for transfers between devices, body(): above = lax.ppermute(codes, 'sy', fall)  8.51 us
    all_to_all x1, starting transfers between devices, body(): whole = lax.all_to_all(part, near, 0, 0).reshape(512, 128)  5.49 us
    ppermute x1, starting transfers between devices, body(): above = lax.ppermute(codes, 'sy', fall)  5.29 us
    all_to_all x1, waiting for transfers between devices, body(): whole = lax.all_to_all(part, near, 0, 0).reshape(512, 128)  4.9 us
  transfers between devices with their start and end apart: 4, of which 3 were waited for; matrix products, arithmetic and copies ran while one was open for 0% of the time, Pallas kernels for 4%

profile of v5, /device:TPU:1, one launch (start us, length us, event | category | flops | bytes accessed | tf_op | source)
XLA Modules:
  0.0 86.3 jit_solution(17770852893006523188)
XLA Ops:
  0.6 0.0 copy-start
  0.6 2.6 %shard_map.68 = (bf16[2048,128]{1,0:T(8,128)(2,1)}, bf16[256,128]{1,0:T(8,128)(2,1)}) custom-call(bf16[1,2,4,4096]{3,2,1,0:T(4,128)(2,1)} %pg_any.1, s32[256,128]{1,0:T(8,128)} %bitcast.20, bf16[1024,272]{1,0:T(8,128)(2,1)} %constant.2.clone.sel_any), custom_call_target="tpu_custom_call" | custom-call | flops 71303168 | bytes 1343488 | tf_op jit(solution)/shard_map/pallas_call | solution.py:203
  3.2 0.0 copy-start.2
  3.2 16.7 %all-to-all-start = ((bf16[32,64,128]{2,1,0:T(8,128)(2,1)}), bf16[32,64,128]{2,1,0:T(8,128)(2,1)S(1)}, u32[]{:S(2)}, u32[]{:S(2)}) async-start(bf16[32,64,128]{2,1,0:T(8,128)(2,1)} %bitcast.18), calls=%async_computation | async-start | bytes 1048576 | tf_op jit(solution)/shard_map/all_to_all | solution.py:229
  19.9 5.3 %collective-permute-start.1 = (bf16[256,128]{1,0:T(8,128)(2,1)}, bf16[256,128]{1,0:T(8,128)(2,1)S(1)}, u32[]{:S(2)}, u32[]{:S(2)}) collective-permute-start(bf16[256,128]{1,0:T(8,128)(2,1)} %get-tuple-element.7.own_ref), channel_id=1, source_target_pairs={{8,0},{16,8},{24,16},{0,24},{9,1},{17,9},{25,17},{1,25},{10,2},{18... | collective-permute-start | bytes 196616 | tf_op jit(solution)/shard_map/ppermute | solution.py:228
  25.2 1.9 %collective-permute-start = (bf16[256,128]{1,0:T(8,128)(2,1)}, bf16[256,128]{1,0:T(8,128)(2,1)S(1)}, u32[]{:S(2)}, u32[]{:S(2)}) collective-permute-start(bf16[256,128]{1,0:T(8,128)(2,1)} %get-tuple-element.7.own_ref), channel_id=1, source_target_pairs={{0,8},{8,16},{16,24},{24,0},{1,9},{9,17},{17,25},{25,1},{2,10},{10... | collective-permute-start | bytes 196616 | tf_op jit(solution)/shard_map/ppermute | solution.py:227
  27.1 0.0 copy-done
  27.1 1.5 %shard_map.69.act_ref = bf16[96,4096]{1,0:T(8,128)(2,1)S(1)} custom-call(bf16[1024,128]{1,0:T(8,128)(2,1)S(1)} %bitcast.15), custom_call_target="tpu_custom_call" | custom-call | flops 100663296 | bytes 1048576 | tf_op jit(solution)/shard_map/pallas_call | solution.py:203
  28.7 8.5 %collective-permute-done.1.above_ref = bf16[256,128]{1,0:T(8,128)(2,1)S(1)} collective-permute-done((bf16[256,128]{1,0:T(8,128)(2,1)}, bf16[256,128]{1,0:T(8,128)(2,1)S(1)}, u32[]{:S(2)}, u32[]{:S(2)}) %collective-permute-start.1) | collective-permute-done | bytes 65568 | tf_op jit(solution)/shard_map/ppermute | solution.py:228
  37.2 0.0 collective-permute-done.below_ref
  37.2 1.8 %all-to-all-done = bf16[32,64,128]{2,1,0:T(8,128)(2,1)S(1)} async-done(((bf16[32,64,128]{2,1,0:T(8,128)(2,1)}), bf16[32,64,128]{2,1,0:T(8,128)(2,1)S(1)}, u32[]{:S(2)}, u32[]{:S(2)}) %all-to-all-start) | async-done | bytes 524320 | tf_op jit(solution)/shard_map/all_to_all | solution.py:229
  39.0 0.0 copy-done.2
  39.0 0.0 copy-start.1
  39.0 2.0 %shard_map.70 = (bf16[512,128]{1,0:T(8,128)(2,1)S(1)}, bf16[64,9216]{1,0:T(8,128)(2,1)S(1)}) custom-call(bf16[2048,128]{1,0:T(8,128)(2,1)S(1)} %bitcast.13, bf16[256,128]{1,0:T(8,128)(2,1)S(1)} %copy-done.2, bf16[256,128]{1,0:T(8,128)(2,1)S(1)} %collective-permute-done.below_ref, bf16[256,128]{1,0:T(8,128)(2,1)S(1)} %collective-permute-done.1.above_ref, ...), custom_call_target="tpu_custom_call" | custom-call | flops 452984832 | bytes 2818048 | tf_op jit(solution)/shard_map/pallas_call | solution.py:203
  41.0 15.6 %all_to_all.20.in_ref = bf16[32,16,128]{2,1,0:T(8,128)(2,1)S(1)} all-to-all(bf16[32,16,128]{2,1,0:T(8,128)(2,1)S(1)} %bitcast.16), channel_id=1, replica_groups=mesh['sample'=16,'sy'=4,'zh'=4,'zl'=2] {'sample','zl'}, dimensions={0} | all-to-all | bytes 262144 | tf_op jit(solution)/shard_map/all_to_all | solution.py:243
  56.6 15.4 %all_to_all.21.in_ref = bf16[16,16,128]{2,1,0:T(8,128)(2,1)S(1)} all-to-all(bf16[16,16,128]{2,1,0:T(8,128)(2,1)S(1)} %shard_map.72), channel_id=1, replica_groups=mesh['sample'=16,'sy'=4,'zh'=4,'zl'=2] {'sy','zh'}, dimensions={0} | all-to-all | bytes 131072 | tf_op jit(solution)/shard_map/all_to_all | solution.py:245
  72.0 0.7 shard_map.73
  72.7 5.5 %all-to-all-start.3 = ((bf16[32,16,128]{2,1,0:T(8,128)(2,1)}), bf16[32,16,128]{2,1,0:T(8,128)(2,1)S(1)}, u32[]{:S(2)}, u32[]{:S(2)}) async-start(bf16[32,16,128]{2,1,0:T(8,128)(2,1)} %shard_map.73), calls=%async_computation.3 | async-start | bytes 262144 | tf_op jit(solution)/shard_map/all_to_all | solution.py:247
  78.2 0.0 copy-done.1
  78.2 2.3 %shard_map.71 = bf16[1024,128]{1,0:T(8,128)(2,1)} custom-call(bf16[64,9216]{1,0:T(8,128)(2,1)S(1)} %get-tuple-element.8.g_ref, bf16[27,32,64]{2,1,0:T(8,128)(2,1)S(1)} %bitcast.17), custom_call_target="tpu_custom_call" | custom-call | flops 452984832 | bytes 1552384 | tf_op jit(solution)/shard_map/pallas_call | solution.py:203
  80.5 4.9 %all-to-all-done.3 = bf16[32,16,128]{2,1,0:T(8,128)(2,1)S(1)} async-done(((bf16[32,16,128]{2,1,0:T(8,128)(2,1)}), bf16[32,16,128]{2,1,0:T(8,128)(2,1)S(1)}, u32[]{:S(2)}, u32[]{:S(2)}) %all-to-all-start.3) | async-done | bytes 131104 | tf_op jit(solution)/shard_map/all_to_all | solution.py:247
  85.4 0.9 %shard_map.74 = f32[27,32,64]{2,1,0:T(8,128)} custom-call(bf16[512,128]{1,0:T(8,128)(2,1)S(1)} %bitcast.14), custom_call_target="tpu_custom_call" | custom-call | bytes 352256 | tf_op jit(solution)/shard_map/pallas_call | solution.py:203
  (1 shorter events, 0.0 us)
Async XLA Ops:
  0.6 26.5 %copy-start = (bf16[1,32,2,16,128]{4,3,2,1,0:T(8,128)(2,1)S(1)}, bf16[1,32,2,16,128]{4,3,2,1,0:T(8,128)(2,1)}, u32[]{:S(2)}) copy-start(bf16[1,32,2,16,128]{4,3,2,1,0:T(8,128)(2,1)} %param.5) | copy-start | bytes 786436
  3.2 35.8 %copy-start.2 = (bf16[256,128]{1,0:T(8,128)(2,1)S(1)}, bf16[256,128]{1,0:T(8,128)(2,1)}, u32[]{:S(2)}) copy-start(bf16[256,128]{1,0:T(8,128)(2,1)} %get-tuple-element.7.own_ref) | copy-start | bytes 196612
  3.2 35.8 %all-to-all-start = ((bf16[32,64,128]{2,1,0:T(8,128)(2,1)}), bf16[32,64,128]{2,1,0:T(8,128)(2,1)S(1)}, u32[]{:S(2)}, u32[]{:S(2)}) async-start(bf16[32,64,128]{2,1,0:T(8,128)(2,1)} %bitcast.18), calls=%async_computation | async-start | bytes 1048576 | tf_op jit(solution)/shard_map/all_to_all | solution.py:229
  19.9 17.3 %collective-permute-start.1 = (bf16[256,128]{1,0:T(8,128)(2,1)}, bf16[256,128]{1,0:T(8,128)(2,1)S(1)}, u32[]{:S(2)}, u32[]{:S(2)}) collective-permute-start(bf16[256,128]{1,0:T(8,128)(2,1)} %get-tuple-element.7.own_ref), channel_id=1, source_target_pairs={{8,0},{16,8},{24,16},{0,24},{9,1},{17,9},{25,17},{1,25},{10,2},{18... | collective-permute-start | bytes 196616 | tf_op jit(solution)/shard_map/ppermute | solution.py:228
  25.2 12.0 %collective-permute-start = (bf16[256,128]{1,0:T(8,128)(2,1)}, bf16[256,128]{1,0:T(8,128)(2,1)S(1)}, u32[]{:S(2)}, u32[]{:S(2)}) collective-permute-start(bf16[256,128]{1,0:T(8,128)(2,1)} %get-tuple-element.7.own_ref), channel_id=1, source_target_pairs={{0,8},{8,16},{16,24},{24,0},{1,9},{9,17},{17,25},{25,1},{2,10},{10... | collective-permute-start | bytes 196616 | tf_op jit(solution)/shard_map/ppermute | solution.py:227
  39.0 39.2 %copy-start.1 = (bf16[64,32,3,3,3]{0,1,4,3,2:T(8,128)(2,1)S(1)}, bf16[64,32,3,3,3]{0,1,4,3,2:T(8,128)(2,1)}, u32[]{:S(2)}) copy-start(bf16[64,32,3,3,3]{0,1,4,3,2:T(8,128)(2,1)} %param.6) | copy-start | bytes 331780
  72.7 12.7 %all-to-all-start.3 = ((bf16[32,16,128]{2,1,0:T(8,128)(2,1)}), bf16[32,16,128]{2,1,0:T(8,128)(2,1)S(1)}, u32[]{:S(2)}, u32[]{:S(2)}) async-start(bf16[32,16,128]{2,1,0:T(8,128)(2,1)} %shard_map.73), calls=%async_computation.3 | async-start | bytes 262144 | tf_op jit(solution)/shard_map/all_to_all | solution.py:247

commit v6 on v5

--- a/solution.py
+++ b/solution.py
@@ -11,21 +11,18 @@
 SY, SZ, SAMPLE = 4, 8, 16
 CIN, COUT = 32, 64
 ROWS = 16
+LEVEL = 80
 F32, BF16 = jnp.float32, jnp.bfloat16
 LIMIT = 24 * 1024 * 1024
 
 
 def selection():
-    sel = np.zeros((SY * SZ * 2 * ROWS, 272), np.float32)
-    for sy in range(SY):
-        for sz in range(SZ):
-            for ch in range(2):
-                for dy in range(3):
-                    py = sy + dy - 1
-                    if 0 <= py < SY:
-                        for j in range(5):
-                            row = ((sy * SZ + sz) * 2 + ch) * ROWS + dy * 5 + j
-                            sel[row, (ch * 4 + py) * 33 + 4 * sz + j] = 1
+    sel = np.zeros((SZ * 2 * ROWS, 3 * LEVEL), np.float32)
+    for sz in range(SZ):
+        for ch in range(2):
+            for dy in range(3):
+                for j in range(5):
+                    sel[(sz * 2 + ch) * ROWS + dy * 5 + j, dy * LEVEL + ch * 33 + 4 * sz + j] = 1
     return sel
 
 
@@ -37,24 +34,14 @@
     return pltpu.roll(value, 64, 1)
 
 
-def pack_kernel(pg_any, am_any, sel_any, out_ref, codes_ref, tiles, pg_ref, am_ref, sel_ref, sems):
+def pack_kernel(pg_any, am_any, sel_any, out_any, codes_ref, tiles, pg_ref, am_ref, sel_ref, out_ref, sems):
     copies = [
         pltpu.make_async_copy(src, dst, sems.at[k])
         for k, (src, dst) in enumerate(((pg_any, pg_ref), (am_any, am_ref), (sel_any, sel_ref)))
     ]
     for copy in copies:
         copy.start()
-    copies[0].wait()
-    low = halves((8, 128))
-    pooled = jnp.concatenate([pg_ref[0, 0].astype(F32), pg_ref[0, 1].astype(F32)], axis=0)
     tiles[...] = jnp.zeros_like(tiles)
-    before = jnp.zeros((8, 128), F32)
-    for k in range(33):
-        tile = pooled[:, k * 128:(k + 1) * 128] if k < 32 else jnp.zeros((8, 128), F32)
-        tiles[pl.ds(k, 8, stride=33), :] = roll64(jnp.where(low, tile, before))
-        before = tile
-    copies[2].wait()
-    sent = jnp.dot(sel_ref[...], tiles[...].astype(BF16), preferred_element_type=F32).astype(BF16)
     copies[1].wait()
     low = halves((32, 128))
     codes = [am_ref[pl.ds(t, 64, stride=4), :].astype(F32) for t in range(4)]
@@ -63,14 +50,34 @@
     first, last = codes[0], codes[3]
     leading = jnp.where(low, first[:32], roll64(first[32:]))
     ending = jnp.where(low, roll64(last[:32]), last[32:])
-    me = (lax.axis_index("zh") * 2 + lax.axis_index("zl"))
-    for sz in range(SZ):
-        edge = jnp.where(sz < me, leading, ending).astype(BF16)
-        for sy in range(SY):
-            for ch in range(2):
-                block = (sy * SZ + sz) * 2 + ch
-                out_ref[pl.ds(block * 32, 16), :] = sent[block * 16:(block + 1) * 16]
-                out_ref[pl.ds(block * 32 + 16, 16), :] = edge[ch * 16:(ch + 1) * 16]
+    me = lax.axis_index("zh") * 2 + lax.axis_index("zl")
+    edges = [jnp.where(sz < me, leading, ending).astype(BF16) for sz in range(SZ)]
+    copies[0].wait()
+    low = halves((8, 128))
+    pooled = jnp.concatenate([pg_ref[0, 0].astype(F32), pg_ref[0, 1].astype(F32)], axis=0)
+    before = jnp.zeros((8, 128), F32)
+    for k in range(33):
+        tile = pooled[:, k * 128:(k + 1) * 128] if k < 32 else jnp.zeros((8, 128), F32)
+        shifted = roll64(jnp.where(low, tile, before))
+        for ch in range(2):
+            tiles[pl.ds(LEVEL + ch * 33 + k, SY, stride=LEVEL), :] = shifted[ch * SY:(ch + 1) * SY]
+        before = tile
+    copies[2].wait()
+    sel = sel_ref[...]
+    levels = tiles[...].astype(BF16)
+    leaving = []
+    for sy in range(SY):
+        near = levels[sy * LEVEL:(sy + 3) * LEVEL]
+        sent = jnp.dot(sel, near, preferred_element_type=F32).astype(BF16)
+        for block in range(2 * SZ):
+            row = sy * 512 + block * 32
+            out_ref[row:row + 16] = sent[block * 16:(block + 1) * 16]
+            out_ref[row + 16:row + 32] = edges[block // 2][block % 2 * 16:block % 2 * 16 + 16]
+        part = pl.ds(sy * 512, 512)
+        leaving.append(pltpu.make_async_copy(out_ref.at[part], out_any.at[part], sems.at[3 + sy]))
+        leaving[-1].start()
+    for copy in leaving:
+        copy.wait()
 
 
 def taps_kernel(act_ref, out_ref, wide):
@@ -88,7 +95,8 @@
 
 def main_kernel(recv_ref, own_ref, below_ref, above_ref, act_ref, dw_ref, g_ref, rows):
     my_sy, my_sz = lax.axis_index("sy"), (lax.axis_index("zh") * 2 + lax.axis_index("zl"))
-    rows[...] = recv_ref[...].astype(F32)
+    for o in range(COUT):
+        rows[o * ROWS:(o + 1) * ROWS] = recv_ref[o * 32:o * 32 + ROWS].astype(F32)
     low = halves((64, 128))
     low32 = halves((32, 128))
     parity = jnp.where(low, 0.0, 1.0)
@@ -100,7 +108,7 @@
     def halo(sy, sz):
         base = (jnp.clip(sy, 0, SY - 1) * SZ + jnp.clip(sz, 0, SZ - 1)) * 64
         packed = jnp.concatenate(
-            [rows[pl.ds(pl.multiple_of(base + 16, 16), 16), :], rows[pl.ds(pl.multiple_of(base + 48, 16), 16), :]], axis=0
+            [recv_ref[pl.ds(pl.multiple_of(base + k, 16), 16), :].astype(F32) for k in (16, 48)], axis=0
         )
         other = roll64(packed)
         return jnp.concatenate(
@@ -114,7 +122,7 @@
         values = None
         for pz in range(10):
             if pz % 2 == 0:
-                values = rows[pl.ds(dy * 5 + pz // 2, 64, stride=32), :]
+                values = rows[pl.ds(dy * 5 + pz // 2, COUT, stride=ROWS), :]
             value = spread(values, pz % 2 == 0)
             if pz == 0:
                 code = before
@@ -204,7 +212,7 @@
         kernel,
         out_shape=tuple(outs) if len(outs) > 1 else outs[0],
         in_specs=specs,
-        out_specs=tuple([vmem] * len(outs)) if len(outs) > 1 else vmem,
+        out_specs=tuple([specs[0]] + [vmem] * (len(outs) - 1)) if len(outs) > 1 else vmem,
         scratch_shapes=scratch,
         compiler_params=pltpu.CompilerParams(vmem_limit_bytes=60 * 1024 * 1024 if hbm else LIMIT),
         cost_estimate=pl.CostEstimate(flops=flops, bytes_accessed=nbytes, transcendentals=0),
@@ -219,10 +227,11 @@
     sent, codes = call(
         pack_kernel, [shape((2048, 128), BF16), shape((256, 128), BF16)],
         [
-            pltpu.VMEM((272, 128), F32), pltpu.VMEM((1, 2, SY, 4096), BF16), pltpu.VMEM((256, 128), jnp.int32),
-            pltpu.VMEM((1024, 272), BF16), pltpu.SemaphoreType.DMA((3,)),
+            pltpu.VMEM(((SY + 2) * LEVEL, 128), F32), pltpu.VMEM((1, 2, SY, 4096), BF16),
+            pltpu.VMEM((256, 128), jnp.int32), pltpu.VMEM((SZ * 2 * ROWS, 3 * LEVEL), BF16),
+            pltpu.VMEM((2048, 128), BF16), pltpu.SemaphoreType.DMA((3 + SY,)),
         ],
-        (pooled_grad, window_argmax.reshape(256, 128), sel), flops=2 * 1024 * 272 * 128, hbm=True,
+        (pooled_grad, window_argmax.reshape(256, 128), sel), flops=2 * 1024 * 240 * 128, hbm=True,
     )
     below = lax.ppermute(codes, "sy", rise)
     above = lax.ppermute(codes, "sy", fall)
@@ -232,7 +241,7 @@
         (activations.reshape(1024, 128),), flops=2 * 1024 * 128 * 384,
     )
     local, grad_out = call(
-        main_kernel, [shape((512, 128), BF16), shape((COUT, 72 * 128), BF16)], [pltpu.VMEM((2048, 128), F32)],
+        main_kernel, [shape((512, 128), BF16), shape((COUT, 72 * 128), BF16)], [pltpu.VMEM((COUT * ROWS, 128), F32)],
         (recv, codes, below, above, taps), flops=2 * 96 * 576 * 4096,
     )
     input_grad = call(

time: 86.7 us -> 86.8 us (level)
  no operation moved by 1% of the time
where the time goes in v6:
time: 86.8 us; the launch traced here: 86.4 us
  blocking collectives  30.9 us (36%)
  starting transfers between devices  29.4 us (34%)
  waiting for transfers between devices  15.2 us (18%)
  Pallas kernels  10.1 us (12%)
    all_to_all x1, starting transfers between devices, body(): lax.all_to_all(sent.reshape(32, 64, 128), ('sy', 'zh', 'zl'), 0, 0)  16.7 us
    all_to_all x1, blocking collectives, body(): part = lax.all_to_all(local.reshape(2 * SAMPLE, 16, 128), near, 0, 0)  15.5 us
    all_to_all x1, blocking collectives, body(): part = lax.all_to_all(part, far, 0, 0)  15.5 us
    pallas_call x7, Pallas kernels, call(): pl.pallas_call(kernel, out_shape=tuple(outs) if len(outs) > 1 else outs[0...  10.1 us
    ppermute x1, waiting for transfers between devices, body(): above = lax.ppermute(codes, 'sy', fall)  8.51 us
    all_to_all x1, starting transfers between devices, body(): whole = lax.all_to_all(part, near, 0, 0).reshape(512, 128)  5.49 us
    ppermute x1, starting transfers between devices, body(): above = lax.ppermute(codes, 'sy', fall)  5.29 us
    all_to_all x1, waiting for transfers between devices, body(): whole = lax.all_to_all(part, near, 0, 0).reshape(512, 128)  4.89 us
  transfers between devices with their start and end apart: 4, of which 3 were waited for; matrix products, arithmetic and copies ran while one was open for 0% of the time, Pallas kernels for 4%

profile of v6, /device:TPU:1, one launch (start us, length us, event | category | flops | bytes accessed | tf_op | source)
XLA Modules:
  0.0 86.4 jit_solution(63030543177350103)
XLA Ops:
  0.6 0.0 copy-start
  0.6 2.9 %shard_map.68 = (bf16[2048,128]{1,0:T(8,128)(2,1)}, bf16[256,128]{1,0:T(8,128)(2,1)}) custom-call(bf16[1,2,4,4096]{3,2,1,0:T(4,128)(2,1)} %pg_any.1, s32[256,128]{1,0:T(8,128)} %bitcast.20, bf16[256,240]{1,0:T(8,128)(2,1)} %constant.2.clone.sel_any), custom_call_target="tpu_custom_call" | custom-call | flops 62914560 | bytes 909312 | tf_op jit(solution)/shard_map/pallas_call | solution.py:211
  3.5 0.0 copy-start.2
  3.5 16.7 %all-to-all-start = ((bf16[32,64,128]{2,1,0:T(8,128)(2,1)}), bf16[32,64,128]{2,1,0:T(8,128)(2,1)S(1)}, u32[]{:S(2)}, u32[]{:S(2)}) async-start(bf16[32,64,128]{2,1,0:T(8,128)(2,1)} %bitcast.18), calls=%async_computation | async-start | bytes 1048576 | tf_op jit(solution)/shard_map/all_to_all | solution.py:238
  20.2 5.3 %collective-permute-start.1 = (bf16[256,128]{1,0:T(8,128)(2,1)}, bf16[256,128]{1,0:T(8,128)(2,1)S(1)}, u32[]{:S(2)}, u32[]{:S(2)}) collective-permute-start(bf16[256,128]{1,0:T(8,128)(2,1)} %get-tuple-element.7.own_ref), channel_id=1, source_target_pairs={{8,0},{16,8},{24,16},{0,24},{9,1},{17,9},{25,17},{1,25},{10,2},{18... | collective-permute-start | bytes 196616 | tf_op jit(solution)/shard_map/ppermute | solution.py:237
  25.5 1.9 %collective-permute-start = (bf16[256,128]{1,0:T(8,128)(2,1)}, bf16[256,128]{1,0:T(8,128)(2,1)S(1)}, u32[]{:S(2)}, u32[]{:S(2)}) collective-permute-start(bf16[256,128]{1,0:T(8,128)(2,1)} %get-tuple-element.7.own_ref), channel_id=1, source_target_pairs={{0,8},{8,16},{16,24},{24,0},{1,9},{9,17},{17,25},{25,1},{2,10},{10... | collective-permute-start | bytes 196616 | tf_op jit(solution)/shard_map/ppermute | solution.py:236
  27.4 0.0 copy-done
  27.5 1.5 %shard_map.69.act_ref = bf16[96,4096]{1,0:T(8,128)(2,1)S(1)} custom-call(bf16[1024,128]{1,0:T(8,128)(2,1)S(1)} %bitcast.15), custom_call_target="tpu_custom_call" | custom-call | flops 100663296 | bytes 1048576 | tf_op jit(solution)/shard_map/pallas_call | solution.py:211
  29.0 8.5 %collective-permute-done.1.above_ref = bf16[256,128]{1,0:T(8,128)(2,1)S(1)} collective-permute-done((bf16[256,128]{1,0:T(8,128)(2,1)}, bf16[256,128]{1,0:T(8,128)(2,1)S(1)}, u32[]{:S(2)}, u32[]{:S(2)}) %collective-permute-start.1) | collective-permute-done | bytes 65568 | tf_op jit(solution)/shard_map/ppermute | solution.py:237
  37.5 0.0 collective-permute-done.below_ref
  37.5 1.8 %all-to-all-done = bf16[32,64,128]{2,1,0:T(8,128)(2,1)S(1)} async-done(((bf16[32,64,128]{2,1,0:T(8,128)(2,1)}), bf16[32,64,128]{2,1,0:T(8,128)(2,1)S(1)}, u32[]{:S(2)}, u32[]{:S(2)}) %all-to-all-start) | async-done | bytes 524320 | tf_op jit(solution)/shard_map/all_to_all | solution.py:238
  39.3 0.0 copy-done.2
  39.3 0.0 copy-start.1
  39.3 1.8 %shard_map.70 = (bf16[512,128]{1,0:T(8,128)(2,1)S(1)}, bf16[64,9216]{1,0:T(8,128)(2,1)S(1)}) custom-call(bf16[2048,128]{1,0:T(8,128)(2,1)S(1)} %bitcast.13, bf16[256,128]{1,0:T(8,128)(2,1)S(1)} %copy-done.2, bf16[256,128]{1,0:T(8,128)(2,1)S(1)} %collective-permute-done.below_ref, bf16[256,128]{1,0:T(8,128)(2,1)S(1)} %collective-permute-done.1.above_ref, ...), custom_call_target="tpu_custom_call" | custom-call | flops 452984832 | bytes 2818048 | tf_op jit(solution)/shard_map/pallas_call | solution.py:211
  41.1 15.5 %all_to_all.20.in_ref = bf16[32,16,128]{2,1,0:T(8,128)(2,1)S(1)} all-to-all(bf16[32,16,128]{2,1,0:T(8,128)(2,1)S(1)} %bitcast.16), channel_id=1, replica_groups=mesh['sample'=16,'sy'=4,'zh'=4,'zl'=2] {'sample','zl'}, dimensions={0} | all-to-all | bytes 262144 | tf_op jit(solution)/shard_map/all_to_all | solution.py:252
  56.7 15.5 %all_to_all.21.in_ref = bf16[16,16,128]{2,1,0:T(8,128)(2,1)S(1)} all-to-all(bf16[16,16,128]{2,1,0:T(8,128)(2,1)S(1)} %shard_map.72), channel_id=1, replica_groups=mesh['sample'=16,'sy'=4,'zh'=4,'zl'=2] {'sy','zh'}, dimensions={0} | all-to-all | bytes 131072 | tf_op jit(solution)/shard_map/all_to_all | solution.py:254
  72.1 0.7 shard_map.73
  72.8 5.5 %all-to-all-start.3 = ((bf16[32,16,128]{2,1,0:T(8,128)(2,1)}), bf16[32,16,128]{2,1,0:T(8,128)(2,1)S(1)}, u32[]{:S(2)}, u32[]{:S(2)}) async-start(bf16[32,16,128]{2,1,0:T(8,128)(2,1)} %shard_map.73), calls=%async_computation.3 | async-start | bytes 262144 | tf_op jit(solution)/shard_map/all_to_all | solution.py:256
  78.3 0.0 copy-done.1
  78.3 2.3 %shard_map.71 = bf16[1024,128]{1,0:T(8,128)(2,1)} custom-call(bf16[64,9216]{1,0:T(8,128)(2,1)S(1)} %get-tuple-element.8.g_ref, bf16[27,32,64]{2,1,0:T(8,128)(2,1)S(1)} %bitcast.17), custom_call_target="tpu_custom_call" | custom-call | flops 452984832 | bytes 1552384 | tf_op jit(solution)/shard_map/pallas_call | solution.py:211
  80.6 4.9 %all-to-all-done.3 = bf16[32,16,128]{2,1,0:T(8,128)(2,1)S(1)} async-done(((bf16[32,16,128]{2,1,0:T(8,128)(2,1)}), bf16[32,16,128]{2,1,0:T(8,128)(2,1)S(1)}, u32[]{:S(2)}, u32[]{:S(2)}) %all-to-all-start.3) | async-done | bytes 131104 | tf_op jit(solution)/shard_map/all_to_all | solution.py:256
  85.5 0.9 %shard_map.74 = f32[27,32,64]{2,1,0:T(8,128)} custom-call(bf16[512,128]{1,0:T(8,128)(2,1)S(1)} %bitcast.14), custom_call_target="tpu_custom_call" | custom-call | bytes 352256 | tf_op jit(solution)/shard_map/pallas_call | solution.py:211
  (1 shorter events, 0.0 us)
Async XLA Ops:
  0.6 26.8 %copy-start = (bf16[1,32,2,16,128]{4,3,2,1,0:T(8,128)(2,1)S(1)}, bf16[1,32,2,16,128]{4,3,2,1,0:T(8,128)(2,1)}, u32[]{:S(2)}) copy-start(bf16[1,32,2,16,128]{4,3,2,1,0:T(8,128)(2,1)} %param.5) | copy-start | bytes 786436
  3.5 35.8 %copy-start.2 = (bf16[256,128]{1,0:T(8,128)(2,1)S(1)}, bf16[256,128]{1,0:T(8,128)(2,1)}, u32[]{:S(2)}) copy-start(bf16[256,128]{1,0:T(8,128)(2,1)} %get-tuple-element.7.own_ref) | copy-start | bytes 196612
  3.5 35.8 %all-to-all-start = ((bf16[32,64,128]{2,1,0:T(8,128)(2,1)}), bf16[32,64,128]{2,1,0:T(8,128)(2,1)S(1)}, u32[]{:S(2)}, u32[]{:S(2)}) async-start(bf16[32,64,128]{2,1,0:T(8,128)(2,1)} %bitcast.18), calls=%async_computation | async-start | bytes 1048576 | tf_op jit(solution)/shard_map/all_to_all | solution.py:238
  20.2 17.3 %collective-permute-start.1 = (bf16[256,128]{1,0:T(8,128)(2,1)}, bf16[256,128]{1,0:T(8,128)(2,1)S(1)}, u32[]{:S(2)}, u32[]{:S(2)}) collective-permute-start(bf16[256,128]{1,0:T(8,128)(2,1)} %get-tuple-element.7.own_ref), channel_id=1, source_target_pairs={{8,0},{16,8},{24,16},{0,24},{9,1},{17,9},{25,17},{1,25},{10,2},{18... | collective-permute-start | bytes 196616 | tf_op jit(solution)/shard_map/ppermute | solution.py:237
  25.5 12.0 %collective-permute-start = (bf16[256,128]{1,0:T(8,128)(2,1)}, bf16[256,128]{1,0:T(8,128)(2,1)S(1)}, u32[]{:S(2)}, u32[]{:S(2)}) collective-permute-start(bf16[256,128]{1,0:T(8,128)(2,1)} %get-tuple-element.7.own_ref), channel_id=1, source_target_pairs={{0,8},{8,16},{16,24},{24,0},{1,9},{9,17},{17,25},{25,1},{2,10},{10... | collective-permute-start | bytes 196616 | tf_op jit(solution)/shard_map/ppermute | solution.py:236
  39.3 39.0 %copy-start.1 = (bf16[64,32,3,3,3]{0,1,4,3,2:T(8,128)(2,1)S(1)}, bf16[64,32,3,3,3]{0,1,4,3,2:T(8,128)(2,1)}, u32[]{:S(2)}) copy-start(bf16[64,32,3,3,3]{0,1,4,3,2:T(8,128)(2,1)} %param.6) | copy-start | bytes 331780
  72.8 12.7 %all-to-all-start.3 = ((bf16[32,16,128]{2,1,0:T(8,128)(2,1)}), bf16[32,16,128]{2,1,0:T(8,128)(2,1)S(1)}, u32[]{:S(2)}, u32[]{:S(2)}) async-start(bf16[32,16,128]{2,1,0:T(8,128)(2,1)} %shard_map.73), calls=%async_computation.3 | async-start | bytes 262144 | tf_op jit(solution)/shard_map/all_to_all | solution.py:256

commit v7 on v5

--- a/solution.py
+++ b/solution.py
@@ -16,7 +16,7 @@
 
 
 def selection():
-    sel = np.zeros((SY * SZ * 2 * ROWS, 272), np.float32)
+    sel = np.zeros((SY * SZ * 2 * ROWS, 256), np.float32)
     for sy in range(SY):
         for sz in range(SZ):
             for ch in range(2):
@@ -25,7 +25,7 @@
                     if 0 <= py < SY:
                         for j in range(5):
                             row = ((sy * SZ + sz) * 2 + ch) * ROWS + dy * 5 + j
-                            sel[row, (ch * 4 + py) * 33 + 4 * sz + j] = 1
+                            sel[row, (ch * 4 + py) * 32 + (4 * sz + j) % 32] = 1
     return sel
 
 
@@ -47,11 +47,10 @@
     copies[0].wait()
     low = halves((8, 128))
     pooled = jnp.concatenate([pg_ref[0, 0].astype(F32), pg_ref[0, 1].astype(F32)], axis=0)
-    tiles[...] = jnp.zeros_like(tiles)
-    before = jnp.zeros((8, 128), F32)
-    for k in range(33):
-        tile = pooled[:, k * 128:(k + 1) * 128] if k < 32 else jnp.zeros((8, 128), F32)
-        tiles[pl.ds(k, 8, stride=33), :] = roll64(jnp.where(low, tile, before))
+    before = pooled[:, 31 * 128:]
+    for k in range(32):
+        tile = pooled[:, k * 128:(k + 1) * 128]
+        tiles[pl.ds(k, 8, stride=32), :] = roll64(jnp.where(low, tile, before))
         before = tile
     copies[2].wait()
     sent = jnp.dot(sel_ref[...], tiles[...].astype(BF16), preferred_element_type=F32).astype(BF16)
@@ -88,7 +87,8 @@
 
 def main_kernel(recv_ref, own_ref, below_ref, above_ref, act_ref, dw_ref, g_ref, rows):
     my_sy, my_sz = lax.axis_index("sy"), (lax.axis_index("zh") * 2 + lax.axis_index("zl"))
-    rows[...] = recv_ref[...].astype(F32)
+    for o in range(COUT):
+        rows[o * ROWS:(o + 1) * ROWS] = recv_ref[o * 32:o * 32 + ROWS].astype(F32)
     low = halves((64, 128))
     low32 = halves((32, 128))
     parity = jnp.where(low, 0.0, 1.0)
@@ -100,7 +100,7 @@
     def halo(sy, sz):
         base = (jnp.clip(sy, 0, SY - 1) * SZ + jnp.clip(sz, 0, SZ - 1)) * 64
         packed = jnp.concatenate(
-            [rows[pl.ds(pl.multiple_of(base + 16, 16), 16), :], rows[pl.ds(pl.multiple_of(base + 48, 16), 16), :]], axis=0
+            [recv_ref[pl.ds(pl.multiple_of(base + k, 16), 16), :].astype(F32) for k in (16, 48)], axis=0
         )
         other = roll64(packed)
         return jnp.concatenate(
@@ -114,8 +114,10 @@
         values = None
         for pz in range(10):
             if pz % 2 == 0:
-                values = rows[pl.ds(dy * 5 + pz // 2, 64, stride=32), :]
+                values = rows[pl.ds(dy * 5 + pz // 2, COUT, stride=ROWS), :]
             value = spread(values, pz % 2 == 0)
+            if pz in (0, 9):
+                value = jnp.where(my_sz == (0 if pz == 0 else SZ - 1), 0.0, value)
             if pz == 0:
                 code = before
             elif pz == 9:
@@ -188,15 +190,22 @@
         out_ref[k] = total
 
 
-def final_kernel(scale, in_ref, out_ref):
+def final_kernel(scale, in_ref, out_any, out_ref, sems):
+    leaving = []
     for ab in range(9):
         j, half = divmod(ab, 2)
         part = in_ref[j * 96:(j + 1) * 96, half * 64:half * 64 + 64].astype(F32) * scale
         for c in range(3):
             out_ref[3 * ab + c] = part[c * 32:(c + 1) * 32]
-
-
-def call(kernel, outs, scratch, args, flops=0, hbm=False):
+        if ab % 3 == 2:
+            done = pl.ds(3 * (ab - 2), 9)
+            leaving.append(pltpu.make_async_copy(out_ref.at[done], out_any.at[done], sems.at[ab // 3]))
+            leaving[-1].start()
+    for copy in leaving:
+        copy.wait()
+
+
+def call(kernel, outs, scratch, args, flops=0, hbm=False, out_hbm=False):
     vmem = pl.BlockSpec(memory_space=pltpu.VMEM)
     specs = [pl.BlockSpec(memory_space=pltpu.HBM) if hbm else vmem] * len(args)
     nbytes = sum(int(np.prod(v.shape)) * v.dtype.itemsize for v in list(args) + list(outs))
@@ -204,7 +213,7 @@
         kernel,
         out_shape=tuple(outs) if len(outs) > 1 else outs[0],
         in_specs=specs,
-        out_specs=tuple([vmem] * len(outs)) if len(outs) > 1 else vmem,
+        out_specs=tuple([vmem] * len(outs)) if len(outs) > 1 else pl.BlockSpec(memory_space=pltpu.HBM) if out_hbm else vmem,
         scratch_shapes=scratch,
         compiler_params=pltpu.CompilerParams(vmem_limit_bytes=60 * 1024 * 1024 if hbm else LIMIT),
         cost_estimate=pl.CostEstimate(flops=flops, bytes_accessed=nbytes, transcendentals=0),
@@ -219,10 +228,10 @@
     sent, codes = call(
         pack_kernel, [shape((2048, 128), BF16), shape((256, 128), BF16)],
         [
-            pltpu.VMEM((272, 128), F32), pltpu.VMEM((1, 2, SY, 4096), BF16), pltpu.VMEM((256, 128), jnp.int32),
-            pltpu.VMEM((1024, 272), BF16), pltpu.SemaphoreType.DMA((3,)),
+            pltpu.VMEM((256, 128), F32), pltpu.VMEM((1, 2, SY, 4096), BF16), pltpu.VMEM((256, 128), jnp.int32),
+            pltpu.VMEM((1024, 256), BF16), pltpu.SemaphoreType.DMA((3,)),
         ],
-        (pooled_grad, window_argmax.reshape(256, 128), sel), flops=2 * 1024 * 272 * 128, hbm=True,
+        (pooled_grad, window_argmax.reshape(256, 128), sel), flops=2 * 1024 * 256 * 128, hbm=True,
     )
     below = lax.ppermute(codes, "sy", rise)
     above = lax.ppermute(codes, "sy", fall)
@@ -232,7 +241,7 @@
         (activations.reshape(1024, 128),), flops=2 * 1024 * 128 * 384,
     )
     local, grad_out = call(
-        main_kernel, [shape((512, 128), BF16), shape((COUT, 72 * 128), BF16)], [pltpu.VMEM((2048, 128), F32)],
+        main_kernel, [shape((512, 128), BF16), shape((COUT, 72 * 128), BF16)], [pltpu.VMEM((COUT * ROWS, 128), F32)],
         (recv, codes, below, above, taps), flops=2 * 96 * 576 * 4096,
     )
     input_grad = call(
@@ -248,7 +257,8 @@
     pooled = SAMPLE * SY * SZ * 8 * 64
     dw = call(
         functools.partial(final_kernel, float(1.0 / np.sqrt(np.float32(pooled)))),
-        [shape((27, CIN, COUT), F32)], [], (whole,),
+        [shape((27, CIN, COUT), F32)], [pltpu.VMEM((27, CIN, COUT), F32), pltpu.SemaphoreType.DMA((3,))],
+        (whole,), out_hbm=True,
     )
     dw = jnp.transpose(dw.reshape(3, 3, 3, CIN, COUT), (4, 3, 0, 1, 2))
     return input_grad.reshape(1, CIN, 2, 16, 128), dw

time: 86.7 us -> 86.3 us (level)
  no operation moved by 1% of the time
where the time goes in v7:
time: 86.3 us; the launch traced here: 85.9 us
  blocking collectives  30.9 us (36%)
  starting transfers between devices  29.4 us (34%)
  waiting for transfers between devices  15.2 us (18%)
  Pallas kernels  9.66 us (11%)
    all_to_all x1, starting transfers between devices, body(): lax.all_to_all(sent.reshape(32, 64, 128), ('sy', 'zh', 'zl'), 0, 0)  16.7 us
    all_to_all x1, blocking collectives, body(): part = lax.all_to_all(local.reshape(2 * SAMPLE, 16, 128), near, 0, 0)  15.6 us
    all_to_all x1, blocking collectives, body(): part = lax.all_to_all(part, far, 0, 0)  15.4 us
    pallas_call x7, Pallas kernels, call(): pl.pallas_call(kernel, out_shape=tuple(outs) if len(outs) > 1 else outs[0...  9.66 us
    ppermute x1, waiting for transfers between devices, body(): above = lax.ppermute(codes, 'sy', fall)  8.51 us
    all_to_all x1, starting transfers between devices, body(): whole = lax.all_to_all(part, near, 0, 0).reshape(512, 128)  5.49 us
    ppermute x1, starting transfers between devices, body(): above = lax.ppermute(codes, 'sy', fall)  5.29 us
    all_to_all x1, waiting for transfers between devices, body(): whole = lax.all_to_all(part, near, 0, 0).reshape(512, 128)  4.88 us
  transfers between devices with their start and end apart: 4, of which 3 were waited for; matrix products, arithmetic and copies ran while one was open for 0% of the time, Pallas kernels for 4%

profile of v7, /device:TPU:1, one launch (start us, length us, event | category | flops | bytes accessed | tf_op | source)
XLA Modules:
  0.0 85.9 jit_solution(11677979202645506346)
XLA Ops:
  0.6 0.0 copy-start
  0.6 2.4 %shard_map.68 = (bf16[2048,128]{1,0:T(8,128)(2,1)}, bf16[256,128]{1,0:T(8,128)(2,1)}) custom-call(bf16[1,2,4,4096]{3,2,1,0:T(4,128)(2,1)} %pg_any.1, s32[256,128]{1,0:T(8,128)} %bitcast.20, bf16[1024,256]{1,0:T(8,128)(2,1)} %constant.2.clone.sel_any), custom_call_target="tpu_custom_call" | custom-call | flops 67108864 | bytes 1310720 | tf_op jit(solution)/shard_map/pallas_call | solution.py:212
  3.1 0.0 copy-start.2
  3.1 16.7 %all-to-all-start = ((bf16[32,64,128]{2,1,0:T(8,128)(2,1)}), bf16[32,64,128]{2,1,0:T(8,128)(2,1)S(1)}, u32[]{:S(2)}, u32[]{:S(2)}) async-start(bf16[32,64,128]{2,1,0:T(8,128)(2,1)} %bitcast.18), calls=%async_computation | async-start | bytes 1048576 | tf_op jit(solution)/shard_map/all_to_all | solution.py:238
  19.7 5.3 %collective-permute-start.1 = (bf16[256,128]{1,0:T(8,128)(2,1)}, bf16[256,128]{1,0:T(8,128)(2,1)S(1)}, u32[]{:S(2)}, u32[]{:S(2)}) collective-permute-start(bf16[256,128]{1,0:T(8,128)(2,1)} %get-tuple-element.7.own_ref), channel_id=1, source_target_pairs={{8,0},{16,8},{24,16},{0,24},{9,1},{17,9},{25,17},{1,25},{10,2},{18... | collective-permute-start | bytes 196616 | tf_op jit(solution)/shard_map/ppermute | solution.py:237
  25.0 1.9 %collective-permute-start = (bf16[256,128]{1,0:T(8,128)(2,1)}, bf16[256,128]{1,0:T(8,128)(2,1)S(1)}, u32[]{:S(2)}, u32[]{:S(2)}) collective-permute-start(bf16[256,128]{1,0:T(8,128)(2,1)} %get-tuple-element.7.own_ref), channel_id=1, source_target_pairs={{0,8},{8,16},{16,24},{24,0},{1,9},{9,17},{17,25},{25,1},{2,10},{10... | collective-permute-start | bytes 196616 | tf_op jit(solution)/shard_map/ppermute | solution.py:236
  27.0 0.0 copy-done
  27.0 1.5 %shard_map.69.act_ref = bf16[96,4096]{1,0:T(8,128)(2,1)S(1)} custom-call(bf16[1024,128]{1,0:T(8,128)(2,1)S(1)} %bitcast.15), custom_call_target="tpu_custom_call" | custom-call | flops 100663296 | bytes 1048576 | tf_op jit(solution)/shard_map/pallas_call | solution.py:212
  28.5 8.5 %collective-permute-done.1.above_ref = bf16[256,128]{1,0:T(8,128)(2,1)S(1)} collective-permute-done((bf16[256,128]{1,0:T(8,128)(2,1)}, bf16[256,128]{1,0:T(8,128)(2,1)S(1)}, u32[]{:S(2)}, u32[]{:S(2)}) %collective-permute-start.1) | collective-permute-done | bytes 65568 | tf_op jit(solution)/shard_map/ppermute | solution.py:237
  37.0 0.0 collective-permute-done.below_ref
  37.0 1.8 %all-to-all-done = bf16[32,64,128]{2,1,0:T(8,128)(2,1)S(1)} async-done(((bf16[32,64,128]{2,1,0:T(8,128)(2,1)}), bf16[32,64,128]{2,1,0:T(8,128)(2,1)S(1)}, u32[]{:S(2)}, u32[]{:S(2)}) %all-to-all-start) | async-done | bytes 524320 | tf_op jit(solution)/shard_map/all_to_all | solution.py:238
  38.9 0.0 copy-done.2
  38.9 0.0 copy-start.1
  38.9 1.8 %shard_map.70 = (bf16[512,128]{1,0:T(8,128)(2,1)S(1)}, bf16[64,9216]{1,0:T(8,128)(2,1)S(1)}) custom-call(bf16[2048,128]{1,0:T(8,128)(2,1)S(1)} %bitcast.13, bf16[256,128]{1,0:T(8,128)(2,1)S(1)} %copy-done.2, bf16[256,128]{1,0:T(8,128)(2,1)S(1)} %collective-permute-done.below_ref, bf16[256,128]{1,0:T(8,128)(2,1)S(1)} %collective-permute-done.1.above_ref, ...), custom_call_target="tpu_custom_call" | custom-call | flops 452984832 | bytes 2818048 | tf_op jit(solution)/shard_map/pallas_call | solution.py:212
  40.7 15.6 %all_to_all.20.in_ref = bf16[32,16,128]{2,1,0:T(8,128)(2,1)S(1)} all-to-all(bf16[32,16,128]{2,1,0:T(8,128)(2,1)S(1)} %bitcast.16), channel_id=1, replica_groups=mesh['sample'=16,'sy'=4,'zh'=4,'zl'=2] {'sample','zl'}, dimensions={0} | all-to-all | bytes 262144 | tf_op jit(solution)/shard_map/all_to_all | solution.py:252
  56.3 15.4 %all_to_all.21.in_ref = bf16[16,16,128]{2,1,0:T(8,128)(2,1)S(1)} all-to-all(bf16[16,16,128]{2,1,0:T(8,128)(2,1)S(1)} %shard_map.72), channel_id=1, replica_groups=mesh['sample'=16,'sy'=4,'zh'=4,'zl'=2] {'sy','zh'}, dimensions={0} | all-to-all | bytes 131072 | tf_op jit(solution)/shard_map/all_to_all | solution.py:254
  71.7 0.7 shard_map.73
  72.4 5.5 %all-to-all-start.3 = ((bf16[32,16,128]{2,1,0:T(8,128)(2,1)}), bf16[32,16,128]{2,1,0:T(8,128)(2,1)S(1)}, u32[]{:S(2)}, u32[]{:S(2)}) async-start(bf16[32,16,128]{2,1,0:T(8,128)(2,1)} %shard_map.73), calls=%async_computation.3 | async-start | bytes 262144 | tf_op jit(solution)/shard_map/all_to_all | solution.py:256
  77.9 0.0 copy-done.1
  77.9 2.3 %shard_map.71 = bf16[1024,128]{1,0:T(8,128)(2,1)} custom-call(bf16[64,9216]{1,0:T(8,128)(2,1)S(1)} %get-tuple-element.8.g_ref, bf16[27,32,64]{2,1,0:T(8,128)(2,1)S(1)} %bitcast.17), custom_call_target="tpu_custom_call" | custom-call | flops 452984832 | bytes 1552384 | tf_op jit(solution)/shard_map/pallas_call | solution.py:212
  80.2 4.9 %all-to-all-done.3 = bf16[32,16,128]{2,1,0:T(8,128)(2,1)S(1)} async-done(((bf16[32,16,128]{2,1,0:T(8,128)(2,1)}), bf16[32,16,128]{2,1,0:T(8,128)(2,1)S(1)}, u32[]{:S(2)}, u32[]{:S(2)}) %all-to-all-start.3) | async-done | bytes 131104 | tf_op jit(solution)/shard_map/all_to_all | solution.py:256
  85.0 0.9 %shard_map.74 = f32[27,32,64]{2,1,0:T(8,128)} custom-call(bf16[512,128]{1,0:T(8,128)(2,1)S(1)} %bitcast.14), custom_call_target="tpu_custom_call" | custom-call | bytes 352256 | tf_op jit(solution)/shard_map/pallas_call | solution.py:212
  (1 shorter events, 0.0 us)
Async XLA Ops:
  0.6 26.3 %copy-start = (bf16[1,32,2,16,128]{4,3,2,1,0:T(8,128)(2,1)S(1)}, bf16[1,32,2,16,128]{4,3,2,1,0:T(8,128)(2,1)}, u32[]{:S(2)}) copy-start(bf16[1,32,2,16,128]{4,3,2,1,0:T(8,128)(2,1)} %param.5) | copy-start | bytes 786436
  3.1 35.8 %copy-start.2 = (bf16[256,128]{1,0:T(8,128)(2,1)S(1)}, bf16[256,128]{1,0:T(8,128)(2,1)}, u32[]{:S(2)}) copy-start(bf16[256,128]{1,0:T(8,128)(2,1)} %get-tuple-element.7.own_ref) | copy-start | bytes 196612
  3.1 35.8 %all-to-all-start = ((bf16[32,64,128]{2,1,0:T(8,128)(2,1)}), bf16[32,64,128]{2,1,0:T(8,128)(2,1)S(1)}, u32[]{:S(2)}, u32[]{:S(2)}) async-start(bf16[32,64,128]{2,1,0:T(8,128)(2,1)} %bitcast.18), calls=%async_computation | async-start | bytes 1048576 | tf_op jit(solution)/shard_map/all_to_all | solution.py:238
  19.7 17.3 %collective-permute-start.1 = (bf16[256,128]{1,0:T(8,128)(2,1)}, bf16[256,128]{1,0:T(8,128)(2,1)S(1)}, u32[]{:S(2)}, u32[]{:S(2)}) collective-permute-start(bf16[256,128]{1,0:T(8,128)(2,1)} %get-tuple-element.7.own_ref), channel_id=1, source_target_pairs={{8,0},{16,8},{24,16},{0,24},{9,1},{17,9},{25,17},{1,25},{10,2},{18... | collective-permute-start | bytes 196616 | tf_op jit(solution)/shard_map/ppermute | solution.py:237
  25.0 12.0 %collective-permute-start = (bf16[256,128]{1,0:T(8,128)(2,1)}, bf16[256,128]{1,0:T(8,128)(2,1)S(1)}, u32[]{:S(2)}, u32[]{:S(2)}) collective-permute-start(bf16[256,128]{1,0:T(8,128)(2,1)} %get-tuple-element.7.own_ref), channel_id=1, source_target_pairs={{0,8},{8,16},{16,24},{24,0},{1,9},{9,17},{17,25},{25,1},{2,10},{10... | collective-permute-start | bytes 196616 | tf_op jit(solution)/shard_map/ppermute | solution.py:236
  38.9 39.0 %copy-start.1 = (bf16[64,32,3,3,3]{0,1,4,3,2:T(8,128)(2,1)S(1)}, bf16[64,32,3,3,3]{0,1,4,3,2:T(8,128)(2,1)}, u32[]{:S(2)}) copy-start(bf16[64,32,3,3,3]{0,1,4,3,2:T(8,128)(2,1)} %param.6) | copy-start | bytes 331780
  72.4 12.7 %all-to-all-start.3 = ((bf16[32,16,128]{2,1,0:T(8,128)(2,1)}), bf16[32,16,128]{2,1,0:T(8,128)(2,1)S(1)}, u32[]{:S(2)}, u32[]{:S(2)}) async-start(bf16[32,16,128]{2,1,0:T(8,128)(2,1)} %shard_map.73), calls=%async_computation.3 | async-start | bytes 262144 | tf_op jit(solution)/shard_map/all_to_all | solution.py:256

commit v8 on v7

--- a/solution.py
+++ b/solution.py
@@ -251,7 +251,7 @@
     near, far = ("sample", "zl"), ("sy", "zh")
     part = lax.all_to_all(local.reshape(2 * SAMPLE, 16, 128), near, 0, 0)
     part = call(sum_kernel, [shape((SY * SZ // 2, 16, 128), BF16)], [], (part,))
-    part = lax.all_to_all(part, far, 0, 0)
+    part, input_grad = lax.optimization_barrier((lax.all_to_all(part, far, 0, 0), input_grad))
     part = call(sum_kernel, [shape((2 * SAMPLE, 16, 128), BF16)], [], (part,))
     whole = lax.all_to_all(part, near, 0, 0).reshape(512, 128)
     pooled = SAMPLE * SY * SZ * 8 * 64

time: 86.3 us -> 85.6 us (level)
  waiting for transfers between devices: 15.2 us -> 19.3 us
  blocking collectives: 30.9 us -> 27.3 us
  starting transfers between devices: 29.4 us -> 28.1 us
    all_to_all x1, waiting for transfers between devices: 4.88 us -> 8.99 us  [body(): lax.all_to_all(part, far, 0, 0)]
    all_to_all x1, blocking collectives: 15.4 us -> 11.8 us  [body(): whole = lax.all_to_all(part, near, 0, 0).reshape(512, 128)]
    all_to_all x1, starting transfers between devices: 5.49 us -> 4.24 us  [body(): lax.all_to_all(part, far, 0, 0)]
  transfers between devices with their start and end apart: 4 -> 4, of which waited for: 3 -> 3; matrix products, arithmetic and copies ran while one was open for 0% -> 0% of each run, Pallas kernels for 4% -> 5%
where the time goes in v8:
time: 85.6 us; the launch traced here: 85.2 us
  starting transfers between devices  28.1 us (33%)
  blocking collectives  27.3 us (32%)
  waiting for transfers between devices  19.3 us (23%)
  Pallas kernels  9.68 us (11%)
    all_to_all x1, starting transfers between devices, body(): lax.all_to_all(sent.reshape(32, 64, 128), ('sy', 'zh', 'zl'), 0, 0)  16.7 us
    all_to_all x1, blocking collectives, body(): part = lax.all_to_all(local.reshape(2 * SAMPLE, 16, 128), near, 0, 0)  15.6 us
    all_to_all x1, blocking collectives, body(): whole = lax.all_to_all(part, near, 0, 0).reshape(512, 128)  11.8 us
    pallas_call x7, Pallas kernels, call(): pl.pallas_call(kernel, out_shape=tuple(outs) if len(outs) > 1 else outs[0...  9.68 us
    all_to_all x1, waiting for transfers between devices, body(): lax.all_to_all(part, far, 0, 0)  8.99 us
    ppermute x1, waiting for transfers between devices, body(): above = lax.ppermute(codes, 'sy', fall)  8.5 us
    ppermute x1, starting transfers between devices, body(): above = lax.ppermute(codes, 'sy', fall)  5.29 us
    all_to_all x1, starting transfers between devices, body(): lax.all_to_all(part, far, 0, 0)  4.24 us
  transfers between devices with their start and end apart: 4, of which 3 were waited for; matrix products, arithmetic and copies ran while one was open for 0% of the time, Pallas kernels for 5%

profile of v8, /device:TPU:1, one launch (start us, length us, event | category | flops | bytes accessed | tf_op | source)
XLA Modules:
  0.0 85.2 jit_solution(4608258842062430576)
XLA Ops:
  0.6 0.0 copy-start
  0.6 2.4 %shard_map.68 = (bf16[2048,128]{1,0:T(8,128)(2,1)}, bf16[256,128]{1,0:T(8,128)(2,1)}) custom-call(bf16[1,2,4,4096]{3,2,1,0:T(4,128)(2,1)} %pg_any.1, s32[256,128]{1,0:T(8,128)} %bitcast.20, bf16[1024,256]{1,0:T(8,128)(2,1)} %constant.2.clone.sel_any), custom_call_target="tpu_custom_call" | custom-call | flops 67108864 | bytes 1310720 | tf_op jit(solution)/shard_map/pallas_call | solution.py:212
  3.1 0.0 copy-start.2
  3.1 16.7 %all-to-all-start = ((bf16[32,64,128]{2,1,0:T(8,128)(2,1)}), bf16[32,64,128]{2,1,0:T(8,128)(2,1)S(1)}, u32[]{:S(2)}, u32[]{:S(2)}) async-start(bf16[32,64,128]{2,1,0:T(8,128)(2,1)} %bitcast.18), calls=%async_computation | async-start | bytes 1048576 | tf_op jit(solution)/shard_map/all_to_all | solution.py:238
  19.7 5.3 %collective-permute-start.1 = (bf16[256,128]{1,0:T(8,128)(2,1)}, bf16[256,128]{1,0:T(8,128)(2,1)S(1)}, u32[]{:S(2)}, u32[]{:S(2)}) collective-permute-start(bf16[256,128]{1,0:T(8,128)(2,1)} %get-tuple-element.9.own_ref), channel_id=1, source_target_pairs={{8,0},{16,8},{24,16},{0,24},{9,1},{17,9},{25,17},{1,25},{10,2},{18... | collective-permute-start | bytes 196616 | tf_op jit(solution)/shard_map/ppermute | solution.py:237
  25.0 1.9 %collective-permute-start = (bf16[256,128]{1,0:T(8,128)(2,1)}, bf16[256,128]{1,0:T(8,128)(2,1)S(1)}, u32[]{:S(2)}, u32[]{:S(2)}) collective-permute-start(bf16[256,128]{1,0:T(8,128)(2,1)} %get-tuple-element.9.own_ref), channel_id=1, source_target_pairs={{0,8},{8,16},{16,24},{24,0},{1,9},{9,17},{17,25},{25,1},{2,10},{10... | collective-permute-start | bytes 196616 | tf_op jit(solution)/shard_map/ppermute | solution.py:236
  27.0 0.0 copy-done
  27.0 1.5 %shard_map.69.act_ref = bf16[96,4096]{1,0:T(8,128)(2,1)S(1)} custom-call(bf16[1024,128]{1,0:T(8,128)(2,1)S(1)} %bitcast.15), custom_call_target="tpu_custom_call" | custom-call | flops 100663296 | bytes 1048576 | tf_op jit(solution)/shard_map/pallas_call | solution.py:212
  28.5 0.0 copy-start.1
  28.5 8.5 %collective-permute-done.1.above_ref = bf16[256,128]{1,0:T(8,128)(2,1)S(1)} collective-permute-done((bf16[256,128]{1,0:T(8,128)(2,1)}, bf16[256,128]{1,0:T(8,128)(2,1)S(1)}, u32[]{:S(2)}, u32[]{:S(2)}) %collective-permute-start.1) | collective-permute-done | bytes 65568 | tf_op jit(solution)/shard_map/ppermute | solution.py:237
  37.0 0.0 collective-permute-done.below_ref
  37.0 1.8 %all-to-all-done = bf16[32,64,128]{2,1,0:T(8,128)(2,1)S(1)} async-done(((bf16[32,64,128]{2,1,0:T(8,128)(2,1)}), bf16[32,64,128]{2,1,0:T(8,128)(2,1)S(1)}, u32[]{:S(2)}, u32[]{:S(2)}) %all-to-all-start) | async-done | bytes 524320 | tf_op jit(solution)/shard_map/all_to_all | solution.py:238
  38.9 0.0 copy-done.2
  38.9 1.8 %shard_map.70 = (bf16[512,128]{1,0:T(8,128)(2,1)S(1)}, bf16[64,9216]{1,0:T(8,128)(2,1)S(1)}) custom-call(bf16[2048,128]{1,0:T(8,128)(2,1)S(1)} %bitcast.13, bf16[256,128]{1,0:T(8,128)(2,1)S(1)} %copy-done.2, bf16[256,128]{1,0:T(8,128)(2,1)S(1)} %collective-permute-done.below_ref, bf16[256,128]{1,0:T(8,128)(2,1)S(1)} %collective-permute-done.1.above_ref, ...), custom_call_target="tpu_custom_call" | custom-call | flops 452984832 | bytes 2818048 | tf_op jit(solution)/shard_map/pallas_call | solution.py:212
  40.7 15.6 %all_to_all.20.in_ref = bf16[32,16,128]{2,1,0:T(8,128)(2,1)S(1)} all-to-all(bf16[32,16,128]{2,1,0:T(8,128)(2,1)S(1)} %bitcast.16), channel_id=1, replica_groups=mesh['sample'=16,'sy'=4,'zh'=4,'zl'=2] {'sample','zl'}, dimensions={0} | all-to-all | bytes 262144 | tf_op jit(solution)/shard_map/all_to_all | solution.py:252
  56.3 0.7 shard_map.71
  56.9 4.2 %all-to-all-start.2 = ((bf16[16,16,128]{2,1,0:T(8,128)(2,1)}), bf16[16,16,128]{2,1,0:T(8,128)(2,1)S(1)}, u32[]{:S(2)}, u32[]{:S(2)}) async-start(bf16[16,16,128]{2,1,0:T(8,128)(2,1)} %shard_map.71), calls=%async_computation.2 | async-start | bytes 131072 | tf_op jit(solution)/shard_map/all_to_all | solution.py:254
  61.2 0.0 copy-done.1
  61.2 2.3 %shard_map.72 = bf16[1024,128]{1,0:T(8,128)(2,1)} custom-call(bf16[64,9216]{1,0:T(8,128)(2,1)S(1)} %get-tuple-element.11.g_ref, bf16[27,32,64]{2,1,0:T(8,128)(2,1)S(1)} %bitcast.17), custom_call_target="tpu_custom_call" | custom-call | flops 452984832 | bytes 1552384 | tf_op jit(solution)/shard_map/pallas_call | solution.py:212
  63.5 9.0 %all-to-all-done.2.in_ref = bf16[16,16,128]{2,1,0:T(8,128)(2,1)S(1)} async-done(((bf16[16,16,128]{2,1,0:T(8,128)(2,1)}), bf16[16,16,128]{2,1,0:T(8,128)(2,1)S(1)}, u32[]{:S(2)}, u32[]{:S(2)}) %all-to-all-start.2) | async-done | bytes 65568 | tf_op jit(solution)/shard_map/all_to_all | solution.py:254
  72.6 11.8 %all_to_all.21 = bf16[32,16,128]{2,1,0:T(8,128)(2,1)S(1)} all-to-all(bf16[32,16,128]{2,1,0:T(8,128)(2,1)S(1)} %shard_map.73), channel_id=1, replica_groups=mesh['sample'=16,'sy'=4,'zh'=4,'zl'=2] {'sample','zl'}, dimensions={0} | all-to-all | bytes 262144 | tf_op jit(solution)/shard_map/all_to_all | solution.py:256
  84.3 0.9 %shard_map.74 = f32[27,32,64]{2,1,0:T(8,128)} custom-call(bf16[512,128]{1,0:T(8,128)(2,1)S(1)} %bitcast.14), custom_call_target="tpu_custom_call" | custom-call | bytes 352256 | tf_op jit(solution)/shard_map/pallas_call | solution.py:212
  (1 shorter events, 0.0 us)
Async XLA Ops:
  0.6 26.3 %copy-start = (bf16[1,32,2,16,128]{4,3,2,1,0:T(8,128)(2,1)S(1)}, bf16[1,32,2,16,128]{4,3,2,1,0:T(8,128)(2,1)}, u32[]{:S(2)}) copy-start(bf16[1,32,2,16,128]{4,3,2,1,0:T(8,128)(2,1)} %param.5) | copy-start | bytes 786436
  3.1 35.8 %copy-start.2 = (bf16[256,128]{1,0:T(8,128)(2,1)S(1)}, bf16[256,128]{1,0:T(8,128)(2,1)}, u32[]{:S(2)}) copy-start(bf16[256,128]{1,0:T(8,128)(2,1)} %get-tuple-element.9.own_ref) | copy-start | bytes 196612
  3.1 35.8 %all-to-all-start = ((bf16[32,64,128]{2,1,0:T(8,128)(2,1)}), bf16[32,64,128]{2,1,0:T(8,128)(2,1)S(1)}, u32[]{:S(2)}, u32[]{:S(2)}) async-start(bf16[32,64,128]{2,1,0:T(8,128)(2,1)} %bitcast.18), calls=%async_computation | async-start | bytes 1048576 | tf_op jit(solution)/shard_map/all_to_all | solution.py:238
  19.7 17.3 %collective-permute-start.1 = (bf16[256,128]{1,0:T(8,128)(2,1)}, bf16[256,128]{1,0:T(8,128)(2,1)S(1)}, u32[]{:S(2)}, u32[]{:S(2)}) collective-permute-start(bf16[256,128]{1,0:T(8,128)(2,1)} %get-tuple-element.9.own_ref), channel_id=1, source_target_pairs={{8,0},{16,8},{24,16},{0,24},{9,1},{17,9},{25,17},{1,25},{10,2},{18... | collective-permute-start | bytes 196616 | tf_op jit(solution)/shard_map/ppermute | solution.py:237
  25.0 12.0 %collective-permute-start = (bf16[256,128]{1,0:T(8,128)(2,1)}, bf16[256,128]{1,0:T(8,128)(2,1)S(1)}, u32[]{:S(2)}, u32[]{:S(2)}) collective-permute-start(bf16[256,128]{1,0:T(8,128)(2,1)} %get-tuple-element.9.own_ref), channel_id=1, source_target_pairs={{0,8},{8,16},{16,24},{24,0},{1,9},{9,17},{17,25},{25,1},{2,10},{10... | collective-permute-start | bytes 196616 | tf_op jit(solution)/shard_map/ppermute | solution.py:236
  28.5 32.7 %copy-start.1 = (bf16[64,32,3,3,3]{0,1,4,3,2:T(8,128)(2,1)S(1)}, bf16[64,32,3,3,3]{0,1,4,3,2:T(8,128)(2,1)}, u32[]{:S(2)}) copy-start(bf16[64,32,3,3,3]{0,1,4,3,2:T(8,128)(2,1)} %param.6) | copy-start | bytes 331780
  56.9 15.6 %all-to-all-start.2 = ((bf16[16,16,128]{2,1,0:T(8,128)(2,1)}), bf16[16,16,128]{2,1,0:T(8,128)(2,1)S(1)}, u32[]{:S(2)}, u32[]{:S(2)}) async-start(bf16[16,16,128]{2,1,0:T(8,128)(2,1)} %shard_map.71), calls=%async_computation.2 | async-start | bytes 131072 | tf_op jit(solution)/shard_map/all_to_all | solution.py:254

commit v9 on v7

--- a/solution.py
+++ b/solution.py
@@ -249,7 +249,9 @@
         (grad_out, jnp.transpose(weight, (2, 3, 4, 1, 0)).reshape(27, CIN, COUT)), flops=2 * 96 * 576 * 4096,
     )
     near, far = ("sample", "zl"), ("sy", "zh")
-    part = lax.all_to_all(local.reshape(2 * SAMPLE, 16, 128), near, 0, 0)
+    part, input_grad = lax.optimization_barrier(
+        (lax.all_to_all(local.reshape(2 * SAMPLE, 16, 128), near, 0, 0), input_grad)
+    )
     part = call(sum_kernel, [shape((SY * SZ // 2, 16, 128), BF16)], [], (part,))
     part = lax.all_to_all(part, far, 0, 0)
     part = call(sum_kernel, [shape((2 * SAMPLE, 16, 128), BF16)], [], (part,))

time: 86.3 us -> 85.6 us (level)
  blocking collectives: 30.9 us -> 27.2 us
  starting transfers between devices: 29.4 us -> 32.6 us
    all_to_all x1, blocking collectives: 15.6 us -> 11.8 us  [body(): whole = lax.all_to_all(part, near, 0, 0).reshape(512, 128)]
    all_to_all x1, starting transfers between devices: 5.49 us -> 8.68 us  [body(): lax.all_to_all(local.reshape(2 * SAMPLE, 16, 128), near, 0, 0)]
  transfers between devices with their start and end apart: 4 -> 4, of which waited for: 3 -> 3; matrix products, arithmetic and copies ran while one was open for 0% -> 0% of each run, Pallas kernels for 4% -> 5%
where the time goes in v9:
time: 85.6 us; the launch traced here: 85.2 us
  starting transfers between devices  32.6 us (38%)
  blocking collectives  27.2 us (32%)
  waiting for transfers between devices  15.1 us (18%)
  Pallas kernels  9.66 us (11%)
    all_to_all x1, starting transfers between devices, body(): lax.all_to_all(sent.reshape(32, 64, 128), ('sy', 'zh', 'zl'), 0, 0)  16.7 us
    all_to_all x1, blocking collectives, body(): part = lax.all_to_all(part, far, 0, 0)  15.4 us
    all_to_all x1, blocking collectives, body(): whole = lax.all_to_all(part, near, 0, 0).reshape(512, 128)  11.8 us
    pallas_call x7, Pallas kernels, call(): pl.pallas_call(kernel, out_shape=tuple(outs) if len(outs) > 1 else outs[0...  9.66 us
    all_to_all x1, starting transfers between devices, body(): lax.all_to_all(local.reshape(2 * SAMPLE, 16, 128), near, 0, 0)  8.68 us
    ppermute x1, waiting for transfers between devices, body(): above = lax.ppermute(codes, 'sy', fall)  8.5 us
    ppermute x1, starting transfers between devices, body(): above = lax.ppermute(codes, 'sy', fall)  5.29 us
    all_to_all x1, waiting for transfers between devices, body(): lax.all_to_all(local.reshape(2 * SAMPLE, 16, 128), near, 0, 0)  4.77 us
  transfers between devices with their start and end apart: 4, of which 3 were waited for; matrix products, arithmetic and copies ran while one was open for 0% of the time, Pallas kernels for 5%

profile of v9, /device:TPU:1, one launch (start us, length us, event | category | flops | bytes accessed | tf_op | source)
XLA Modules:
  0.0 85.2 jit_solution(16563605680193895100)
XLA Ops:
  0.6 0.0 copy-start
  0.6 2.4 %shard_map.68 = (bf16[2048,128]{1,0:T(8,128)(2,1)}, bf16[256,128]{1,0:T(8,128)(2,1)}) custom-call(bf16[1,2,4,4096]{3,2,1,0:T(4,128)(2,1)} %pg_any.1, s32[256,128]{1,0:T(8,128)} %bitcast.19, bf16[1024,256]{1,0:T(8,128)(2,1)} %constant.2.clone.sel_any), custom_call_target="tpu_custom_call" | custom-call | flops 67108864 | bytes 1310720 | tf_op jit(solution)/shard_map/pallas_call | solution.py:212
  3.1 0.0 copy-start.2
  3.1 16.7 %all-to-all-start = ((bf16[32,64,128]{2,1,0:T(8,128)(2,1)}), bf16[32,64,128]{2,1,0:T(8,128)(2,1)S(1)}, u32[]{:S(2)}, u32[]{:S(2)}) async-start(bf16[32,64,128]{2,1,0:T(8,128)(2,1)} %bitcast.17), calls=%async_computation | async-start | bytes 1048576 | tf_op jit(solution)/shard_map/all_to_all | solution.py:238
  19.7 5.3 %collective-permute-start.1 = (bf16[256,128]{1,0:T(8,128)(2,1)}, bf16[256,128]{1,0:T(8,128)(2,1)S(1)}, u32[]{:S(2)}, u32[]{:S(2)}) collective-permute-start(bf16[256,128]{1,0:T(8,128)(2,1)} %get-tuple-element.9.own_ref), channel_id=1, source_target_pairs={{8,0},{16,8},{24,16},{0,24},{9,1},{17,9},{25,17},{1,25},{10,2},{18... | collective-permute-start | bytes 196616 | tf_op jit(solution)/shard_map/ppermute | solution.py:237
  25.0 1.9 %collective-permute-start = (bf16[256,128]{1,0:T(8,128)(2,1)}, bf16[256,128]{1,0:T(8,128)(2,1)S(1)}, u32[]{:S(2)}, u32[]{:S(2)}) collective-permute-start(bf16[256,128]{1,0:T(8,128)(2,1)} %get-tuple-element.9.own_ref), channel_id=1, source_target_pairs={{0,8},{8,16},{16,24},{24,0},{1,9},{9,17},{17,25},{25,1},{2,10},{10... | collective-permute-start | bytes 196616 | tf_op jit(solution)/shard_map/ppermute | solution.py:236
  27.0 0.0 copy-done
  27.0 1.5 %shard_map.69.act_ref = bf16[96,4096]{1,0:T(8,128)(2,1)S(1)} custom-call(bf16[1024,128]{1,0:T(8,128)(2,1)S(1)} %bitcast.15), custom_call_target="tpu_custom_call" | custom-call | flops 100663296 | bytes 1048576 | tf_op jit(solution)/shard_map/pallas_call | solution.py:212
  28.5 0.0 copy-start.1
  28.5 8.5 %collective-permute-done.1.above_ref = bf16[256,128]{1,0:T(8,128)(2,1)S(1)} collective-permute-done((bf16[256,128]{1,0:T(8,128)(2,1)}, bf16[256,128]{1,0:T(8,128)(2,1)S(1)}, u32[]{:S(2)}, u32[]{:S(2)}) %collective-permute-start.1) | collective-permute-done | bytes 65568 | tf_op jit(solution)/shard_map/ppermute | solution.py:237
  37.0 0.0 collective-permute-done.below_ref
  37.0 1.8 %all-to-all-done = bf16[32,64,128]{2,1,0:T(8,128)(2,1)S(1)} async-done(((bf16[32,64,128]{2,1,0:T(8,128)(2,1)}), bf16[32,64,128]{2,1,0:T(8,128)(2,1)S(1)}, u32[]{:S(2)}, u32[]{:S(2)}) %all-to-all-start) | async-done | bytes 524320 | tf_op jit(solution)/shard_map/all_to_all | solution.py:238
  38.9 0.0 copy-done.2
  38.9 2.5 %shard_map.70 = (bf16[512,128]{1,0:T(8,128)(2,1)}, bf16[64,9216]{1,0:T(8,128)(2,1)S(1)}) custom-call(bf16[2048,128]{1,0:T(8,128)(2,1)S(1)} %bitcast.13, bf16[256,128]{1,0:T(8,128)(2,1)S(1)} %copy-done.2, bf16[256,128]{1,0:T(8,128)(2,1)S(1)} %collective-permute-done.below_ref, bf16[256,128]{1,0:T(8,128)(2,1)S(1)} %collective-permute-done.1.above_ref, ...), custom_call_target="tpu_custom_call" | custom-call | flops 452984832 | bytes 2818048 | tf_op jit(solution)/shard_map/pallas_call | solution.py:212
  41.3 8.7 %all-to-all-start.1 = ((bf16[32,16,128]{2,1,0:T(8,128)(2,1)}), bf16[32,16,128]{2,1,0:T(8,128)(2,1)S(1)}, u32[]{:S(2)}, u32[]{:S(2)}) async-start(bf16[32,16,128]{2,1,0:T(8,128)(2,1)} %bitcast.4), calls=%async_computation.1 | async-start | bytes 262144 | tf_op jit(solution)/shard_map/all_to_all | solution.py:253
  50.0 0.0 copy-done.1
  50.0 2.3 %shard_map.71 = bf16[1024,128]{1,0:T(8,128)(2,1)} custom-call(bf16[64,9216]{1,0:T(8,128)(2,1)S(1)} %get-tuple-element.11.g_ref, bf16[27,32,64]{2,1,0:T(8,128)(2,1)S(1)} %bitcast.16), custom_call_target="tpu_custom_call" | custom-call | flops 452984832 | bytes 1552384 | tf_op jit(solution)/shard_map/pallas_call | solution.py:212
  52.3 4.8 %all-to-all-done.1.in_ref = bf16[32,16,128]{2,1,0:T(8,128)(2,1)S(1)} async-done(((bf16[32,16,128]{2,1,0:T(8,128)(2,1)}), bf16[32,16,128]{2,1,0:T(8,128)(2,1)S(1)}, u32[]{:S(2)}, u32[]{:S(2)}) %all-to-all-start.1) | async-done | bytes 131104 | tf_op jit(solution)/shard_map/all_to_all | solution.py:253
  57.1 15.4 %all_to_all.20.in_ref = bf16[16,16,128]{2,1,0:T(8,128)(2,1)S(1)} all-to-all(bf16[16,16,128]{2,1,0:T(8,128)(2,1)S(1)} %shard_map.72), channel_id=1, replica_groups=mesh['sample'=16,'sy'=4,'zh'=4,'zl'=2] {'sy','zh'}, dimensions={0} | all-to-all | bytes 131072 | tf_op jit(solution)/shard_map/all_to_all | solution.py:256
  72.6 11.8 %all_to_all.21 = bf16[32,16,128]{2,1,0:T(8,128)(2,1)S(1)} all-to-all(bf16[32,16,128]{2,1,0:T(8,128)(2,1)S(1)} %shard_map.73), channel_id=1, replica_groups=mesh['sample'=16,'sy'=4,'zh'=4,'zl'=2] {'sample','zl'}, dimensions={0} | all-to-all | bytes 262144 | tf_op jit(solution)/shard_map/all_to_all | solution.py:258
  84.3 0.9 %shard_map.74 = f32[27,32,64]{2,1,0:T(8,128)} custom-call(bf16[512,128]{1,0:T(8,128)(2,1)S(1)} %bitcast.14), custom_call_target="tpu_custom_call" | custom-call | bytes 352256 | tf_op jit(solution)/shard_map/pallas_call | solution.py:212
  (2 shorter events, 0.1 us)
Async XLA Ops:
  0.6 26.3 %copy-start = (bf16[1,32,2,16,128]{4,3,2,1,0:T(8,128)(2,1)S(1)}, bf16[1,32,2,16,128]{4,3,2,1,0:T(8,128)(2,1)}, u32[]{:S(2)}) copy-start(bf16[1,32,2,16,128]{4,3,2,1,0:T(8,128)(2,1)} %param.5) | copy-start | bytes 786436
  3.1 35.8 %copy-start.2 = (bf16[256,128]{1,0:T(8,128)(2,1)S(1)}, bf16[256,128]{1,0:T(8,128)(2,1)}, u32[]{:S(2)}) copy-start(bf16[256,128]{1,0:T(8,128)(2,1)} %get-tuple-element.9.own_ref) | copy-start | bytes 196612
  3.1 35.8 %all-to-all-start = ((bf16[32,64,128]{2,1,0:T(8,128)(2,1)}), bf16[32,64,128]{2,1,0:T(8,128)(2,1)S(1)}, u32[]{:S(2)}, u32[]{:S(2)}) async-start(bf16[32,64,128]{2,1,0:T(8,128)(2,1)} %bitcast.17), calls=%async_computation | async-start | bytes 1048576 | tf_op jit(solution)/shard_map/all_to_all | solution.py:238
  19.7 17.3 %collective-permute-start.1 = (bf16[256,128]{1,0:T(8,128)(2,1)}, bf16[256,128]{1,0:T(8,128)(2,1)S(1)}, u32[]{:S(2)}, u32[]{:S(2)}) collective-permute-start(bf16[256,128]{1,0:T(8,128)(2,1)} %get-tuple-element.9.own_ref), channel_id=1, source_target_pairs={{8,0},{16,8},{24,16},{0,24},{9,1},{17,9},{25,17},{1,25},{10,2},{18... | collective-permute-start | bytes 196616 | tf_op jit(solution)/shard_map/ppermute | solution.py:237
  25.0 12.0 %collective-permute-start = (bf16[256,128]{1,0:T(8,128)(2,1)}, bf16[256,128]{1,0:T(8,128)(2,1)S(1)}, u32[]{:S(2)}, u32[]{:S(2)}) collective-permute-start(bf16[256,128]{1,0:T(8,128)(2,1)} %get-tuple-element.9.own_ref), channel_id=1, source_target_pairs={{0,8},{8,16},{16,24},{24,0},{1,9},{9,17},{17,25},{25,1},{2,10},{10... | collective-permute-start | bytes 196616 | tf_op jit(solution)/shard_map/ppermute | solution.py:236
  28.5 21.5 %copy-start.1 = (bf16[64,32,3,3,3]{0,1,4,3,2:T(8,128)(2,1)S(1)}, bf16[64,32,3,3,3]{0,1,4,3,2:T(8,128)(2,1)}, u32[]{:S(2)}) copy-start(bf16[64,32,3,3,3]{0,1,4,3,2:T(8,128)(2,1)} %param.6) | copy-start | bytes 331780
  41.3 15.8 %all-to-all-start.1 = ((bf16[32,16,128]{2,1,0:T(8,128)(2,1)}), bf16[32,16,128]{2,1,0:T(8,128)(2,1)S(1)}, u32[]{:S(2)}, u32[]{:S(2)}) async-start(bf16[32,16,128]{2,1,0:T(8,128)(2,1)} %bitcast.4), calls=%async_computation.1 | async-start | bytes 262144 | tf_op jit(solution)/shard_map/all_to_all | solution.py:253

commit v10 on v8

--- a/solution.py
+++ b/solution.py
@@ -222,7 +222,7 @@
 
 def body(activations, weight, pooled_grad, window_argmax):
     shape = jax.ShapeDtypeStruct
-    rise = [(i, (i + 1) % SY) for i in range(SY)]
+    rise = [(i, i + 1) for i in range(SY - 1)]
     fall = [(j, i) for i, j in rise]
     sel = jnp.asarray(selection(), BF16)
     sent, codes = call(

time: 85.6 us -> 85.6 us (level)
  waiting for transfers between devices: 19.3 us -> 20.5 us
    ppermute x1, starting transfers between devices: 5.29 us -> 1.29 us  [body(): above = lax.ppermute(codes, 'sy', fall)]
    ppermute x1, starting transfers between devices: 1.92 us -> 4.89 us  [body(): below = lax.ppermute(codes, 'sy', rise)]
where the time goes in v10:
time: 85.6 us; the launch traced here: 85.2 us
  starting transfers between devices  27.3 us (32%)
  blocking collectives  26.9 us (31%)
  waiting for transfers between devices  20.5 us (24%)
  Pallas kernels  9.68 us (11%)
    all_to_all x1, starting transfers between devices, body(): lax.all_to_all(sent.reshape(32, 64, 128), ('sy', 'zh', 'zl'), 0, 0)  16.7 us
    all_to_all x1, blocking collectives, body(): part = lax.all_to_all(local.reshape(2 * SAMPLE, 16, 128), near, 0, 0)  15.1 us
    all_to_all x1, blocking collectives, body(): whole = lax.all_to_all(part, near, 0, 0).reshape(512, 128)  11.8 us
    pallas_call x7, Pallas kernels, call(): pl.pallas_call(kernel, out_shape=tuple(outs) if len(outs) > 1 else outs[0...  9.68 us
    ppermute x1, waiting for transfers between devices, body(): above = lax.ppermute(codes, 'sy', fall)  9.18 us
    all_to_all x1, waiting for transfers between devices, body(): lax.all_to_all(part, far, 0, 0)  8.99 us
    ppermute x1, starting transfers between devices, body(): below = lax.ppermute(codes, 'sy', rise)  4.89 us
    all_to_all x1, starting transfers between devices, body(): lax.all_to_all(part, far, 0, 0)  4.47 us
  transfers between devices with their start and end apart: 4, of which 3 were waited for; matrix products, arithmetic and copies ran while one was open for 0% of the time, Pallas kernels for 5%

profile of v10, /device:TPU:1, one launch (start us, length us, event | category | flops | bytes accessed | tf_op | source)
XLA Modules:
  0.0 85.2 jit_solution(13156592533860478535)
XLA Ops:
  0.6 0.0 copy-start
  0.6 2.4 %shard_map.68 = (bf16[2048,128]{1,0:T(8,128)(2,1)}, bf16[256,128]{1,0:T(8,128)(2,1)}) custom-call(bf16[1,2,4,4096]{3,2,1,0:T(4,128)(2,1)} %pg_any.1, s32[256,128]{1,0:T(8,128)} %bitcast.20, bf16[1024,256]{1,0:T(8,128)(2,1)} %constant.2.clone.sel_any), custom_call_target="tpu_custom_call" | custom-call | flops 67108864 | bytes 1310720 | tf_op jit(solution)/shard_map/pallas_call | solution.py:212
  3.1 0.0 copy-start.2
  3.1 16.7 %all-to-all-start = ((bf16[32,64,128]{2,1,0:T(8,128)(2,1)}), bf16[32,64,128]{2,1,0:T(8,128)(2,1)S(1)}, u32[]{:S(2)}, u32[]{:S(2)}) async-start(bf16[32,64,128]{2,1,0:T(8,128)(2,1)} %bitcast.18), calls=%async_computation | async-start | bytes 1048576 | tf_op jit(solution)/shard_map/all_to_all | solution.py:238
  19.7 1.3 %collective-permute-start.1 = (bf16[256,128]{1,0:T(8,128)(2,1)}, bf16[256,128]{1,0:T(8,128)(2,1)S(1)}, u32[]{:S(2)}, u32[]{:S(2)}) collective-permute-start(bf16[256,128]{1,0:T(8,128)(2,1)} %get-tuple-element.9.own_ref), channel_id=1, source_target_pairs={{8,0},{16,8},{24,16},{9,1},{17,9},{25,17},{10,2},{18,10},{26,18},{... | collective-permute-start | bytes 196616 | tf_op jit(solution)/shard_map/ppermute | solution.py:237
  21.0 4.9 %collective-permute-start = (bf16[256,128]{1,0:T(8,128)(2,1)}, bf16[256,128]{1,0:T(8,128)(2,1)S(1)}, u32[]{:S(2)}, u32[]{:S(2)}) collective-permute-start(bf16[256,128]{1,0:T(8,128)(2,1)} %get-tuple-element.9.own_ref), channel_id=1, source_target_pairs={{0,8},{8,16},{16,24},{1,9},{9,17},{17,25},{2,10},{10,18},{18,26},{... | collective-permute-start | bytes 196616 | tf_op jit(solution)/shard_map/ppermute | solution.py:236
  25.9 0.0 copy-done
  25.9 1.5 %shard_map.69.act_ref = bf16[96,4096]{1,0:T(8,128)(2,1)S(1)} custom-call(bf16[1024,128]{1,0:T(8,128)(2,1)S(1)} %bitcast.15), custom_call_target="tpu_custom_call" | custom-call | flops 100663296 | bytes 1048576 | tf_op jit(solution)/shard_map/pallas_call | solution.py:212
  27.5 0.0 copy-start.1
  27.5 9.2 %collective-permute-done.1.above_ref = bf16[256,128]{1,0:T(8,128)(2,1)S(1)} collective-permute-done((bf16[256,128]{1,0:T(8,128)(2,1)}, bf16[256,128]{1,0:T(8,128)(2,1)S(1)}, u32[]{:S(2)}, u32[]{:S(2)}) %collective-permute-start.1) | collective-permute-done | bytes 65568 | tf_op jit(solution)/shard_map/ppermute | solution.py:237
  36.7 0.0 collective-permute-done.below_ref
  36.7 2.4 %all-to-all-done = bf16[32,64,128]{2,1,0:T(8,128)(2,1)S(1)} async-done(((bf16[32,64,128]{2,1,0:T(8,128)(2,1)}), bf16[32,64,128]{2,1,0:T(8,128)(2,1)S(1)}, u32[]{:S(2)}, u32[]{:S(2)}) %all-to-all-start) | async-done | bytes 524320 | tf_op jit(solution)/shard_map/all_to_all | solution.py:238
  39.1 0.0 copy-done.2
  39.1 1.8 %shard_map.70 = (bf16[512,128]{1,0:T(8,128)(2,1)S(1)}, bf16[64,9216]{1,0:T(8,128)(2,1)S(1)}) custom-call(bf16[2048,128]{1,0:T(8,128)(2,1)S(1)} %bitcast.13, bf16[256,128]{1,0:T(8,128)(2,1)S(1)} %copy-done.2, bf16[256,128]{1,0:T(8,128)(2,1)S(1)} %collective-permute-done.below_ref, bf16[256,128]{1,0:T(8,128)(2,1)S(1)} %collective-permute-done.1.above_ref, ...), custom_call_target="tpu_custom_call" | custom-call | flops 452984832 | bytes 2818048 | tf_op jit(solution)/shard_map/pallas_call | solution.py:212
  40.9 15.1 %all_to_all.20.in_ref = bf16[32,16,128]{2,1,0:T(8,128)(2,1)S(1)} all-to-all(bf16[32,16,128]{2,1,0:T(8,128)(2,1)S(1)} %bitcast.16), channel_id=1, replica_groups=mesh['sample'=16,'sy'=4,'zh'=4,'zl'=2] {'sample','zl'}, dimensions={0} | all-to-all | bytes 262144 | tf_op jit(solution)/shard_map/all_to_all | solution.py:252
  56.0 0.7 shard_map.71
  56.7 4.5 %all-to-all-start.2 = ((bf16[16,16,128]{2,1,0:T(8,128)(2,1)}), bf16[16,16,128]{2,1,0:T(8,128)(2,1)S(1)}, u32[]{:S(2)}, u32[]{:S(2)}) async-start(bf16[16,16,128]{2,1,0:T(8,128)(2,1)} %shard_map.71), calls=%async_computation.2 | async-start | bytes 131072 | tf_op jit(solution)/shard_map/all_to_all | solution.py:254
  61.2 0.0 copy-done.1
  61.2 2.3 %shard_map.72 = bf16[1024,128]{1,0:T(8,128)(2,1)} custom-call(bf16[64,9216]{1,0:T(8,128)(2,1)S(1)} %get-tuple-element.11.g_ref, bf16[27,32,64]{2,1,0:T(8,128)(2,1)S(1)} %bitcast.17), custom_call_target="tpu_custom_call" | custom-call | flops 452984832 | bytes 1552384 | tf_op jit(solution)/shard_map/pallas_call | solution.py:212
  63.5 9.0 %all-to-all-done.2.in_ref = bf16[16,16,128]{2,1,0:T(8,128)(2,1)S(1)} async-done(((bf16[16,16,128]{2,1,0:T(8,128)(2,1)}), bf16[16,16,128]{2,1,0:T(8,128)(2,1)S(1)}, u32[]{:S(2)}, u32[]{:S(2)}) %all-to-all-start.2) | async-done | bytes 65568 | tf_op jit(solution)/shard_map/all_to_all | solution.py:254
  72.6 11.8 %all_to_all.21 = bf16[32,16,128]{2,1,0:T(8,128)(2,1)S(1)} all-to-all(bf16[32,16,128]{2,1,0:T(8,128)(2,1)S(1)} %shard_map.73), channel_id=1, replica_groups=mesh['sample'=16,'sy'=4,'zh'=4,'zl'=2] {'sample','zl'}, dimensions={0} | all-to-all | bytes 262144 | tf_op jit(solution)/shard_map/all_to_all | solution.py:256
  84.3 0.9 %shard_map.74 = f32[27,32,64]{2,1,0:T(8,128)} custom-call(bf16[512,128]{1,0:T(8,128)(2,1)S(1)} %bitcast.14), custom_call_target="tpu_custom_call" | custom-call | bytes 352256 | tf_op jit(solution)/shard_map/pallas_call | solution.py:212
  (1 shorter events, 0.0 us)
Async XLA Ops:
  0.6 25.3 %copy-start = (bf16[1,32,2,16,128]{4,3,2,1,0:T(8,128)(2,1)S(1)}, bf16[1,32,2,16,128]{4,3,2,1,0:T(8,128)(2,1)}, u32[]{:S(2)}) copy-start(bf16[1,32,2,16,128]{4,3,2,1,0:T(8,128)(2,1)} %param.5) | copy-start | bytes 786436
  3.1 36.0 %copy-start.2 = (bf16[256,128]{1,0:T(8,128)(2,1)S(1)}, bf16[256,128]{1,0:T(8,128)(2,1)}, u32[]{:S(2)}) copy-start(bf16[256,128]{1,0:T(8,128)(2,1)} %get-tuple-element.9.own_ref) | copy-start | bytes 196612
  3.1 36.0 %all-to-all-start = ((bf16[32,64,128]{2,1,0:T(8,128)(2,1)}), bf16[32,64,128]{2,1,0:T(8,128)(2,1)S(1)}, u32[]{:S(2)}, u32[]{:S(2)}) async-start(bf16[32,64,128]{2,1,0:T(8,128)(2,1)} %bitcast.18), calls=%async_computation | async-start | bytes 1048576 | tf_op jit(solution)/shard_map/all_to_all | solution.py:238
  19.7 17.0 %collective-permute-start.1 = (bf16[256,128]{1,0:T(8,128)(2,1)}, bf16[256,128]{1,0:T(8,128)(2,1)S(1)}, u32[]{:S(2)}, u32[]{:S(2)}) collective-permute-start(bf16[256,128]{1,0:T(8,128)(2,1)} %get-tuple-element.9.own_ref), channel_id=1, source_target_pairs={{8,0},{16,8},{24,16},{9,1},{17,9},{25,17},{10,2},{18,10},{26,18},{... | collective-permute-start | bytes 196616 | tf_op jit(solution)/shard_map/ppermute | solution.py:237
  21.0 15.7 %collective-permute-start = (bf16[256,128]{1,0:T(8,128)(2,1)}, bf16[256,128]{1,0:T(8,128)(2,1)S(1)}, u32[]{:S(2)}, u32[]{:S(2)}) collective-permute-start(bf16[256,128]{1,0:T(8,128)(2,1)} %get-tuple-element.9.own_ref), channel_id=1, source_target_pairs={{0,8},{8,16},{16,24},{1,9},{9,17},{17,25},{2,10},{10,18},{18,26},{... | collective-permute-start | bytes 196616 | tf_op jit(solution)/shard_map/ppermute | solution.py:236
  27.5 33.7 %copy-start.1 = (bf16[64,32,3,3,3]{0,1,4,3,2:T(8,128)(2,1)S(1)}, bf16[64,32,3,3,3]{0,1,4,3,2:T(8,128)(2,1)}, u32[]{:S(2)}) copy-start(bf16[64,32,3,3,3]{0,1,4,3,2:T(8,128)(2,1)} %param.6) | copy-start | bytes 331780
  56.7 15.8 %all-to-all-start.2 = ((bf16[16,16,128]{2,1,0:T(8,128)(2,1)}), bf16[16,16,128]{2,1,0:T(8,128)(2,1)S(1)}, u32[]{:S(2)}, u32[]{:S(2)}) async-start(bf16[16,16,128]{2,1,0:T(8,128)(2,1)} %shard_map.71), calls=%async_computation.2 | async-start | bytes 131072 | tf_op jit(solution)/shard_map/all_to_all | solution.py:254
